TPU v7x, 256 devices: a whole 4x4x8 slice. The times are simulated.
256 devices in a mesh: mem: 64 (over z, y, core), job: 4 (over x).
Axes of the slice: x: 4, y: 4, z: 8, core: 2. Of those that a mesh axis runs over, the one named last changes fastest.
Arguments:
- pair_cost: bfloat16 [12288, 128, 128], P(('mem', 'job')), may hold values from -6 to 6
- pair_coef: bfloat16 [12288, 128, 128], P(('mem', 'job')), may hold values from 0.049804688 to 0.5
- slot_member: int32 [256, 48], P(('mem', 'job')), may hold values from 0 to 31, never falling along the last dimension, each value on 1 to 4 neighbouring positions
- slot_owner: int32 [256, 48, 1], P(('mem', 'job')), may hold values from 0 to 63; in each aligned block of 48 rows (0 to 47, 48 to 95, ..., all dimensions but the last counted through in order) at most 2 rows name the same one
- slot_local: int32 [256, 48], P(('mem', 'job')), may hold values from 0 to 15
- duals: float32 [4096, 128], P(('mem', 'job')), may hold values from 0.1 to 3
- capacity: int32 [4096, 128], P(('mem', 'job')), may hold values from 0 to 39
Outputs:
- primal: bfloat16 [12288, 128, 128], P(('mem', 'job'))
- gradient: float32 [4096, 128], P(('mem', 'job'))
- member_share: float32 [2048, 128], P('mem')
Inputs may be any that keep to these rules, and one draw needn't show every extreme that they name: `slot_member`: in each device's row the values never fall, every value appears, none more than 4 times, and one exactly 4 times. `slot_owner`: among the 48 entries of one device no value appears more than 2 times, and in some devices one appears exactly 2 times.
All inputs are finite; a program needn't handle non-finite values.
Results may differ from a plain program's by a relative error of at most 0.001.
Values sent between devices are 32-bit elements; how exact they have to be, the bound alone decides.
No kernel may reach another device: no remote copies, remote signals or barrier semaphores. Data moves between devices by JAX's collectives and lax.ppermute only.
A program may use at most 64 MiB of HBM per device.

v0:
```python
import jax
import jax.numpy as jnp
from jax import lax
from jax.sharding import PartitionSpec as P

MB_DEV = 32


RIDGE = 1.0


def allocate(pair_cost, pair_coef, dual_rows):
    reduced = pair_cost.astype(jnp.float32) + pair_coef.astype(jnp.float32) * dual_rows[:, None, :]
    allocation = jnp.clip(-reduced / RIDGE, 0.0, 1.0)
    column_part = jnp.sum(pair_coef.astype(jnp.float32) * allocation, axis=1)
    row_part = jnp.sum(allocation, axis=2)
    return (allocation.astype(jnp.bfloat16), column_part, row_part)


def per_device(pair_cost, pair_coef, slot_member, slot_owner, slot_local, duals, capacity):
    block_size = pair_cost.shape[1]
    job_blocks = duals.shape[0]
    mem_count = lax.axis_size("mem")
    owner_index = slot_owner[0, :, 0]
    local_index = slot_local[0]
    column_duals = lax.all_gather(duals, "mem", axis=0, tiled=True)
    range_index = owner_index * job_blocks + local_index
    dual_rows = column_duals[range_index]
    primal, column_part, row_part = allocate(pair_cost, pair_coef, dual_rows)
    partial_sums = jax.ops.segment_sum(
        column_part, range_index, num_segments=mem_count * job_blocks
    )
    totals = lax.psum_scatter(partial_sums, "mem", scatter_dimension=0, tiled=True)
    gradient = totals - capacity.astype(jnp.float32)
    member_table = (jnp.arange(MB_DEV, dtype=jnp.int32)[:, None] == slot_member[0][None, :]).astype(
        jnp.float32
    )
    member_part = jnp.dot(
        member_table, row_part, precision=lax.Precision.HIGHEST, preferred_element_type=jnp.float32
    )
    member_share = lax.psum(member_part, "job") / block_size
    return (primal, gradient, member_share)


def solution(mesh):
    placed = (
        P(("mem", "job"), None, None),
        P(("mem", "job"), None, None),
        P(("mem", "job"), None),
        P(("mem", "job"), None, None),
        P(("mem", "job"), None),
        P(("mem", "job"), None),
        P(("mem", "job"), None),
    )
    return jax.shard_map(
        per_device,
        mesh=mesh,
        in_specs=placed,
        out_specs=(P(("mem", "job"), None, None), P(("mem", "job"), None), P("mem", None)),
        check_vma=False,
    )
```

profile of v0, /device:TPU:1, one launch (start us, length us, event | category | flops | bytes accessed | tf_op | source)
XLA Modules:
  0.0 254.1 jit_solution(2715587856253178641)
XLA Ops:
  7.2 0.0 all-reduce.3.cloned.1.call-start
  7.2 0.7 fusion.11
  7.9 54.9 %all_gather.3 = f32[1024,128]{1,0:T(8,128)S(1)} all-gather(f32[16,128]{1,0:T(8,128)} %param.12), channel_id=1, replica_groups=mesh['mem'=64,'job'=4] {'mem'}, dimensions={0}, use_global_device_ids=true | all-gather | bytes 532480 | tf_op jit(solution)/shard_map/all_gather | solution.py:26
  62.8 0.6 gather_fusion
  63.4 0.0 copy-start.1
  63.4 0.0 copy-start.2
  63.4 0.0 copy-start
  63.4 4.1 %fusion.4 = (f32[48,128]{1,0:T(8,128)S(1)}, f32[48,128]{1,0:T(8,128)S(1)}, bf16[48,128,128]{2,1,0:T(8,128)(2,1)}) fusion(bf16[48,128,128]{2,1,0:T(8,128)(2,1)} %param.8, bf16[48,128,128]{2,1,0:T(8,128)(2,1)} %param.7, f32[48,128]{1,0:T(8,128)S(1)} %gather_fusion), kind=kLoop, calls=%fused_computation.8 | loop fusion | flops 7852032 | bytes 4792320 | tf_op jit(solution)/shard_map/reduce_sum | solution.py:16
  67.5 1.5 scatter_custom_fusion
  69.1 0.0 all-reduce.3.cloned.1.call-update
  69.1 0.0 copy-done.1
  69.1 0.1 fusion.8
  69.3 0.0 copy-done.2
  69.3 0.6 dynamic-slice
  70.5 13.9 %psum.7 = f32[32,128]{1,0:T(8,128)S(1)} all-reduce(f32[32,128]{1,0:T(8,128)S(1)} %fusion.8), channel_id=1, replica_groups=mesh['mem'=64,'job'=4] {'job'}, use_global_device_ids=true, to_apply=%region_4.5 | all-reduce | flops 4096 | bytes 32768 | tf_op jit(solution)/shard_map/psum | solution.py:41
  84.4 0.6 broadcast_multiply_fusion
  85.0 161.0 %all-reduce.3.cloned.1.call-done = f32[1024,128]{1,0:T(8,128)} async-done(((f32[1024,128]{1,0:T(8,128)}), f32[1024,128]{1,0:T(8,128)}) %all-reduce.3.cloned.1.call-update) | async-done | bytes 524304
  246.0 0.0 copy-done
  246.0 1.3 dynamic-slice_subtract_fusion
  (1 shorter events, 0.0 us)
Async XLA Ops:
  7.2 238.8 %all-reduce.3.cloned.1.call-start = ((), (), s32[]{:S(2)}) async-start(), calls=%async_computation | async-start | bytes 1048576
  63.4 5.7 %copy-start.1 = (s32[1,48]{1,0:T(1,128)S(1)}, s32[1,48]{1,0:T(1,128)}, u32[]{:S(2)}) copy-start(s32[1,48]{1,0:T(1,128)} %param.9) | copy-start | bytes 580
  63.4 5.9 %copy-start.2 = (u32[256]{0:T(256)S(1)}, u32[256]{0:T(256)}, u32[]{:S(2)}) copy-start(u32[256]{0:T(256)} %constant.24) | copy-start | bytes 3076
  63.4 182.6 %copy-start = (s32[16,128]{1,0:T(8,128)S(1)}, s32[16,128]{1,0:T(8,128)}, u32[]{:S(2)}) copy-start(s32[16,128]{1,0:T(8,128)} %param.13) | copy-start | bytes 24580
Sparse Core Ops, SparseCore 0:
  69.2 176.6 all-reduce.2
where the time goes:
time: 255 us; the launch traced here: 254 us
  waiting for transfers between devices  161 us (63%)
  blocking collectives  68.8 us (27%)
  between operations  14.7 us (6%)
  other arithmetic  8.25 us (3%)
    unnamed x2, waiting for transfers between devices  161 us
    all_gather x1, blocking collectives, per_device(): column_duals = lax.all_gather(duals, 'mem', axis=0, tiled=True)  54.9 us
    psum x1, blocking collectives, per_device(): member_share = lax.psum(member_part, 'job') / block_size  13.9 us
  transfers between devices with their start and end apart: 1, of which 1 were waited for; matrix products, arithmetic and copies ran while one was open for 1% of the time, Pallas kernels for 0%

commit v1 on v0

v1 whole, which is shorter than its diff:
```python
import jax
import jax.numpy as jnp
from jax import lax
from jax.experimental import pallas as pl
from jax.experimental.pallas import tpu as pltpu
from jax.sharding import Mesh, PartitionSpec as P

Z, Y, C, X = 8, 4, 2, 4
CAP = 48
BLOCK = 128
MB_DEV = 32
JB_DEV = 16
MEM = Z * Y * C
ROWS = 4
RIDGE = 1.0


def allocate_kernel(
    owner_ref, local_ref, member_ref, rows_ref, cost_ref, coef_ref,
    primal_ref, send_ref, member_out_ref, count_ref,
):
    send_ref[...] = jnp.full((MEM * ROWS, BLOCK), -1.0, jnp.float32)
    member_out_ref[...] = jnp.zeros((MB_DEV, BLOCK), jnp.float32)
    ones = jnp.ones((8, BLOCK), jnp.bfloat16)

    def clear(i, carry):
        count_ref[i] = 0
        return carry

    lax.fori_loop(0, MEM, clear, 0, unroll=8)

    def block(s, carry):
        owner = owner_ref[0, s]
        local = local_ref[0, s]
        member = member_ref[0, s]
        row = (owner & 1) * (Z * Y * JB_DEV) + (owner >> 1) * JB_DEV + local
        minus_dual = -rows_ref[pl.ds(row, 1), :]
        cost = cost_ref[s].astype(jnp.float32)
        coef = coef_ref[s].astype(jnp.float32)
        alloc = jnp.minimum(jnp.maximum(coef * minus_dual - cost, 0.0), 1.0)
        high = alloc.astype(jnp.bfloat16)
        primal_ref[s] = high
        rest = (alloc - high.astype(jnp.float32)).astype(jnp.bfloat16)
        column = jnp.sum(coef * alloc, axis=0, keepdims=True)
        k = count_ref[owner]
        count_ref[owner] = k + 1
        place = owner * ROWS + k
        send_ref[pl.ds(place, 1), :] = column
        send_ref[pl.ds(place + 2, 1), :] = jnp.full((1, BLOCK), local.astype(jnp.float32))
        dims = (((1,), (1,)), ((), ()))
        sums = lax.dot_general(ones, high, dims, preferred_element_type=jnp.float32)
        sums = sums + lax.dot_general(ones, rest, dims, preferred_element_type=jnp.float32)
        member_out_ref[pl.ds(member, 1), :] += sums[0:1]
        return carry

    lax.fori_loop(0, CAP, block, 0, unroll=2)


def finish_kernel(recv_ref, m0_ref, m1_ref, m2_ref, m3_ref, capacity_ref, gradient_ref, share_ref):
    share_ref[...] = ((m0_ref[...] + m1_ref[...]) + (m2_ref[...] + m3_ref[...])) * (1.0 / BLOCK)
    sub = lax.broadcasted_iota(jnp.int32, (8, BLOCK), 0) % 4
    data = sub < 2
    totals = [jnp.zeros((8, BLOCK), jnp.float32) for _ in range(JB_DEV)]
    for i in range(MEM * ROWS // 8):
        got = recv_ref[i * 8:(i + 1) * 8, :]
        name = jnp.where(data, pltpu.roll(got, 6, 0), -1.0)
        for k in range(JB_DEV):
            totals[k] = totals[k] + jnp.where(name == float(k), got, 0.0)
    summed = jnp.concatenate([jnp.sum(t, axis=0, keepdims=True) for t in totals], axis=0)
    gradient_ref[...] = summed - capacity_ref[...].astype(jnp.float32)


def per_device(pair_cost, pair_coef, slot_member, slot_owner, slot_local, duals, capacity):
    vmem = pl.BlockSpec(memory_space=pltpu.VMEM)
    smem = pl.BlockSpec(memory_space=pltpu.SMEM)
    copies = jnp.broadcast_to(duals[None], (Z * Y, JB_DEV, BLOCK))
    rows = lax.all_to_all(copies, ("z", "y"), split_axis=0, concat_axis=0, tiled=True)
    rows = lax.all_gather(rows.reshape(Z * Y * JB_DEV, BLOCK), "c", axis=0, tiled=True)
    primal, send, member = pl.pallas_call(
        allocate_kernel,
        out_shape=(
            jax.ShapeDtypeStruct((CAP, BLOCK, BLOCK), jnp.bfloat16),
            jax.ShapeDtypeStruct((MEM * ROWS, BLOCK), jnp.float32),
            jax.ShapeDtypeStruct((MB_DEV, BLOCK), jnp.float32),
        ),
        in_specs=[smem, smem, smem, vmem, vmem, vmem],
        out_specs=(vmem, vmem, vmem),
        scratch_shapes=[pltpu.SMEM((MEM,), jnp.int32)],
        compiler_params=pltpu.CompilerParams(vmem_limit_bytes=16 * 1024 * 1024),
        cost_estimate=pl.CostEstimate(flops=8 * CAP * BLOCK * BLOCK, bytes_accessed=6 * CAP * BLOCK * BLOCK, transcendentals=0),
        name="allocate",
    )(slot_owner.reshape(1, CAP), slot_local, slot_member, rows, pair_cost, pair_coef)
    others = [lax.ppermute(member, "x", [(i, i ^ k) for i in range(X)]) for k in (1, 2, 3)]
    recv = lax.all_to_all(
        send.reshape(MEM, ROWS, BLOCK), ("z", "y", "c"), split_axis=0, concat_axis=0, tiled=True
    ).reshape(MEM * ROWS, BLOCK)
    gradient, share = pl.pallas_call(
        finish_kernel,
        out_shape=(
            jax.ShapeDtypeStruct((JB_DEV, BLOCK), jnp.float32),
            jax.ShapeDtypeStruct((MB_DEV, BLOCK), jnp.float32),
        ),
        in_specs=[vmem] * 6,
        out_specs=(vmem, vmem),
        name="finish",
    )(recv, member, *others, capacity)
    return primal, gradient, share


def solution(mesh):
    axes = ("z", "y", "c", "x")
    fine = Mesh(mesh.devices.reshape(Z, Y, C, X), axes)
    each = lambda n: P(axes, *([None] * (n - 1)))
    return jax.shard_map(
        per_device,
        mesh=fine,
        in_specs=(each(3), each(3), each(2), each(3), each(2), each(2), each(2)),
        out_specs=(each(3), each(2), P(("z", "y", "c"), None)),
        check_vma=False,
    )
```

time: 255 us -> 55.1 us (0.22)
  waiting for transfers between devices: 161 us -> 7.76 us
  blocking collectives: 68.8 us -> 27.3 us
  between operations: 14.7 us -> 0.71 us
  other arithmetic: 8.25 us -> 0 us
  Pallas kernels: 0 us -> 8.19 us
  starting transfers between devices: 0.04 us -> 7.98 us
    unnamed x2 -> x0, waiting for transfers between devices: 161 us -> none
    all_gather x1, blocking collectives: 54.9 us -> 4.25 us  [per_device(): lax.all_gather(rows.reshape(Z * Y * JB_DEV, BLOCK), 'c', axis=0, tiled=True)]
    all_to_all x0 -> x1, blocking collectives: none -> 23 us  [per_device(): lax.all_to_all(copies, ('z', 'y'), split_axis=0, concat_axis=0, tiled=True)]
    psum x1 -> x0, blocking collectives: 13.9 us -> none  [per_device(): member_share = lax.psum(member_part, 'job') / block_size]
    pallas_call x0 -> x2, Pallas kernels: none -> 8.19 us  [the longest x1 6.41 us: per_device(): pl.pallas_call(allocate_kernel, out_shape=(jax.ShapeDtypeStruct((CAP, BLO...]
    all_to_all x0 -> x1, starting transfers between devices: none -> 4.64 us  [per_device(): lax.all_to_all(send.reshape(MEM, ROWS, BLOCK), ('z', 'y', 'c'), split_axi...]
    all_to_all x0 -> x1, waiting for transfers between devices: none -> 4.15 us  [per_device(): lax.all_to_all(send.reshape(MEM, ROWS, BLOCK), ('z', 'y', 'c'), split_axi...]
    reduce_sum x1 -> x0, other arithmetic: 4.11 us -> none  [allocate(): row_part = jnp.sum(allocation, axis=2)]
  transfers between devices with their start and end apart: 1 -> 4, of which waited for: 1 -> 3; matrix products, arithmetic and copies ran while one was open for 1% -> 0% of each run, Pallas kernels for 0% -> 0%
where the time goes in v1:
time: 55.1 us; the launch traced here: 54.8 us
  blocking collectives  27.3 us (50%)
  Pallas kernels  8.19 us (15%)
  starting transfers between devices  7.98 us (14%)
  waiting for transfers between devices  7.76 us (14%)
  local copies, waits for them, and re-layouts  2.9 us (5%)
  between operations  0.71 us (1%)
    all_to_all x1, blocking collectives, per_device(): lax.all_to_all(copies, ('z', 'y'), split_axis=0, concat_axis=0, tiled=True)  23 us
    pallas_call x1, Pallas kernels, per_device(): pl.pallas_call(allocate_kernel, out_shape=(jax.ShapeDtypeStruct((CAP, BLO...  6.41 us
    all_to_all x1, starting transfers between devices, per_device(): lax.all_to_all(send.reshape(MEM, ROWS, BLOCK), ('z', 'y', 'c'), split_axi...  4.64 us
    all_gather x1, blocking collectives, per_device(): lax.all_gather(rows.reshape(Z * Y * JB_DEV, BLOCK), 'c', axis=0, tiled=True)  4.25 us
    all_to_all x1, waiting for transfers between devices, per_device(): lax.all_to_all(send.reshape(MEM, ROWS, BLOCK), ('z', 'y', 'c'), split_axi...  4.15 us
    ppermute x3, waiting for transfers between devices, per_device(): lax.ppermute(member, 'x', [(i, i ^ k) for i in range(X)])  3.61 us
    ppermute x3, starting transfers between devices, per_device(): lax.ppermute(member, 'x', [(i, i ^ k) for i in range(X)])  3.34 us
    unnamed x20, local copies, waits for them, and re-layouts  2.07 us
  transfers between devices with their start and end apart: 4, of which 3 were waited for; matrix products, arithmetic and copies ran while one was open for 0% of the time, Pallas kernels for 0%

profile of v1, /device:TPU:1, one launch (start us, length us, event | category | flops | bytes accessed | tf_op | source)
XLA Modules:
  0.0 54.8 jit_solution(7810597074789273071)
XLA Ops:
  0.6 0.0 copy-start.4
  0.6 0.0 copy-start.3
  0.7 0.0 copy-start.5
  0.7 0.0 copy-start
  0.7 0.8 %broadcast_in_dim.2 = f32[32,16,128]{2,1,0:T(8,128)S(1)} broadcast(f32[16,128]{1,0:T(8,128)} %param.12), dimensions={1,2} | broadcast | bytes 270336 | tf_op jit(solution)/shard_map/broadcast_in_dim | solution.py:76
  1.5 23.0 %all_to_all.10 = f32[32,16,128]{2,1,0:T(8,128)S(1)} all-to-all(f32[32,16,128]{2,1,0:T(8,128)S(1)} %broadcast_in_dim.2), channel_id=1, replica_groups=mesh['z'=8,'y'=4,'c'=2,'x'=4] {'z','y'}, dimensions={0} | all-to-all | bytes 524288 | tf_op jit(solution)/shard_map/all_to_all | solution.py:77
  24.5 4.2 %all_gather.3.rows_ref = f32[1024,128]{1,0:T(8,128)S(1)} all-gather(f32[512,128]{1,0:T(8,128)S(1)} %bitcast.5), channel_id=1, replica_groups=mesh['z'=8,'y'=4,'c'=2,'x'=4] {'c'}, dimensions={0}, use_global_device_ids=true | all-gather | bytes 786432 | tf_op jit(solution)/shard_map/all_gather | solution.py:78
  28.8 0.0 copy-done.4
  28.8 0.0 copy-done.3
  28.8 0.0 copy-done.5
  28.8 0.0 copy-start.1
  28.8 1.4 %copy-done.1 = bf16[48,128,128]{2,1,0:T(8,128)(2,1)S(1)} copy-done((bf16[48,128,128]{2,1,0:T(8,128)(2,1)S(1)}, bf16[48,128,128]{2,1,0:T(8,128)(2,1)}, u32[]{:S(2)}) %copy-start.1) | copy-done | bytes 1572888
  30.2 6.4 %allocate.1 = (bf16[48,128,128]{2,1,0:T(8,128)(2,1)}, f32[256,128]{1,0:T(8,128)}, f32[32,128]{1,0:T(8,128)S(1)}) custom-call(s32[1,48]{1,0:T(1,128)S(1)} %bitcast.4, s32[1,48]{1,0:T(1,128)S(1)} %copy-done.4, s32[1,48]{1,0:T(1,128)S(1)} %copy-done.5, f32[1024,128]{1,0:T(8,128)S(1)} %all_gather.3.rows_ref, bf16[48,128,128]{2,1,0:T(8,128)(2,1)S(1)} %copy-done, ...), custom_call_target="tpu_custom_call" | custom-call | flops 6291456 | bytes 4718592 | tf_op jit(solution)/shard_map/allocate/pallas_call | solution.py:79
  36.6 4.6 %all-to-all-start.1 = ((f32[64,4,128]{2,1,0:T(4,128)}), f32[64,4,128]{2,1,0:T(4,128)S(1)}, u32[]{:S(2)}, u32[]{:S(2)}) async-start(f32[64,4,128]{2,1,0:T(4,128)} %bitcast.2), calls=%async_computation.1 | async-start | bytes 262144 | tf_op jit(solution)/shard_map/all_to_all | solution.py:94
  41.3 2.6 %collective-permute-start.2 = (f32[32,128]{1,0:T(8,128)S(1)}, f32[32,128]{1,0:T(8,128)S(1)}, u32[]{:S(2)}, u32[]{:S(2)}) collective-permute-start(f32[32,128]{1,0:T(8,128)S(1)} %get-tuple-element.10.m0_ref), channel_id=1, source_target_pairs={{0,3},{1,2},{2,1},{3,0},{4,7},{5,6},{6,5},{7,4},{8,11},{9,10},{10,... | collective-permute-start | bytes 49160 | tf_op jit(solution)/shard_map/ppermute | solution.py:93
  43.8 0.5 collective-permute-start.1
  44.4 0.3 collective-permute-start
  44.6 0.8 %collective-permute-done.2.m3_ref = f32[32,128]{1,0:T(8,128)S(1)} collective-permute-done((f32[32,128]{1,0:T(8,128)S(1)}, f32[32,128]{1,0:T(8,128)S(1)}, u32[]{:S(2)}, u32[]{:S(2)}) %collective-permute-start.2) | collective-permute-done | bytes 16416 | tf_op jit(solution)/shard_map/ppermute | solution.py:93
  45.5 2.8 %collective-permute-done.1.m2_ref = f32[32,128]{1,0:T(8,128)S(1)} collective-permute-done((f32[32,128]{1,0:T(8,128)S(1)}, f32[32,128]{1,0:T(8,128)S(1)}, u32[]{:S(2)}, u32[]{:S(2)}) %collective-permute-start.1) | collective-permute-done | bytes 16416 | tf_op jit(solution)/shard_map/ppermute | solution.py:93
  48.2 0.0 collective-permute-done.m1_ref
  48.2 4.2 %all-to-all-done.1 = f32[64,4,128]{2,1,0:T(4,128)S(1)} async-done(((f32[64,4,128]{2,1,0:T(4,128)}), f32[64,4,128]{2,1,0:T(4,128)S(1)}, u32[]{:S(2)}, u32[]{:S(2)}) %all-to-all-start.1) | async-done | bytes 131104 | tf_op jit(solution)/shard_map/all_to_all | solution.py:94
  52.4 0.0 copy-done.2
  52.4 0.6 %copy-done.6 = f32[64,4,128]{2,1,0:T(4,128)} copy-done((f32[64,4,128]{2,1,0:T(4,128)}, f32[64,4,128]{2,1,0:T(4,128)S(1)}, u32[]{:S(2)}) %copy-start.6) | copy-done | bytes 131096
  53.0 1.8 %finish.1 = (f32[16,128]{1,0:T(8,128)}, f32[32,128]{1,0:T(8,128)}) custom-call(f32[256,128]{1,0:T(8,128)} %bitcast.6, f32[32,128]{1,0:T(8,128)} %copy-done.2, f32[32,128]{1,0:T(8,128)} %copy-done.9, f32[32,128]{1,0:T(8,128)} %copy-done.8, f32[32,128]{1,0:T(8,128)} %copy-done.7, s32[16,128]{1,0:T(8,128)} %capacity_ref.1), custom_call_target="tpu_custom_call" | custom-call | tf_op jit(solution)/shard_map/finish/pallas_call | solution.py:97
  (9 shorter events, 0.0 us)
Async XLA Ops:
  0.6 28.2 %copy-start.4 = (s32[1,48]{1,0:T(1,128)S(1)}, s32[1,48]{1,0:T(1,128)}, u32[]{:S(2)}) copy-start(s32[1,48]{1,0:T(1,128)} %local_ref.1) | copy-start | bytes 580
  0.6 28.1 %copy-start.3 = (s32[1,48,1]{1,2,0:T(1,128)S(1)}, s32[1,48,1]{1,2,0:T(1,128)}, u32[]{:S(2)}) copy-start(s32[1,48,1]{1,2,0:T(1,128)} %param.10) | copy-start | bytes 580
  0.7 28.1 %copy-start.5 = (s32[1,48]{1,0:T(1,128)S(1)}, s32[1,48]{1,0:T(1,128)}, u32[]{:S(2)}) copy-start(s32[1,48]{1,0:T(1,128)} %member_ref.1) | copy-start | bytes 580
  0.7 28.1 %copy-start = (bf16[48,128,128]{2,1,0:T(8,128)(2,1)S(1)}, bf16[48,128,128]{2,1,0:T(8,128)(2,1)}, u32[]{:S(2)}) copy-start(bf16[48,128,128]{2,1,0:T(8,128)(2,1)} %cost_ref.1) | copy-start | bytes 4718596
  28.8 1.4 %copy-start.1 = (bf16[48,128,128]{2,1,0:T(8,128)(2,1)S(1)}, bf16[48,128,128]{2,1,0:T(8,128)(2,1)}, u32[]{:S(2)}) copy-start(bf16[48,128,128]{2,1,0:T(8,128)(2,1)} %coef_ref.1) | copy-start | bytes 4718596
  36.6 15.8 %copy-start.2 = (f32[32,128]{1,0:T(8,128)}, f32[32,128]{1,0:T(8,128)S(1)}, u32[]{:S(2)}) copy-start(f32[32,128]{1,0:T(8,128)S(1)} %get-tuple-element.10.m0_ref) | copy-start | bytes 49156
  36.6 15.8 %all-to-all-start.1 = ((f32[64,4,128]{2,1,0:T(4,128)}), f32[64,4,128]{2,1,0:T(4,128)S(1)}, u32[]{:S(2)}, u32[]{:S(2)}) async-start(f32[64,4,128]{2,1,0:T(4,128)} %bitcast.2), calls=%async_computation.1 | async-start | bytes 262144 | tf_op jit(solution)/shard_map/all_to_all | solution.py:94
  41.3 4.2 %collective-permute-start.2 = (f32[32,128]{1,0:T(8,128)S(1)}, f32[32,128]{1,0:T(8,128)S(1)}, u32[]{:S(2)}, u32[]{:S(2)}) collective-permute-start(f32[32,128]{1,0:T(8,128)S(1)} %get-tuple-element.10.m0_ref), channel_id=1, source_target_pairs={{0,3},{1,2},{2,1},{3,0},{4,7},{5,6},{6,5},{7,4},{8,11},{9,10},{10,... | collective-permute-start | bytes 49160 | tf_op jit(solution)/shard_map/ppermute | solution.py:93
  43.8 4.4 %collective-permute-start.1 = (f32[32,128]{1,0:T(8,128)S(1)}, f32[32,128]{1,0:T(8,128)S(1)}, u32[]{:S(2)}, u32[]{:S(2)}) collective-permute-start(f32[32,128]{1,0:T(8,128)S(1)} %get-tuple-element.10.m0_ref), channel_id=1, source_target_pairs={{0,2},{1,3},{2,0},{3,1},{4,6},{5,7},{6,4},{7,5},{8,10},{9,11},{10,... | collective-permute-start | bytes 49160 | tf_op jit(solution)/shard_map/ppermute | solution.py:93
  44.4 3.9 %collective-permute-start = (f32[32,128]{1,0:T(8,128)S(1)}, f32[32,128]{1,0:T(8,128)S(1)}, u32[]{:S(2)}, u32[]{:S(2)}) collective-permute-start(f32[32,128]{1,0:T(8,128)S(1)} %get-tuple-element.10.m0_ref), channel_id=1, source_target_pairs={{0,1},{1,0},{2,3},{3,2},{4,5},{5,4},{6,7},{7,6},{8,9},{9,8},{10,11... | collective-permute-start | bytes 49160 | tf_op jit(solution)/shard_map/ppermute | solution.py:93
  45.4 6.9 %copy-start.7 = (f32[32,128]{1,0:T(8,128)}, f32[32,128]{1,0:T(8,128)S(1)}, u32[]{:S(2)}) copy-start(f32[32,128]{1,0:T(8,128)S(1)} %collective-permute-done.2.m3_ref) | copy-start | bytes 49156
  48.2 4.2 %copy-start.8 = (f32[32,128]{1,0:T(8,128)}, f32[32,128]{1,0:T(8,128)S(1)}, u32[]{:S(2)}) copy-start(f32[32,128]{1,0:T(8,128)S(1)} %collective-permute-done.1.m2_ref) | copy-start | bytes 49156
  48.2 4.2 %copy-start.9 = (f32[32,128]{1,0:T(8,128)}, f32[32,128]{1,0:T(8,128)S(1)}, u32[]{:S(2)}) copy-start(f32[32,128]{1,0:T(8,128)S(1)} %collective-permute-done.m1_ref) | copy-start | bytes 49156
  52.4 0.7 %copy-start.6 = (f32[64,4,128]{2,1,0:T(4,128)}, f32[64,4,128]{2,1,0:T(4,128)S(1)}, u32[]{:S(2)}) copy-start(f32[64,4,128]{2,1,0:T(4,128)S(1)} %all-to-all-done.1) | copy-start | bytes 393220

commit v2 on v1

v2 whole, which is shorter than its diff:
```python
import jax
import jax.numpy as jnp
from jax import lax
from jax.experimental import pallas as pl
from jax.experimental.pallas import tpu as pltpu
from jax.sharding import Mesh, PartitionSpec as P

Z, Y, C, X = 8, 4, 2, 4
CAP = 48
BLOCK = 128
MB_DEV = 32
JB_DEV = 16
MEM = Z * Y * C
ROWS = 4
EARLY = 24
LATE = CAP - EARLY
HALF = Z * Y * JB_DEV
LOCAL, MEMBER, ROW, OTHER, PLACE = (i * CAP for i in range(5))
VMEM = pl.BlockSpec(memory_space=pltpu.VMEM)
SMEM = pl.BlockSpec(memory_space=pltpu.SMEM)
ANY = pl.BlockSpec(memory_space=pl.ANY)


def in_hbm(a):
    return pltpu.with_memory_space_constraint(a, pltpu.HBM)


def in_vmem(a):
    return pltpu.with_memory_space_constraint(a, pltpu.VMEM)


def stage_kernel(
    owner_ref, local_in_ref, member_in_ref, cost_in_ref, coef_in_ref,
    cost_ref, coef_ref, number_ref, count_ref, sem,
):
    load_cost = pltpu.make_async_copy(cost_in_ref.at[pl.ds(0, EARLY)], cost_ref, sem.at[0])
    load_coef = pltpu.make_async_copy(coef_in_ref.at[pl.ds(0, EARLY)], coef_ref, sem.at[1])
    load_cost.start()
    load_coef.start()
    core = lax.axis_index("c")

    def clear(i, carry):
        count_ref[i] = 0
        return carry

    lax.fori_loop(0, MEM, clear, 0)

    def slot(s, carry):
        owner = owner_ref[0, s]
        local = local_in_ref[0, s]
        number_ref[LOCAL + s] = local
        number_ref[MEMBER + s] = member_in_ref[0, s]
        number_ref[ROW + s] = (owner >> 1) * JB_DEV + local
        number_ref[OTHER + s] = (owner & 1) ^ core
        k = count_ref[owner]
        count_ref[owner] = k + 1
        number_ref[PLACE + s] = owner * ROWS + k
        return carry

    lax.fori_loop(0, CAP, slot, 0)
    load_cost.wait()
    load_coef.wait()


def stage_late_kernel(cost_in_ref, coef_in_ref, cost_ref, coef_ref, sem):
    load_cost = pltpu.make_async_copy(cost_in_ref.at[pl.ds(EARLY, LATE)], cost_ref, sem.at[0])
    load_coef = pltpu.make_async_copy(coef_in_ref.at[pl.ds(EARLY, LATE)], coef_ref, sem.at[1])
    load_cost.start()
    load_coef.start()
    load_cost.wait()
    load_coef.wait()


def allocate_kernel(
    number_ref, own_rows_ref, other_rows_ref,
    early_cost_ref, early_coef_ref, late_cost_ref, late_coef_ref,
    primal_ref, send_ref, member_out_ref, slot_ref, column_ref, sums_ref,
):
    send_ref[...] = jnp.full((MEM * ROWS, BLOCK), -1.0, jnp.float32)
    member_out_ref[...] = jnp.zeros((MB_DEV, BLOCK), jnp.float32)
    for s in range(CAP):
        at = pl.ds(number_ref[ROW + s], 1)
        slot_ref[s:s + 1, :] = -jnp.where(number_ref[OTHER + s] == 1, other_rows_ref[at, :], own_rows_ref[at, :])
    ones = jnp.ones((8, 2 * BLOCK), jnp.bfloat16)

    def block(s, cost_ref, coef_ref, at):
        minus_dual = slot_ref[pl.ds(s, 1), :]
        column, parts = None, []
        for g in range(0, BLOCK, 32):
            cost = cost_ref[at, g:g + 32].astype(jnp.float32)
            coef = coef_ref[at, g:g + 32].astype(jnp.float32)
            alloc = jnp.minimum(jnp.maximum(coef * minus_dual - cost, 0.0), 1.0)
            high = alloc.astype(jnp.bfloat16)
            primal_ref[s, g:g + 32] = high
            rest = (alloc - high.astype(jnp.float32)).astype(jnp.bfloat16)
            parts.append(jnp.concatenate([high, rest], axis=1))
            part = jnp.sum((coef * alloc).reshape(4, 8, BLOCK), axis=0)
            column = part if column is None else column + part
        column_ref[pl.ds(pl.multiple_of(s * 8, 8), 8), :] = column
        return parts

    def run(first, count, cost_ref, coef_ref, unroll):
        def pair(i, carry):
            s = first + 2 * i
            parts = block(s, cost_ref, coef_ref, 2 * i) + block(s + 1, cost_ref, coef_ref, 2 * i + 1)
            both = jnp.concatenate(parts, axis=0)
            sums = lax.dot_general(ones, both, (((1,), (1,)), ((), ())), preferred_element_type=jnp.float32)
            sums_ref[pl.ds(s, 1), :] = sums[0:1, :BLOCK]
            sums_ref[pl.ds(s + 1, 1), :] = sums[0:1, BLOCK:]
            return carry

        lax.fori_loop(0, count // 2, pair, 0, unroll=unroll)

    run(0, EARLY, early_cost_ref, early_coef_ref, 12)
    run(EARLY, LATE, late_cost_ref, late_coef_ref, 12)
    slot_ref[...] = jnp.sum(column_ref[...].reshape(CAP, 8, BLOCK), axis=1)
    for s in range(CAP):
        place = number_ref[PLACE + s]
        send_ref[pl.ds(place, 1), :] = slot_ref[s:s + 1, :]
        send_ref[pl.ds(place + 2, 1), :] = jnp.full((1, BLOCK), number_ref[LOCAL + s].astype(jnp.float32))
        member_out_ref[pl.ds(number_ref[MEMBER + s], 1), :] += sums_ref[s:s + 1, :]


def finish_kernel(recv_ref, m0_ref, m1_ref, m2_ref, m3_ref, capacity_ref, gradient_ref, share_ref):
    share_ref[...] = ((m0_ref[...] + m1_ref[...]) + (m2_ref[...] + m3_ref[...])) * (1.0 / BLOCK)
    sub = lax.broadcasted_iota(jnp.int32, (8, BLOCK), 0) % 4
    data = sub < 2
    totals = [jnp.zeros((8, BLOCK), jnp.float32) for _ in range(JB_DEV)]
    for i in range(MEM * ROWS // 8):
        got = recv_ref[i * 8:(i + 1) * 8, :]
        name = jnp.where(data, pltpu.roll(got, 6, 0), -1.0)
        for k in range(JB_DEV):
            totals[k] = totals[k] + jnp.where(name == float(k), got, 0.0)
    summed = jnp.concatenate([jnp.sum(t, axis=0, keepdims=True) for t in totals], axis=0)
    gradient_ref[...] = summed - capacity_ref[...].astype(jnp.float32)


def stage(owner, local, member, cost, coef):
    early = pltpu.VMEM((EARLY, BLOCK, BLOCK), jnp.bfloat16)
    return pl.pallas_call(
        stage_kernel,
        out_shape=(early, early, jax.ShapeDtypeStruct((5 * CAP,), jnp.int32)),
        in_specs=[SMEM] * 3 + [ANY] * 2,
        out_specs=(VMEM, VMEM, SMEM),
        scratch_shapes=[pltpu.SMEM((MEM,), jnp.int32), pltpu.SemaphoreType.DMA((2,))],
        compiler_params=pltpu.CompilerParams(vmem_limit_bytes=4 * 1024 * 1024),
        cost_estimate=pl.CostEstimate(flops=0, bytes_accessed=8 * EARLY * BLOCK * BLOCK, transcendentals=0),
        name="stage",
    )(owner, local, member, in_hbm(cost), in_hbm(coef))


def stage_late(cost, coef):
    late = pltpu.VMEM((LATE, BLOCK, BLOCK), jnp.bfloat16)
    return pl.pallas_call(
        stage_late_kernel,
        out_shape=(late, late),
        in_specs=[ANY] * 2,
        out_specs=(VMEM, VMEM),
        scratch_shapes=[pltpu.SemaphoreType.DMA((2,))],
        compiler_params=pltpu.CompilerParams(vmem_limit_bytes=4 * 1024 * 1024),
        cost_estimate=pl.CostEstimate(flops=0, bytes_accessed=8 * LATE * BLOCK * BLOCK, transcendentals=0),
        name="stage_late",
    )(in_hbm(cost), in_hbm(coef))


def allocate(number, *blocks):
    return pl.pallas_call(
        allocate_kernel,
        out_shape=(
            pltpu.VMEM((CAP, BLOCK, BLOCK), jnp.bfloat16),
            jax.ShapeDtypeStruct((MEM * ROWS, BLOCK), jnp.float32),
            pltpu.VMEM((MB_DEV, BLOCK), jnp.float32),
        ),
        in_specs=[SMEM] + [VMEM] * 6,
        out_specs=(VMEM, VMEM, VMEM),
        scratch_shapes=[
            pltpu.VMEM((CAP, BLOCK), jnp.float32),
            pltpu.VMEM((CAP * 8, BLOCK), jnp.float32),
            pltpu.VMEM((CAP, BLOCK), jnp.float32),
        ],
        compiler_params=pltpu.CompilerParams(vmem_limit_bytes=8 * 1024 * 1024),
        cost_estimate=pl.CostEstimate(
            flops=8 * CAP * BLOCK * BLOCK, bytes_accessed=6 * CAP * BLOCK * BLOCK, transcendentals=0
        ),
        name="allocate",
    )(number, *map(in_vmem, blocks))


def finish(recv, share, others, capacity):
    return pl.pallas_call(
        finish_kernel,
        out_shape=(
            jax.ShapeDtypeStruct((JB_DEV, BLOCK), jnp.float32),
            jax.ShapeDtypeStruct((MB_DEV, BLOCK), jnp.float32),
        ),
        in_specs=[VMEM] * 6,
        out_specs=(VMEM, VMEM),
        compiler_params=pltpu.CompilerParams(vmem_limit_bytes=2 * 1024 * 1024),
        name="finish",
    )(recv, share, *others, capacity)


def per_device(pair_cost, pair_coef, slot_member, slot_owner, slot_local, duals, capacity):
    copies = jnp.broadcast_to(duals[None], (Z * Y, JB_DEV, BLOCK))
    rows = lax.all_to_all(copies, ("z", "y"), split_axis=0, concat_axis=0, tiled=True).reshape(HALF, BLOCK)
    cost, coef, number = stage(
        slot_owner.reshape(1, CAP), slot_local, slot_member, pair_cost, pair_coef
    )
    rows, number, late_cost, late_coef = lax.optimization_barrier((rows, number, pair_cost, pair_coef))
    other_rows = lax.ppermute(rows, "c", [(0, 1), (1, 0)])
    late_cost, late_coef = stage_late(late_cost, late_coef)
    primal, send, share = allocate(number, rows, other_rows, cost, coef, late_cost, late_coef)
    others = [lax.ppermute(share, "x", [(i, i ^ k) for i in range(X)]) for k in (1, 2, 3)]
    recv = lax.all_to_all(
        send.reshape(MEM, ROWS, BLOCK), ("z", "y", "c"), split_axis=0, concat_axis=0, tiled=True
    ).reshape(MEM * ROWS, BLOCK)
    gradient, share = finish(recv, share, others, capacity)
    return primal, gradient, share


def solution(mesh):
    axes = ("z", "y", "c", "x")
    fine = Mesh(mesh.devices.reshape(Z, Y, C, X), axes)
    each = lambda n: P(axes, *([None] * (n - 1)))
    return jax.shard_map(
        per_device,
        mesh=fine,
        in_specs=(each(3), each(3), each(2), each(3), each(2), each(2), each(2)),
        out_specs=(each(3), each(2), P(("z", "y", "c"), None)),
        check_vma=False,
    )
```

time: 55.1 us -> 48.3 us (0.88)
  blocking collectives: 27.3 us -> 0 us
  starting transfers between devices: 7.98 us -> 22.2 us
  waiting for transfers between devices: 7.76 us -> 13.3 us
  local copies, waits for them, and re-layouts: 2.9 us -> 4.52 us
  Pallas kernels: 8.19 us -> 7.18 us
    all_to_all x1 -> x0, blocking collectives: 23 us -> none  [per_device(): lax.all_to_all(copies, ('z', 'y'), split_axis=0, concat_axis=0, tiled=True)]
    all_to_all x0 -> x1, starting transfers between devices: none -> 12 us  [per_device(): lax.all_to_all(copies, ('z', 'y'), split_axis=0, concat_axis=0, tiled=True)]
    all_to_all x0 -> x1, waiting for transfers between devices: none -> 6.67 us  [per_device(): lax.all_to_all(copies, ('z', 'y'), split_axis=0, concat_axis=0, tiled=True)]
    all_gather x1 -> x0, blocking collectives: 4.25 us -> none  [per_device(): lax.all_gather(rows.reshape(Z * Y * JB_DEV, BLOCK), 'c', axis=0, tiled=True)]
    ppermute x3 -> x4, starting transfers between devices: 3.34 us -> 5.79 us  [the longest x3 3.34 us: per_device(): lax.ppermute(share, 'x', [(i, i ^ k) for i in range(X)])]
    ppermute x3 -> x4, waiting for transfers between devices: 3.61 us -> 2.47 us  [the longest x3 2.47 us: per_device(): lax.ppermute(share, 'x', [(i, i ^ k) for i in range(X)])]
    unnamed x20 -> x9, local copies, waits for them, and re-layouts: 2.07 us -> 3.11 us
    pallas_call x2 -> x4, Pallas kernels: 8.19 us -> 7.18 us  [the longest x1 2.54 us: stage(): pl.pallas_call(stage_kernel, out_shape=(early, early, jax.ShapeDtypeStruc...]
  transfers between devices with their start and end apart: 4 -> 6, of which waited for: 3 -> 3; matrix products, arithmetic and copies ran while one was open for 0% -> 2% of each run, Pallas kernels for 0% -> 8%
where the time goes in v2:
time: 48.3 us; the launch traced here: 47.9 us
  starting transfers between devices  22.2 us (46%)
  waiting for transfers between devices  13.3 us (28%)
  Pallas kernels  7.18 us (15%)
  local copies, waits for them, and re-layouts  4.52 us (9%)
  between operations  0.69 us (1%)
    all_to_all x1, starting transfers between devices, per_device(): lax.all_to_all(copies, ('z', 'y'), split_axis=0, concat_axis=0, tiled=True)  12 us
    all_to_all x1, waiting for transfers between devices, per_device(): lax.all_to_all(copies, ('z', 'y'), split_axis=0, concat_axis=0, tiled=True)  6.67 us
    all_to_all x1, starting transfers between devices, per_device(): lax.all_to_all(send.reshape(MEM, ROWS, BLOCK), ('z', 'y', 'c'), split_axi...  4.41 us
    all_to_all x1, waiting for transfers between devices, per_device(): lax.all_to_all(send.reshape(MEM, ROWS, BLOCK), ('z', 'y', 'c'), split_axi...  4.16 us
    ppermute x3, starting transfers between devices, per_device(): lax.ppermute(share, 'x', [(i, i ^ k) for i in range(X)])  3.34 us
    unnamed x9, local copies, waits for them, and re-layouts  3.11 us
    pallas_call x1, Pallas kernels, stage(): pl.pallas_call(stage_kernel, out_shape=(early, early, jax.ShapeDtypeStruc...  2.54 us
    ppermute x3, waiting for transfers between devices, per_device(): lax.ppermute(share, 'x', [(i, i ^ k) for i in range(X)])  2.47 us
  transfers between devices with their start and end apart: 6, of which 3 were waited for; matrix products, arithmetic and copies ran while one was open for 2% of the time, Pallas kernels for 8%

profile of v2, /device:TPU:1, one launch (start us, length us, event | category | flops | bytes accessed | tf_op | source)
XLA Modules:
  0.0 47.9 jit_solution(4335474327685323712)
XLA Ops:
  0.6 1.4 %broadcast_in_dim.2 = f32[32,16,128]{2,1,0:T(8,128)} broadcast(f32[16,128]{1,0:T(8,128)} %param.12), dimensions={1,2} | broadcast | bytes 270336 | tf_op jit(solution)/shard_map/broadcast_in_dim | solution.py:204
  2.0 12.0 %all-to-all-start = ((f32[32,16,128]{2,1,0:T(8,128)}), f32[32,16,128]{2,1,0:T(8,128)S(1)}, u32[]{:S(2)}, u32[]{:S(2)}) async-start(f32[32,16,128]{2,1,0:T(8,128)} %broadcast_in_dim.2), calls=%async_computation | async-start | bytes 524288 | tf_op jit(solution)/shard_map/all_to_all | solution.py:205
  14.1 0.0 copy-start.1
  14.1 0.6 %copy-done.1 = s32[1,48,1]{1,2,0:T(1,128)S(1)} copy-done((s32[1,48,1]{1,2,0:T(1,128)S(1)}, s32[1,48,1]{1,2,0:T(1,128)}, u32[]{:S(2)}) %copy-start.1) | copy-done | bytes 216
  14.7 0.0 copy-start.2
  14.7 0.7 %copy-done.2 = s32[1,48]{1,0:T(1,128)S(1)} copy-done((s32[1,48]{1,0:T(1,128)S(1)}, s32[1,48]{1,0:T(1,128)}, u32[]{:S(2)}) %copy-start.2) | copy-done | bytes 216
  15.4 0.7 %copy-done.3 = s32[1,48]{1,0:T(1,128)S(1)} copy-done((s32[1,48]{1,0:T(1,128)S(1)}, s32[1,48]{1,0:T(1,128)}, u32[]{:S(2)}) %copy-start.3) | copy-done | bytes 216
  16.1 2.5 %stage.1 = (bf16[24,128,128]{2,1,0:T(8,128)(2,1)S(1)}, bf16[24,128,128]{2,1,0:T(8,128)(2,1)S(1)}, s32[240]{0:T(256)S(1)}) custom-call(s32[1,48]{1,0:T(1,128)S(1)} %bitcast.7, s32[1,48]{1,0:T(1,128)S(1)} %copy-done.2, s32[1,48]{1,0:T(1,128)S(1)} %copy-done.3, bf16[48,128,128]{2,1,0:T(8,128)(2,1)} %cost_in_ref.2, bf16[48,128,128]{2,1,0:T(8,128)(2,1)} %coef_in_ref.2), custom_call_target="tpu_custom_call" | custom-call | bytes 3145728 | tf_op jit(solution)/shard_map/stage/pallas_call | solution.py:140
  18.6 6.7 %all-to-all-done = f32[32,16,128]{2,1,0:T(8,128)S(1)} async-done(((f32[32,16,128]{2,1,0:T(8,128)}), f32[32,16,128]{2,1,0:T(8,128)S(1)}, u32[]{:S(2)}, u32[]{:S(2)}) %all-to-all-start) | async-done | bytes 262176 | tf_op jit(solution)/shard_map/all_to_all | solution.py:205
  25.3 2.5 %collective-permute-start = (f32[512,128]{1,0:T(8,128)S(1)}, f32[512,128]{1,0:T(8,128)S(1)}, u32[]{:S(2)}, u32[]{:S(2)}) collective-permute-start(f32[512,128]{1,0:T(8,128)S(1)} %bitcast.4), channel_id=1, source_target_pairs={{0,4},{4,0},{1,5},{5,1},{2,6},{6,2},{3,7},{7,3},{8,12},{12,8},{9,1... | collective-permute-start | bytes 786440 | tf_op jit(solution)/shard_map/ppermute | solution.py:210
  27.7 1.4 %stage_late.1 = (bf16[24,128,128]{2,1,0:T(8,128)(2,1)S(1)}, bf16[24,128,128]{2,1,0:T(8,128)(2,1)S(1)}) custom-call(bf16[48,128,128]{2,1,0:T(8,128)(2,1)} %cost_in_ref.2, bf16[48,128,128]{2,1,0:T(8,128)(2,1)} %coef_in_ref.2), custom_call_target="tpu_custom_call" | custom-call | bytes 3145728 | tf_op jit(solution)/shard_map/stage_late/pallas_call | solution.py:154
  29.1 0.0 collective-permute-done.other_rows_ref
  29.1 2.4 %allocate.1 = (bf16[48,128,128]{2,1,0:T(8,128)(2,1)S(1)}, f32[256,128]{1,0:T(8,128)}, f32[32,128]{1,0:T(8,128)S(1)}) custom-call(s32[240]{0:T(256)S(1)} %get-tuple-element.18.number_ref, f32[512,128]{1,0:T(8,128)S(1)} %bitcast.5, f32[512,128]{1,0:T(8,128)S(1)} %collective-permute-done.other_rows_ref, ...), custom_call_target="tpu_custom_call" | custom-call | flops 6291456 | bytes 4718592 | tf_op jit(solution)/shard_map/allocate/pallas_call | solution.py:167
  31.6 4.4 %all-to-all-start.1 = ((f32[64,4,128]{2,1,0:T(4,128)}), f32[64,4,128]{2,1,0:T(4,128)S(1)}, u32[]{:S(2)}, u32[]{:S(2)}) async-start(f32[64,4,128]{2,1,0:T(4,128)} %bitcast.2), calls=%async_computation.1 | async-start | bytes 262144 | tf_op jit(solution)/shard_map/all_to_all | solution.py:214
  36.0 2.6 %collective-permute-start.3 = (f32[32,128]{1,0:T(8,128)S(1)}, f32[32,128]{1,0:T(8,128)S(1)}, u32[]{:S(2)}, u32[]{:S(2)}) collective-permute-start(f32[32,128]{1,0:T(8,128)S(1)} %get-tuple-element.28.m0_ref), channel_id=1, source_target_pairs={{0,3},{1,2},{2,1},{3,0},{4,7},{5,6},{6,5},{7,4},{8,11},{9,10},{10,... | collective-permute-start | bytes 49160 | tf_op jit(solution)/shard_map/ppermute | solution.py:213
  38.5 0.5 %collective-permute-start.2 = (f32[32,128]{1,0:T(8,128)S(1)}, f32[32,128]{1,0:T(8,128)S(1)}, u32[]{:S(2)}, u32[]{:S(2)}) collective-permute-start(f32[32,128]{1,0:T(8,128)S(1)} %get-tuple-element.28.m0_ref), channel_id=1, source_target_pairs={{0,2},{1,3},{2,0},{3,1},{4,6},{5,7},{6,4},{7,5},{8,10},{9,11},{10,... | collective-permute-start | bytes 49160 | tf_op jit(solution)/shard_map/ppermute | solution.py:213
  39.1 0.3 collective-permute-start.1
  39.3 1.1 %copy.10 = bf16[48,128,128]{2,1,0:T(8,128)(2,1)} copy(bf16[48,128,128]{2,1,0:T(8,128)(2,1)S(1)} %get-tuple-element.31) | data formatting | bytes 3145728
  40.5 0.0 collective-permute-done.3.m3_ref
  40.5 2.5 %collective-permute-done.2.m2_ref = f32[32,128]{1,0:T(8,128)S(1)} collective-permute-done((f32[32,128]{1,0:T(8,128)S(1)}, f32[32,128]{1,0:T(8,128)S(1)}, u32[]{:S(2)}, u32[]{:S(2)}) %collective-permute-start.2) | collective-permute-done | bytes 16416 | tf_op jit(solution)/shard_map/ppermute | solution.py:213
  42.9 0.0 collective-permute-done.1.m1_ref
  42.9 4.2 %all-to-all-done.1 = f32[64,4,128]{2,1,0:T(4,128)S(1)} async-done(((f32[64,4,128]{2,1,0:T(4,128)}), f32[64,4,128]{2,1,0:T(4,128)S(1)}, u32[]{:S(2)}, u32[]{:S(2)}) %all-to-all-start.1) | async-done | bytes 131104 | tf_op jit(solution)/shard_map/all_to_all | solution.py:214
  47.1 0.0 copy-done
  47.1 0.8 %finish.1 = (f32[16,128]{1,0:T(8,128)}, f32[32,128]{1,0:T(8,128)}) custom-call(f32[256,128]{1,0:T(8,128)S(1)} %bitcast.6, f32[32,128]{1,0:T(8,128)S(1)} %get-tuple-element.28.m0_ref, f32[32,128]{1,0:T(8,128)S(1)} %collective-permute-done.1.m1_ref, f32[32,128]{1,0:T(8,128)S(1)} %collective-permute-done.2.m2_ref, f32[32,128]{1,0:T(8,128)S(1)} %collective-permute-done.3.m3_ref, ...), custom_call_target="tpu_custom_call" | custom-call | tf_op jit(solution)/shard_map/finish/pallas_call | solution.py:190
  (2 shorter events, 0.0 us)
Async XLA Ops:
  2.0 23.2 %all-to-all-start = ((f32[32,16,128]{2,1,0:T(8,128)}), f32[32,16,128]{2,1,0:T(8,128)S(1)}, u32[]{:S(2)}, u32[]{:S(2)}) async-start(f32[32,16,128]{2,1,0:T(8,128)} %broadcast_in_dim.2), calls=%async_computation | async-start | bytes 524288 | tf_op jit(solution)/shard_map/all_to_all | solution.py:205
  14.1 0.7 %copy-start.1 = (s32[1,48,1]{1,2,0:T(1,128)S(1)}, s32[1,48,1]{1,2,0:T(1,128)}, u32[]{:S(2)}) copy-start(s32[1,48,1]{1,2,0:T(1,128)} %param.10) | copy-start | bytes 580
  14.7 0.7 %copy-start.2 = (s32[1,48]{1,0:T(1,128)S(1)}, s32[1,48]{1,0:T(1,128)}, u32[]{:S(2)}) copy-start(s32[1,48]{1,0:T(1,128)} %local_in_ref.1) | copy-start | bytes 580
  15.4 0.7 %copy-start.3 = (s32[1,48]{1,0:T(1,128)S(1)}, s32[1,48]{1,0:T(1,128)}, u32[]{:S(2)}) copy-start(s32[1,48]{1,0:T(1,128)} %member_in_ref.1) | copy-start | bytes 580
  25.3 3.8 %collective-permute-start = (f32[512,128]{1,0:T(8,128)S(1)}, f32[512,128]{1,0:T(8,128)S(1)}, u32[]{:S(2)}, u32[]{:S(2)}) collective-permute-start(f32[512,128]{1,0:T(8,128)S(1)} %bitcast.4), channel_id=1, source_target_pairs={{0,4},{4,0},{1,5},{5,1},{2,6},{6,2},{3,7},{7,3},{8,12},{12,8},{9,1... | collective-permute-start | bytes 786440 | tf_op jit(solution)/shard_map/ppermute | solution.py:210
  31.6 15.5 %all-to-all-start.1 = ((f32[64,4,128]{2,1,0:T(4,128)}), f32[64,4,128]{2,1,0:T(4,128)S(1)}, u32[]{:S(2)}, u32[]{:S(2)}) async-start(f32[64,4,128]{2,1,0:T(4,128)} %bitcast.2), calls=%async_computation.1 | async-start | bytes 262144 | tf_op jit(solution)/shard_map/all_to_all | solution.py:214
  36.0 4.5 %collective-permute-start.3 = (f32[32,128]{1,0:T(8,128)S(1)}, f32[32,128]{1,0:T(8,128)S(1)}, u32[]{:S(2)}, u32[]{:S(2)}) collective-permute-start(f32[32,128]{1,0:T(8,128)S(1)} %get-tuple-element.28.m0_ref), channel_id=1, source_target_pairs={{0,3},{1,2},{2,1},{3,0},{4,7},{5,6},{6,5},{7,4},{8,11},{9,10},{10,... | collective-permute-start | bytes 49160 | tf_op jit(solution)/shard_map/ppermute | solution.py:213
  38.5 4.4 %collective-permute-start.2 = (f32[32,128]{1,0:T(8,128)S(1)}, f32[32,128]{1,0:T(8,128)S(1)}, u32[]{:S(2)}, u32[]{:S(2)}) collective-permute-start(f32[32,128]{1,0:T(8,128)S(1)} %get-tuple-element.28.m0_ref), channel_id=1, source_target_pairs={{0,2},{1,3},{2,0},{3,1},{4,6},{5,7},{6,4},{7,5},{8,10},{9,11},{10,... | collective-permute-start | bytes 49160 | tf_op jit(solution)/shard_map/ppermute | solution.py:213
  39.1 3.9 %collective-permute-start.1 = (f32[32,128]{1,0:T(8,128)S(1)}, f32[32,128]{1,0:T(8,128)S(1)}, u32[]{:S(2)}, u32[]{:S(2)}) collective-permute-start(f32[32,128]{1,0:T(8,128)S(1)} %get-tuple-element.28.m0_ref), channel_id=1, source_target_pairs={{0,1},{1,0},{2,3},{3,2},{4,5},{5,4},{6,7},{7,6},{8,9},{9,8},{10,11... | collective-permute-start | bytes 49160 | tf_op jit(solution)/shard_map/ppermute | solution.py:213
  39.3 7.8 %copy-start = (s32[16,128]{1,0:T(8,128)S(1)}, s32[16,128]{1,0:T(8,128)}, u32[]{:S(2)}) copy-start(s32[16,128]{1,0:T(8,128)} %capacity_ref.1) | copy-start | bytes 24580

commit v3 on v2

--- a/solution.py
+++ b/solution.py
@@ -11,11 +11,12 @@
 MB_DEV = 32
 JB_DEV = 16
 MEM = Z * Y * C
-ROWS = 4
+ROWS = 3
+MIB = 1024 * 1024
 EARLY = 24
 LATE = CAP - EARLY
 HALF = Z * Y * JB_DEV
-LOCAL, MEMBER, ROW, OTHER, PLACE = (i * CAP for i in range(5))
+MEMBER, ROW, OTHER, PLACE = (i * CAP for i in range(4))
 VMEM = pl.BlockSpec(memory_space=pltpu.VMEM)
 SMEM = pl.BlockSpec(memory_space=pltpu.SMEM)
 ANY = pl.BlockSpec(memory_space=pl.ANY)
@@ -29,15 +30,44 @@
     return pltpu.with_memory_space_constraint(a, pltpu.VMEM)
 
 
+def spread_kernel(duals_ref, out_ref, one_ref, many_ref, sem):
+    load = pltpu.make_async_copy(duals_ref, one_ref, sem.at[0])
+    load.start()
+    load.wait()
+    many_ref[...] = jnp.broadcast_to(one_ref[...][None], many_ref.shape)
+    store = pltpu.make_async_copy(many_ref, out_ref, sem.at[1])
+    store.start()
+    store.wait()
+
+
+def spread(duals):
+    copies = (Z * Y, JB_DEV, BLOCK)
+    return pl.pallas_call(
+        spread_kernel,
+        out_shape=jax.ShapeDtypeStruct(copies, jnp.float32),
+        in_specs=[ANY],
+        out_specs=ANY,
+        scratch_shapes=[
+            pltpu.VMEM((JB_DEV, BLOCK), jnp.float32),
+            pltpu.VMEM(copies, jnp.float32),
+            pltpu.SemaphoreType.DMA((2,)),
+        ],
+        compiler_params=pltpu.CompilerParams(vmem_limit_bytes=2 * MIB),
+        name="spread",
+    )(in_hbm(duals))
+
+
 def stage_kernel(
     owner_ref, local_in_ref, member_in_ref, cost_in_ref, coef_in_ref,
-    cost_ref, coef_ref, number_ref, count_ref, sem,
+    cost_ref, coef_ref, named_ref, number_ref, count_ref, sem,
 ):
     load_cost = pltpu.make_async_copy(cost_in_ref.at[pl.ds(0, EARLY)], cost_ref, sem.at[0])
     load_coef = pltpu.make_async_copy(coef_in_ref.at[pl.ds(0, EARLY)], coef_ref, sem.at[1])
     load_cost.start()
     load_coef.start()
     core = lax.axis_index("c")
+    lane = lax.broadcasted_iota(jnp.int32, (1, BLOCK), 1)
+    named_ref[...] = jnp.full((MEM, 1, BLOCK), -1.0, jnp.float32)
 
     def clear(i, carry):
         count_ref[i] = 0
@@ -48,13 +78,14 @@
     def slot(s, carry):
         owner = owner_ref[0, s]
         local = local_in_ref[0, s]
-        number_ref[LOCAL + s] = local
         number_ref[MEMBER + s] = member_in_ref[0, s]
         number_ref[ROW + s] = (owner >> 1) * JB_DEV + local
         number_ref[OTHER + s] = (owner & 1) ^ core
         k = count_ref[owner]
         count_ref[owner] = k + 1
         number_ref[PLACE + s] = owner * ROWS + k
+        half = (lane >= BLOCK // 2) == (k == 1)
+        named_ref[owner] = jnp.where(half, local.astype(jnp.float32), named_ref[owner])
         return carry
 
     lax.fori_loop(0, CAP, slot, 0)
@@ -72,11 +103,13 @@
 
 
 def allocate_kernel(
-    number_ref, own_rows_ref, other_rows_ref,
+    number_ref, named_ref, own_rows_ref, other_rows_ref,
     early_cost_ref, early_coef_ref, late_cost_ref, late_coef_ref,
     primal_ref, send_ref, member_out_ref, slot_ref, column_ref, sums_ref,
 ):
-    send_ref[...] = jnp.full((MEM * ROWS, BLOCK), -1.0, jnp.float32)
+    send_ref[...] = jnp.zeros((MEM * ROWS, 1, BLOCK), jnp.float32)
+    for i in range(MEM):
+        send_ref[i * ROWS + 2] = named_ref[i]
     member_out_ref[...] = jnp.zeros((MB_DEV, BLOCK), jnp.float32)
     for s in range(CAP):
         at = pl.ds(number_ref[ROW + s], 1)
@@ -115,22 +148,22 @@
     run(EARLY, LATE, late_cost_ref, late_coef_ref, 12)
     slot_ref[...] = jnp.sum(column_ref[...].reshape(CAP, 8, BLOCK), axis=1)
     for s in range(CAP):
-        place = number_ref[PLACE + s]
-        send_ref[pl.ds(place, 1), :] = slot_ref[s:s + 1, :]
-        send_ref[pl.ds(place + 2, 1), :] = jnp.full((1, BLOCK), number_ref[LOCAL + s].astype(jnp.float32))
+        send_ref[number_ref[PLACE + s]] = slot_ref[s:s + 1, :]
         member_out_ref[pl.ds(number_ref[MEMBER + s], 1), :] += sums_ref[s:s + 1, :]
 
 
 def finish_kernel(recv_ref, m0_ref, m1_ref, m2_ref, m3_ref, capacity_ref, gradient_ref, share_ref):
     share_ref[...] = ((m0_ref[...] + m1_ref[...]) + (m2_ref[...] + m3_ref[...])) * (1.0 / BLOCK)
-    sub = lax.broadcasted_iota(jnp.int32, (8, BLOCK), 0) % 4
-    data = sub < 2
+    low = lax.broadcasted_iota(jnp.int32, (8, BLOCK), 1) < BLOCK // 2
     totals = [jnp.zeros((8, BLOCK), jnp.float32) for _ in range(JB_DEV)]
-    for i in range(MEM * ROWS // 8):
-        got = recv_ref[i * 8:(i + 1) * 8, :]
-        name = jnp.where(data, pltpu.roll(got, 6, 0), -1.0)
+    for i in range(0, MEM, 8):
+        first, second, named = (recv_ref[i:i + 8, 0, j * BLOCK:(j + 1) * BLOCK] for j in range(ROWS))
+        turned = pltpu.roll(named, BLOCK // 2, 1)
+        name_first = jnp.where(low, named, turned)
+        name_second = jnp.where(low, turned, named)
         for k in range(JB_DEV):
-            totals[k] = totals[k] + jnp.where(name == float(k), got, 0.0)
+            totals[k] = totals[k] + jnp.where(name_first == float(k), first, 0.0)
+            totals[k] = totals[k] + jnp.where(name_second == float(k), second, 0.0)
     summed = jnp.concatenate([jnp.sum(t, axis=0, keepdims=True) for t in totals], axis=0)
     gradient_ref[...] = summed - capacity_ref[...].astype(jnp.float32)
 
@@ -139,9 +172,14 @@
     early = pltpu.VMEM((EARLY, BLOCK, BLOCK), jnp.bfloat16)
     return pl.pallas_call(
         stage_kernel,
-        out_shape=(early, early, jax.ShapeDtypeStruct((5 * CAP,), jnp.int32)),
+        out_shape=(
+            early,
+            early,
+            pltpu.VMEM((MEM, 1, BLOCK), jnp.float32),
+            jax.ShapeDtypeStruct((4 * CAP,), jnp.int32),
+        ),
         in_specs=[SMEM] * 3 + [ANY] * 2,
-        out_specs=(VMEM, VMEM, SMEM),
+        out_specs=(VMEM, VMEM, VMEM, SMEM),
         scratch_shapes=[pltpu.SMEM((MEM,), jnp.int32), pltpu.SemaphoreType.DMA((2,))],
         compiler_params=pltpu.CompilerParams(vmem_limit_bytes=4 * 1024 * 1024),
         cost_estimate=pl.CostEstimate(flops=0, bytes_accessed=8 * EARLY * BLOCK * BLOCK, transcendentals=0),
@@ -168,10 +206,10 @@
         allocate_kernel,
         out_shape=(
             pltpu.VMEM((CAP, BLOCK, BLOCK), jnp.bfloat16),
-            jax.ShapeDtypeStruct((MEM * ROWS, BLOCK), jnp.float32),
+            jax.ShapeDtypeStruct((MEM * ROWS, 1, BLOCK), jnp.float32),
             pltpu.VMEM((MB_DEV, BLOCK), jnp.float32),
         ),
-        in_specs=[SMEM] + [VMEM] * 6,
+        in_specs=[SMEM] + [VMEM] * 7,
         out_specs=(VMEM, VMEM, VMEM),
         scratch_shapes=[
             pltpu.VMEM((CAP, BLOCK), jnp.float32),
@@ -201,19 +239,18 @@
 
 
 def per_device(pair_cost, pair_coef, slot_member, slot_owner, slot_local, duals, capacity):
-    copies = jnp.broadcast_to(duals[None], (Z * Y, JB_DEV, BLOCK))
+    copies = spread(duals)
     rows = lax.all_to_all(copies, ("z", "y"), split_axis=0, concat_axis=0, tiled=True).reshape(HALF, BLOCK)
-    cost, coef, number = stage(
+    cost, coef, named, number = stage(
         slot_owner.reshape(1, CAP), slot_local, slot_member, pair_cost, pair_coef
     )
     rows, number, late_cost, late_coef = lax.optimization_barrier((rows, number, pair_cost, pair_coef))
     other_rows = lax.ppermute(rows, "c", [(0, 1), (1, 0)])
     late_cost, late_coef = stage_late(late_cost, late_coef)
-    primal, send, share = allocate(number, rows, other_rows, cost, coef, late_cost, late_coef)
+    primal, send, share = allocate(number, named, rows, other_rows, cost, coef, late_cost, late_coef)
     others = [lax.ppermute(share, "x", [(i, i ^ k) for i in range(X)]) for k in (1, 2, 3)]
-    recv = lax.all_to_all(
-        send.reshape(MEM, ROWS, BLOCK), ("z", "y", "c"), split_axis=0, concat_axis=0, tiled=True
-    ).reshape(MEM * ROWS, BLOCK)
+    send = send.reshape(MEM, 1, ROWS * BLOCK)
+    recv = lax.all_to_all(send, ("z", "y", "c"), split_axis=0, concat_axis=0, tiled=True)
     gradient, share = finish(recv, share, others, capacity)
     return primal, gradient, share
 

time: 48.3 us -> 47.8 us (0.990)
  Pallas kernels: 7.18 us -> 8.63 us
  local copies, waits for them, and re-layouts: 4.52 us -> 3.11 us
  waiting for transfers between devices: 13.3 us -> 12.7 us
    pallas_call x1 -> x2, Pallas kernels: 2.54 us -> 3.97 us  [the longest x1 2.54 us: stage(): pl.pallas_call(stage_kernel, out_shape=(early, early, pltpu.VMEM((MEM, 1,...]
    broadcast_in_dim x1 -> x0, local copies, waits for them, and re-layouts: 1.42 us -> none  [per_device(): copies = jnp.broadcast_to(duals[None], (Z * Y, JB_DEV, BLOCK))]
    all_to_all x1, waiting for transfers between devices: 4.16 us -> 3.6 us  [per_device(): lax.all_to_all(send, ('z', 'y', 'c'), split_axis=0, concat_axis=0, tiled=...]
where the time goes in v3:
time: 47.8 us; the launch traced here: 47.4 us
  starting transfers between devices  22.2 us (46%)
  waiting for transfers between devices  12.7 us (27%)
  Pallas kernels  8.63 us (18%)
  local copies, waits for them, and re-layouts  3.11 us (7%)
  between operations  0.69 us (1%)
    all_to_all x1, starting transfers between devices, per_device(): lax.all_to_all(copies, ('z', 'y'), split_axis=0, concat_axis=0, tiled=True)  12 us
    all_to_all x1, waiting for transfers between devices, per_device(): lax.all_to_all(copies, ('z', 'y'), split_axis=0, concat_axis=0, tiled=True)  6.67 us
    all_to_all x1, starting transfers between devices, per_device(): lax.all_to_all(send, ('z', 'y', 'c'), split_axis=0, concat_axis=0, tiled=...  4.41 us
    all_to_all x1, waiting for transfers between devices, per_device(): lax.all_to_all(send, ('z', 'y', 'c'), split_axis=0, concat_axis=0, tiled=...  3.6 us
    ppermute x3, starting transfers between devices, per_device(): lax.ppermute(share, 'x', [(i, i ^ k) for i in range(X)])  3.34 us
    unnamed x9, local copies, waits for them, and re-layouts  3.11 us
    pallas_call x1, Pallas kernels, stage(): pl.pallas_call(stage_kernel, out_shape=(early, early, pltpu.VMEM((MEM, 1,...  2.54 us
    pallas_call x1, Pallas kernels, allocate(): pl.pallas_call(allocate_kernel, out_shape=(pltpu.VMEM((CAP, BLOCK, BLOCK)...  2.47 us
  transfers between devices with their start and end apart: 6, of which 3 were waited for; matrix products, arithmetic and copies ran while one was open for 2% of the time, Pallas kernels for 8%

profile of v3, /device:TPU:1, one launch (start us, length us, event | category | flops | bytes accessed | tf_op | source)
XLA Modules:
  0.0 47.4 jit_solution(16209891694642530879)
XLA Ops:
  0.6 1.4 %spread.1 = f32[32,16,128]{2,1,0:T(8,128)} custom-call(f32[16,128]{1,0:T(8,128)} %duals_ref.1), custom_call_target="tpu_custom_call" | custom-call | tf_op jit(solution)/shard_map/spread/pallas_call | solution.py:45
  2.1 12.0 %all-to-all-start = ((f32[32,16,128]{2,1,0:T(8,128)}), f32[32,16,128]{2,1,0:T(8,128)S(1)}, u32[]{:S(2)}, u32[]{:S(2)}) async-start(f32[32,16,128]{2,1,0:T(8,128)} %spread.1), calls=%async_computation | async-start | bytes 524288 | tf_op jit(solution)/shard_map/all_to_all | solution.py:243
  14.1 0.0 copy-start.1
  14.1 0.6 %copy-done.1 = s32[1,48,1]{1,2,0:T(1,128)S(1)} copy-done((s32[1,48,1]{1,2,0:T(1,128)S(1)}, s32[1,48,1]{1,2,0:T(1,128)}, u32[]{:S(2)}) %copy-start.1) | copy-done | bytes 216
  14.8 0.0 copy-start.2
  14.8 0.7 %copy-done.2 = s32[1,48]{1,0:T(1,128)S(1)} copy-done((s32[1,48]{1,0:T(1,128)S(1)}, s32[1,48]{1,0:T(1,128)}, u32[]{:S(2)}) %copy-start.2) | copy-done | bytes 216
  15.4 0.7 %copy-done.3 = s32[1,48]{1,0:T(1,128)S(1)} copy-done((s32[1,48]{1,0:T(1,128)S(1)}, s32[1,48]{1,0:T(1,128)}, u32[]{:S(2)}) %copy-start.3) | copy-done | bytes 216
  16.1 2.5 %stage.1 = (bf16[24,128,128]{2,1,0:T(8,128)(2,1)S(1)}, bf16[24,128,128]{2,1,0:T(8,128)(2,1)S(1)}, f32[64,1,128]{2,1,0:T(1,128)S(1)}, s32[192]{0:T(256)S(1)}) custom-call(s32[1,48]{1,0:T(1,128)S(1)} %bitcast.5, s32[1,48]{1,0:T(1,128)S(1)} %copy-done.2, s32[1,48]{1,0:T(1,128)S(1)} %copy-done.3, bf16[48,128,128]{2,1,0:T(8,128)(2,1)} %cost_in_ref.2, ...), custom_call_target="tpu_custom_call" | custom-call | bytes 3145728 | tf_op jit(solution)/shard_map/stage/pallas_call | solution.py:173
  18.6 6.7 %all-to-all-done = f32[32,16,128]{2,1,0:T(8,128)S(1)} async-done(((f32[32,16,128]{2,1,0:T(8,128)}), f32[32,16,128]{2,1,0:T(8,128)S(1)}, u32[]{:S(2)}, u32[]{:S(2)}) %all-to-all-start) | async-done | bytes 262176 | tf_op jit(solution)/shard_map/all_to_all | solution.py:243
  25.3 2.5 %collective-permute-start = (f32[512,128]{1,0:T(8,128)S(1)}, f32[512,128]{1,0:T(8,128)S(1)}, u32[]{:S(2)}, u32[]{:S(2)}) collective-permute-start(f32[512,128]{1,0:T(8,128)S(1)} %bitcast.3), channel_id=1, source_target_pairs={{0,4},{4,0},{1,5},{5,1},{2,6},{6,2},{3,7},{7,3},{8,12},{12,8},{9,1... | collective-permute-start | bytes 786440 | tf_op jit(solution)/shard_map/ppermute | solution.py:248
  27.8 1.4 %stage_late.1 = (bf16[24,128,128]{2,1,0:T(8,128)(2,1)S(1)}, bf16[24,128,128]{2,1,0:T(8,128)(2,1)S(1)}) custom-call(bf16[48,128,128]{2,1,0:T(8,128)(2,1)} %cost_in_ref.2, bf16[48,128,128]{2,1,0:T(8,128)(2,1)} %coef_in_ref.2), custom_call_target="tpu_custom_call" | custom-call | bytes 3145728 | tf_op jit(solution)/shard_map/stage_late/pallas_call | solution.py:192
  29.2 0.0 collective-permute-done.other_rows_ref
  29.2 2.5 %allocate.1 = (bf16[48,128,128]{2,1,0:T(8,128)(2,1)S(1)}, f32[192,1,128]{2,1,0:T(1,128)}, f32[32,128]{1,0:T(8,128)S(1)}) custom-call(s32[192]{0:T(256)S(1)} %get-tuple-element.19.number_ref, f32[64,1,128]{2,1,0:T(1,128)S(1)} %get-tuple-element.20.named_ref, f32[512,128]{1,0:T(8,128)S(1)} %bitcast.4, f32[512,128]{1,0:T(8,128)S(1)} %collective-permute-done.other_rows_ref, ...), custom_call_target="tpu_custom_call" | custom-call | flops 6291456 | bytes 4718592 | tf_op jit(solution)/shard_map/allocate/pallas_call | solution.py:205
  31.6 4.4 %all-to-all-start.1 = ((f32[64,1,384]{2,1,0:T(1,128)}), f32[64,1,384]{2,1,0:T(1,128)S(1)}, u32[]{:S(2)}, u32[]{:S(2)}) async-start(f32[64,1,384]{2,1,0:T(1,128)} %bitcast.2), calls=%async_computation.1 | async-start | bytes 196608 | tf_op jit(solution)/shard_map/all_to_all | solution.py:253
  36.1 2.6 %collective-permute-start.3 = (f32[32,128]{1,0:T(8,128)S(1)}, f32[32,128]{1,0:T(8,128)S(1)}, u32[]{:S(2)}, u32[]{:S(2)}) collective-permute-start(f32[32,128]{1,0:T(8,128)S(1)} %get-tuple-element.30.m0_ref), channel_id=1, source_target_pairs={{0,3},{1,2},{2,1},{3,0},{4,7},{5,6},{6,5},{7,4},{8,11},{9,10},{10,... | collective-permute-start | bytes 49160 | tf_op jit(solution)/shard_map/ppermute | solution.py:251
  38.6 0.5 %collective-permute-start.2 = (f32[32,128]{1,0:T(8,128)S(1)}, f32[32,128]{1,0:T(8,128)S(1)}, u32[]{:S(2)}, u32[]{:S(2)}) collective-permute-start(f32[32,128]{1,0:T(8,128)S(1)} %get-tuple-element.30.m0_ref), channel_id=1, source_target_pairs={{0,2},{1,3},{2,0},{3,1},{4,6},{5,7},{6,4},{7,5},{8,10},{9,11},{10,... | collective-permute-start | bytes 49160 | tf_op jit(solution)/shard_map/ppermute | solution.py:251
  39.1 0.3 collective-permute-start.1
  39.4 1.1 %copy.10 = bf16[48,128,128]{2,1,0:T(8,128)(2,1)} copy(bf16[48,128,128]{2,1,0:T(8,128)(2,1)S(1)} %get-tuple-element.33) | data formatting | bytes 3145728
  40.5 0.0 collective-permute-done.3.m3_ref
  40.5 2.5 %collective-permute-done.2.m2_ref = f32[32,128]{1,0:T(8,128)S(1)} collective-permute-done((f32[32,128]{1,0:T(8,128)S(1)}, f32[32,128]{1,0:T(8,128)S(1)}, u32[]{:S(2)}, u32[]{:S(2)}) %collective-permute-start.2) | collective-permute-done | bytes 16416 | tf_op jit(solution)/shard_map/ppermute | solution.py:251
  43.0 0.0 collective-permute-done.1.m1_ref
  43.0 3.6 %all-to-all-done.1.recv_ref = f32[64,1,384]{2,1,0:T(1,128)S(1)} async-done(((f32[64,1,384]{2,1,0:T(1,128)}), f32[64,1,384]{2,1,0:T(1,128)S(1)}, u32[]{:S(2)}, u32[]{:S(2)}) %all-to-all-start.1) | async-done | bytes 98336 | tf_op jit(solution)/shard_map/all_to_all | solution.py:253
  46.6 0.0 copy-done
  46.6 0.8 %finish.1 = (f32[16,128]{1,0:T(8,128)}, f32[32,128]{1,0:T(8,128)}) custom-call(f32[64,1,384]{2,1,0:T(1,128)S(1)} %all-to-all-done.1.recv_ref, f32[32,128]{1,0:T(8,128)S(1)} %get-tuple-element.30.m0_ref, f32[32,128]{1,0:T(8,128)S(1)} %collective-permute-done.1.m1_ref, f32[32,128]{1,0:T(8,128)S(1)} %collective-permute-done.2.m2_ref, ...), custom_call_target="tpu_custom_call" | custom-call | tf_op jit(solution)/shard_map/finish/pallas_call | solution.py:228
  (2 shorter events, 0.0 us)
Async XLA Ops:
  2.1 23.2 %all-to-all-start = ((f32[32,16,128]{2,1,0:T(8,128)}), f32[32,16,128]{2,1,0:T(8,128)S(1)}, u32[]{:S(2)}, u32[]{:S(2)}) async-start(f32[32,16,128]{2,1,0:T(8,128)} %spread.1), calls=%async_computation | async-start | bytes 524288 | tf_op jit(solution)/shard_map/all_to_all | solution.py:243
  14.1 0.7 %copy-start.1 = (s32[1,48,1]{1,2,0:T(1,128)S(1)}, s32[1,48,1]{1,2,0:T(1,128)}, u32[]{:S(2)}) copy-start(s32[1,48,1]{1,2,0:T(1,128)} %param.10) | copy-start | bytes 580
  14.8 0.7 %copy-start.2 = (s32[1,48]{1,0:T(1,128)S(1)}, s32[1,48]{1,0:T(1,128)}, u32[]{:S(2)}) copy-start(s32[1,48]{1,0:T(1,128)} %local_in_ref.1) | copy-start | bytes 580
  15.4 0.7 %copy-start.3 = (s32[1,48]{1,0:T(1,128)S(1)}, s32[1,48]{1,0:T(1,128)}, u32[]{:S(2)}) copy-start(s32[1,48]{1,0:T(1,128)} %member_in_ref.1) | copy-start | bytes 580
  25.3 3.8 %collective-permute-start = (f32[512,128]{1,0:T(8,128)S(1)}, f32[512,128]{1,0:T(8,128)S(1)}, u32[]{:S(2)}, u32[]{:S(2)}) collective-permute-start(f32[512,128]{1,0:T(8,128)S(1)} %bitcast.3), channel_id=1, source_target_pairs={{0,4},{4,0},{1,5},{5,1},{2,6},{6,2},{3,7},{7,3},{8,12},{12,8},{9,1... | collective-permute-start | bytes 786440 | tf_op jit(solution)/shard_map/ppermute | solution.py:248
  31.6 15.0 %all-to-all-start.1 = ((f32[64,1,384]{2,1,0:T(1,128)}), f32[64,1,384]{2,1,0:T(1,128)S(1)}, u32[]{:S(2)}, u32[]{:S(2)}) async-start(f32[64,1,384]{2,1,0:T(1,128)} %bitcast.2), calls=%async_computation.1 | async-start | bytes 196608 | tf_op jit(solution)/shard_map/all_to_all | solution.py:253
  36.1 4.5 %collective-permute-start.3 = (f32[32,128]{1,0:T(8,128)S(1)}, f32[32,128]{1,0:T(8,128)S(1)}, u32[]{:S(2)}, u32[]{:S(2)}) collective-permute-start(f32[32,128]{1,0:T(8,128)S(1)} %get-tuple-element.30.m0_ref), channel_id=1, source_target_pairs={{0,3},{1,2},{2,1},{3,0},{4,7},{5,6},{6,5},{7,4},{8,11},{9,10},{10,... | collective-permute-start | bytes 49160 | tf_op jit(solution)/shard_map/ppermute | solution.py:251
  38.6 4.4 %collective-permute-start.2 = (f32[32,128]{1,0:T(8,128)S(1)}, f32[32,128]{1,0:T(8,128)S(1)}, u32[]{:S(2)}, u32[]{:S(2)}) collective-permute-start(f32[32,128]{1,0:T(8,128)S(1)} %get-tuple-element.30.m0_ref), channel_id=1, source_target_pairs={{0,2},{1,3},{2,0},{3,1},{4,6},{5,7},{6,4},{7,5},{8,10},{9,11},{10,... | collective-permute-start | bytes 49160 | tf_op jit(solution)/shard_map/ppermute | solution.py:251
  39.1 3.9 %collective-permute-start.1 = (f32[32,128]{1,0:T(8,128)S(1)}, f32[32,128]{1,0:T(8,128)S(1)}, u32[]{:S(2)}, u32[]{:S(2)}) collective-permute-start(f32[32,128]{1,0:T(8,128)S(1)} %get-tuple-element.30.m0_ref), channel_id=1, source_target_pairs={{0,1},{1,0},{2,3},{3,2},{4,5},{5,4},{6,7},{7,6},{8,9},{9,8},{10,11... | collective-permute-start | bytes 49160 | tf_op jit(solution)/shard_map/ppermute | solution.py:251
  39.4 7.2 %copy-start = (s32[16,128]{1,0:T(8,128)S(1)}, s32[16,128]{1,0:T(8,128)}, u32[]{:S(2)}) copy-start(s32[16,128]{1,0:T(8,128)} %capacity_ref.1) | copy-start | bytes 24580

commit v4 on v3

--- a/solution.py
+++ b/solution.py
@@ -15,6 +15,8 @@
 MIB = 1024 * 1024
 EARLY = 24
 LATE = CAP - EARLY
+CHUNKS = 3
+PER = CAP // CHUNKS
 HALF = Z * Y * JB_DEV
 MEMBER, ROW, OTHER, PLACE = (i * CAP for i in range(4))
 VMEM = pl.BlockSpec(memory_space=pltpu.VMEM)
@@ -102,54 +104,93 @@
     load_coef.wait()
 
 
-def allocate_kernel(
+def columns_kernel(
     number_ref, named_ref, own_rows_ref, other_rows_ref,
     early_cost_ref, early_coef_ref, late_cost_ref, late_coef_ref,
-    primal_ref, send_ref, member_out_ref, slot_ref, column_ref, sums_ref,
+    send_ref, minus_ref, column_ref, total_ref,
 ):
     send_ref[...] = jnp.zeros((MEM * ROWS, 1, BLOCK), jnp.float32)
     for i in range(MEM):
         send_ref[i * ROWS + 2] = named_ref[i]
-    member_out_ref[...] = jnp.zeros((MB_DEV, BLOCK), jnp.float32)
     for s in range(CAP):
         at = pl.ds(number_ref[ROW + s], 1)
-        slot_ref[s:s + 1, :] = -jnp.where(number_ref[OTHER + s] == 1, other_rows_ref[at, :], own_rows_ref[at, :])
+        minus_ref[s:s + 1, :] = -jnp.where(number_ref[OTHER + s] == 1, other_rows_ref[at, :], own_rows_ref[at, :])
+
+    def run(first, count, cost_ref, coef_ref):
+        def block(i, carry):
+            s = first + i
+            minus_dual = minus_ref[pl.ds(s, 1), :]
+            column = None
+            for g in range(0, BLOCK, 32):
+                cost = cost_ref[i, g:g + 32].astype(jnp.float32)
+                coef = coef_ref[i, g:g + 32].astype(jnp.float32)
+                alloc = jnp.minimum(jnp.maximum(coef * minus_dual - cost, 0.0), 1.0)
+                part = jnp.sum((coef * alloc).reshape(4, 8, BLOCK), axis=0)
+                column = part if column is None else column + part
+            column_ref[pl.ds(pl.multiple_of(s * 8, 8), 8), :] = column
+            return carry
+
+        lax.fori_loop(0, count, block, 0, unroll=count)
+
+    run(0, EARLY, early_cost_ref, early_coef_ref)
+    run(EARLY, LATE, late_cost_ref, late_coef_ref)
+    total_ref[...] = jnp.sum(column_ref[...].reshape(CAP, 8, BLOCK), axis=1)
+    for s in range(CAP):
+        send_ref[number_ref[PLACE + s]] = total_ref[s:s + 1, :]
+
+
+def primal_kernel(
+    number_ref, minus_ref, cost_in_ref, coef_in_ref,
+    primal_out_ref, member_out_ref, cost_ref, coef_ref, primal_ref, sums_ref, in_sem, out_sem,
+):
+    def loads(k):
+        part = pl.ds(k * PER, PER)
+        return (
+            pltpu.make_async_copy(cost_in_ref.at[part], cost_ref.at[part], in_sem.at[0, k]),
+            pltpu.make_async_copy(coef_in_ref.at[part], coef_ref.at[part], in_sem.at[1, k]),
+        )
+
+    def leave(k):
+        part = pl.ds(k * PER, PER)
+        return pltpu.make_async_copy(primal_ref.at[part], primal_out_ref.at[part], out_sem.at[k])
+
+    for k in range(CHUNKS):
+        for load in loads(k):
+            load.start()
+    member_out_ref[...] = jnp.zeros((MB_DEV, BLOCK), jnp.float32)
     ones = jnp.ones((8, 2 * BLOCK), jnp.bfloat16)
 
-    def block(s, cost_ref, coef_ref, at):
-        minus_dual = slot_ref[pl.ds(s, 1), :]
-        column, parts = None, []
+    def block(s):
+        minus_dual = minus_ref[pl.ds(s, 1), :]
+        parts = []
         for g in range(0, BLOCK, 32):
-            cost = cost_ref[at, g:g + 32].astype(jnp.float32)
-            coef = coef_ref[at, g:g + 32].astype(jnp.float32)
+            cost = cost_ref[s, g:g + 32].astype(jnp.float32)
+            coef = coef_ref[s, g:g + 32].astype(jnp.float32)
             alloc = jnp.minimum(jnp.maximum(coef * minus_dual - cost, 0.0), 1.0)
             high = alloc.astype(jnp.bfloat16)
             primal_ref[s, g:g + 32] = high
             rest = (alloc - high.astype(jnp.float32)).astype(jnp.bfloat16)
             parts.append(jnp.concatenate([high, rest], axis=1))
-            part = jnp.sum((coef * alloc).reshape(4, 8, BLOCK), axis=0)
-            column = part if column is None else column + part
-        column_ref[pl.ds(pl.multiple_of(s * 8, 8), 8), :] = column
         return parts
 
-    def run(first, count, cost_ref, coef_ref, unroll):
+    for k in range(CHUNKS):
+        for load in loads(k):
+            load.wait()
+
         def pair(i, carry):
-            s = first + 2 * i
-            parts = block(s, cost_ref, coef_ref, 2 * i) + block(s + 1, cost_ref, coef_ref, 2 * i + 1)
-            both = jnp.concatenate(parts, axis=0)
+            s = k * PER + 2 * i
+            both = jnp.concatenate(block(s) + block(s + 1), axis=0)
             sums = lax.dot_general(ones, both, (((1,), (1,)), ((), ())), preferred_element_type=jnp.float32)
             sums_ref[pl.ds(s, 1), :] = sums[0:1, :BLOCK]
             sums_ref[pl.ds(s + 1, 1), :] = sums[0:1, BLOCK:]
             return carry
 
-        lax.fori_loop(0, count // 2, pair, 0, unroll=unroll)
-
-    run(0, EARLY, early_cost_ref, early_coef_ref, 12)
-    run(EARLY, LATE, late_cost_ref, late_coef_ref, 12)
-    slot_ref[...] = jnp.sum(column_ref[...].reshape(CAP, 8, BLOCK), axis=1)
+        lax.fori_loop(0, PER // 2, pair, 0, unroll=PER // 2)
+        leave(k).start()
     for s in range(CAP):
-        send_ref[number_ref[PLACE + s]] = slot_ref[s:s + 1, :]
         member_out_ref[pl.ds(number_ref[MEMBER + s], 1), :] += sums_ref[s:s + 1, :]
+    for k in range(CHUNKS):
+        leave(k).wait()
 
 
 def finish_kernel(recv_ref, m0_ref, m1_ref, m2_ref, m3_ref, capacity_ref, gradient_ref, share_ref):
@@ -201,27 +242,45 @@
     )(in_hbm(cost), in_hbm(coef))
 
 
-def allocate(number, *blocks):
-    return pl.pallas_call(
-        allocate_kernel,
+def columns(number, *blocks):
+    return pl.pallas_call(
+        columns_kernel,
         out_shape=(
-            pltpu.VMEM((CAP, BLOCK, BLOCK), jnp.bfloat16),
             jax.ShapeDtypeStruct((MEM * ROWS, 1, BLOCK), jnp.float32),
-            pltpu.VMEM((MB_DEV, BLOCK), jnp.float32),
+            pltpu.VMEM((CAP, BLOCK), jnp.float32),
         ),
         in_specs=[SMEM] + [VMEM] * 7,
-        out_specs=(VMEM, VMEM, VMEM),
+        out_specs=(VMEM, VMEM),
+        scratch_shapes=[pltpu.VMEM((CAP * 8, BLOCK), jnp.float32), pltpu.VMEM((CAP, BLOCK), jnp.float32)],
+        compiler_params=pltpu.CompilerParams(vmem_limit_bytes=8 * MIB),
+        cost_estimate=pl.CostEstimate(
+            flops=6 * CAP * BLOCK * BLOCK, bytes_accessed=4 * CAP * BLOCK * BLOCK, transcendentals=0
+        ),
+        name="columns",
+    )(number, *map(in_vmem, blocks))
+
+
+def primal_and_members(number, minus, cost, coef):
+    blocks = (CAP, BLOCK, BLOCK)
+    return pl.pallas_call(
+        primal_kernel,
+        out_shape=(jax.ShapeDtypeStruct(blocks, jnp.bfloat16), pltpu.VMEM((MB_DEV, BLOCK), jnp.float32)),
+        in_specs=[SMEM, VMEM, ANY, ANY],
+        out_specs=(ANY, VMEM),
         scratch_shapes=[
+            pltpu.VMEM(blocks, jnp.bfloat16),
+            pltpu.VMEM(blocks, jnp.bfloat16),
+            pltpu.VMEM(blocks, jnp.bfloat16),
             pltpu.VMEM((CAP, BLOCK), jnp.float32),
-            pltpu.VMEM((CAP * 8, BLOCK), jnp.float32),
-            pltpu.VMEM((CAP, BLOCK), jnp.float32),
+            pltpu.SemaphoreType.DMA((2, CHUNKS)),
+            pltpu.SemaphoreType.DMA((CHUNKS,)),
         ],
-        compiler_params=pltpu.CompilerParams(vmem_limit_bytes=8 * 1024 * 1024),
+        compiler_params=pltpu.CompilerParams(vmem_limit_bytes=8 * MIB),
         cost_estimate=pl.CostEstimate(
-            flops=8 * CAP * BLOCK * BLOCK, bytes_accessed=6 * CAP * BLOCK * BLOCK, transcendentals=0
-        ),
-        name="allocate",
-    )(number, *map(in_vmem, blocks))
+            flops=6 * CAP * BLOCK * BLOCK, bytes_accessed=6 * CAP * BLOCK * BLOCK, transcendentals=0
+        ),
+        name="primal",
+    )(number, minus, in_hbm(cost), in_hbm(coef))
 
 
 def finish(recv, share, others, capacity):
@@ -247,10 +306,11 @@
     rows, number, late_cost, late_coef = lax.optimization_barrier((rows, number, pair_cost, pair_coef))
     other_rows = lax.ppermute(rows, "c", [(0, 1), (1, 0)])
     late_cost, late_coef = stage_late(late_cost, late_coef)
-    primal, send, share = allocate(number, named, rows, other_rows, cost, coef, late_cost, late_coef)
-    others = [lax.ppermute(share, "x", [(i, i ^ k) for i in range(X)]) for k in (1, 2, 3)]
+    send, minus = columns(number, named, rows, other_rows, cost, coef, late_cost, late_coef)
     send = send.reshape(MEM, 1, ROWS * BLOCK)
     recv = lax.all_to_all(send, ("z", "y", "c"), split_axis=0, concat_axis=0, tiled=True)
+    primal, share = primal_and_members(number, minus, pair_cost, pair_coef)
+    others = [lax.ppermute(share, "x", [(i, i ^ k) for i in range(X)]) for k in (1, 2, 3)]
     gradient, share = finish(recv, share, others, capacity)
     return primal, gradient, share
 

time: 47.8 us -> 47.6 us (level)
  Pallas kernels: 8.63 us -> 11.9 us
  waiting for transfers between devices: 12.7 us -> 10.2 us
  local copies, waits for them, and re-layouts: 3.11 us -> 1.97 us
    all_to_all x1, waiting for transfers between devices: 3.6 us -> 0.01 us  [per_device(): lax.all_to_all(send, ('z', 'y', 'c'), split_axis=0, concat_axis=0, tiled=...]
    pallas_call x1 -> x2, Pallas kernels: 2.47 us -> 5.78 us  [the longest x1 3.72 us: primal_and_members(): pl.pallas_call(primal_kernel, out_shape=(jax.ShapeDtypeStruct(blocks, jnp...]
    unnamed x9 -> x8, local copies, waits for them, and re-layouts: 3.11 us -> 1.97 us
    ppermute x3, waiting for transfers between devices: 2.47 us -> 3.48 us  [per_device(): lax.ppermute(share, 'x', [(i, i ^ k) for i in range(X)])]
  transfers between devices with their start and end apart: 6 -> 6, of which waited for: 3 -> 3; matrix products, arithmetic and copies ran while one was open for 2% -> 0% of each run, Pallas kernels for 8% -> 16%
where the time goes in v4:
time: 47.6 us; the launch traced here: 47 us
  starting transfers between devices  22.2 us (47%)
  Pallas kernels  11.9 us (25%)
  waiting for transfers between devices  10.2 us (21%)
  local copies, waits for them, and re-layouts  1.97 us (4%)
  between operations  0.71 us (1%)
    all_to_all x1, starting transfers between devices, per_device(): lax.all_to_all(copies, ('z', 'y'), split_axis=0, concat_axis=0, tiled=True)  12 us
    all_to_all x1, waiting for transfers between devices, per_device(): lax.all_to_all(copies, ('z', 'y'), split_axis=0, concat_axis=0, tiled=True)  6.67 us
    all_to_all x1, starting transfers between devices, per_device(): lax.all_to_all(send, ('z', 'y', 'c'), split_axis=0, concat_axis=0, tiled=...  4.41 us
    pallas_call x1, Pallas kernels, primal_and_members(): pl.pallas_call(primal_kernel, out_shape=(jax.ShapeDtypeStruct(blocks, jnp...  3.72 us
    ppermute x3, waiting for transfers between devices, per_device(): lax.ppermute(share, 'x', [(i, i ^ k) for i in range(X)])  3.48 us
    ppermute x3, starting transfers between devices, per_device(): lax.ppermute(share, 'x', [(i, i ^ k) for i in range(X)])  3.34 us
    pallas_call x1, Pallas kernels, stage(): pl.pallas_call(stage_kernel, out_shape=(early, early, pltpu.VMEM((MEM, 1,...  2.54 us
    ppermute x1, starting transfers between devices, per_device(): other_rows = lax.ppermute(rows, 'c', [(0, 1), (1, 0)])  2.45 us
  transfers between devices with their start and end apart: 6, of which 3 were waited for; matrix products, arithmetic and copies ran while one was open for 0% of the time, Pallas kernels for 16%

profile of v4, /device:TPU:1, one launch (start us, length us, event | category | flops | bytes accessed | tf_op | source)
XLA Modules:
  0.0 47.0 jit_solution(4686999300687166089)
XLA Ops:
  0.6 1.4 %spread.1 = f32[32,16,128]{2,1,0:T(8,128)} custom-call(f32[16,128]{1,0:T(8,128)} %duals_ref.1), custom_call_target="tpu_custom_call" | custom-call | tf_op jit(solution)/shard_map/spread/pallas_call | solution.py:47
  2.1 12.0 %all-to-all-start = ((f32[32,16,128]{2,1,0:T(8,128)}), f32[32,16,128]{2,1,0:T(8,128)S(1)}, u32[]{:S(2)}, u32[]{:S(2)}) async-start(f32[32,16,128]{2,1,0:T(8,128)} %spread.1), calls=%async_computation | async-start | bytes 524288 | tf_op jit(solution)/shard_map/all_to_all | solution.py:302
  14.1 0.0 copy-start.1
  14.1 0.6 %copy-done.1 = s32[1,48,1]{1,2,0:T(1,128)S(1)} copy-done((s32[1,48,1]{1,2,0:T(1,128)S(1)}, s32[1,48,1]{1,2,0:T(1,128)}, u32[]{:S(2)}) %copy-start.1) | copy-done | bytes 216
  14.8 0.7 %copy-done.2 = s32[1,48]{1,0:T(1,128)S(1)} copy-done((s32[1,48]{1,0:T(1,128)S(1)}, s32[1,48]{1,0:T(1,128)}, u32[]{:S(2)}) %copy-start.2) | copy-done | bytes 216
  15.4 0.7 %copy-done.3 = s32[1,48]{1,0:T(1,128)S(1)} copy-done((s32[1,48]{1,0:T(1,128)S(1)}, s32[1,48]{1,0:T(1,128)}, u32[]{:S(2)}) %copy-start.3) | copy-done | bytes 216
  16.1 2.5 %stage.1 = (bf16[24,128,128]{2,1,0:T(8,128)(2,1)S(1)}, bf16[24,128,128]{2,1,0:T(8,128)(2,1)S(1)}, f32[64,1,128]{2,1,0:T(1,128)S(1)}, s32[192]{0:T(256)S(1)}) custom-call(s32[1,48]{1,0:T(1,128)S(1)} %bitcast.5, s32[1,48]{1,0:T(1,128)S(1)} %copy-done.2, s32[1,48]{1,0:T(1,128)S(1)} %copy-done.3, bf16[48,128,128]{2,1,0:T(8,128)(2,1)} %cost_in_ref.4, ...), custom_call_target="tpu_custom_call" | custom-call | bytes 3145728 | tf_op jit(solution)/shard_map/stage/pallas_call | solution.py:214
  18.6 6.7 %all-to-all-done = f32[32,16,128]{2,1,0:T(8,128)S(1)} async-done(((f32[32,16,128]{2,1,0:T(8,128)}), f32[32,16,128]{2,1,0:T(8,128)S(1)}, u32[]{:S(2)}, u32[]{:S(2)}) %all-to-all-start) | async-done | bytes 262176 | tf_op jit(solution)/shard_map/all_to_all | solution.py:302
  25.3 2.5 %collective-permute-start = (f32[512,128]{1,0:T(8,128)S(1)}, f32[512,128]{1,0:T(8,128)S(1)}, u32[]{:S(2)}, u32[]{:S(2)}) collective-permute-start(f32[512,128]{1,0:T(8,128)S(1)} %bitcast.3), channel_id=1, source_target_pairs={{0,4},{4,0},{1,5},{5,1},{2,6},{6,2},{3,7},{7,3},{8,12},{12,8},{9,1... | collective-permute-start | bytes 786440 | tf_op jit(solution)/shard_map/ppermute | solution.py:307
  27.8 1.4 %stage_late.1 = (bf16[24,128,128]{2,1,0:T(8,128)(2,1)S(1)}, bf16[24,128,128]{2,1,0:T(8,128)(2,1)S(1)}) custom-call(bf16[48,128,128]{2,1,0:T(8,128)(2,1)} %cost_in_ref.4, bf16[48,128,128]{2,1,0:T(8,128)(2,1)} %coef_in_ref.4), custom_call_target="tpu_custom_call" | custom-call | bytes 3145728 | tf_op jit(solution)/shard_map/stage_late/pallas_call | solution.py:233
  29.2 0.0 collective-permute-done.other_rows_ref
  29.2 2.1 %columns.1 = (f32[192,1,128]{2,1,0:T(1,128)}, f32[48,128]{1,0:T(8,128)S(1)}) custom-call(s32[192]{0:T(256)S(1)} %get-tuple-element.20.number_ref, f32[64,1,128]{2,1,0:T(1,128)S(1)} %get-tuple-element.21.named_ref, f32[512,128]{1,0:T(8,128)S(1)} %bitcast.4, f32[512,128]{1,0:T(8,128)S(1)} %collective-permute-done.other_rows_ref, ...), custom_call_target="tpu_custom_call" | custom-call | flops 4718592 | bytes 3145728 | tf_op jit(solution)/shard_map/columns/pallas_call | solution.py:246
  31.2 4.4 %all-to-all-start.1 = ((f32[64,1,384]{2,1,0:T(1,128)}), f32[64,1,384]{2,1,0:T(1,128)S(1)}, u32[]{:S(2)}, u32[]{:S(2)}) async-start(f32[64,1,384]{2,1,0:T(1,128)} %bitcast.2), calls=%async_computation.1 | async-start | bytes 196608 | tf_op jit(solution)/shard_map/all_to_all | solution.py:311
  35.6 0.0 copy-start
  35.7 3.7 %primal.1 = (bf16[48,128,128]{2,1,0:T(8,128)(2,1)}, f32[32,128]{1,0:T(8,128)S(1)}) custom-call(s32[192]{0:T(256)S(1)} %get-tuple-element.20.number_ref, f32[48,128]{1,0:T(8,128)S(1)} %get-tuple-element.29.minus_ref, bf16[48,128,128]{2,1,0:T(8,128)(2,1)} %cost_in_ref.4, bf16[48,128,128]{2,1,0:T(8,128)(2,1)} %coef_in_ref.4), custom_call_target="tpu_custom_call" | custom-call | flops 4718592 | bytes 4718592 | tf_op jit(solution)/shard_map/primal/pallas_call | solution.py:265
  39.4 2.6 %collective-permute-start.3 = (f32[32,128]{1,0:T(8,128)S(1)}, f32[32,128]{1,0:T(8,128)S(1)}, u32[]{:S(2)}, u32[]{:S(2)}) collective-permute-start(f32[32,128]{1,0:T(8,128)S(1)} %get-tuple-element.32.m0_ref), channel_id=1, source_target_pairs={{0,3},{1,2},{2,1},{3,0},{4,7},{5,6},{6,5},{7,4},{8,11},{9,10},{10,... | collective-permute-start | bytes 49160 | tf_op jit(solution)/shard_map/ppermute | solution.py:313
  42.0 0.5 %collective-permute-start.2 = (f32[32,128]{1,0:T(8,128)S(1)}, f32[32,128]{1,0:T(8,128)S(1)}, u32[]{:S(2)}, u32[]{:S(2)}) collective-permute-start(f32[32,128]{1,0:T(8,128)S(1)} %get-tuple-element.32.m0_ref), channel_id=1, source_target_pairs={{0,2},{1,3},{2,0},{3,1},{4,6},{5,7},{6,4},{7,5},{8,10},{9,11},{10,... | collective-permute-start | bytes 49160 | tf_op jit(solution)/shard_map/ppermute | solution.py:313
  42.5 0.3 collective-permute-start.1
  42.7 0.8 %collective-permute-done.3.m3_ref = f32[32,128]{1,0:T(8,128)S(1)} collective-permute-done((f32[32,128]{1,0:T(8,128)S(1)}, f32[32,128]{1,0:T(8,128)S(1)}, u32[]{:S(2)}, u32[]{:S(2)}) %collective-permute-start.3) | collective-permute-done | bytes 16416 | tf_op jit(solution)/shard_map/ppermute | solution.py:313
  43.6 2.6 %collective-permute-done.2.m2_ref = f32[32,128]{1,0:T(8,128)S(1)} collective-permute-done((f32[32,128]{1,0:T(8,128)S(1)}, f32[32,128]{1,0:T(8,128)S(1)}, u32[]{:S(2)}, u32[]{:S(2)}) %collective-permute-start.2) | collective-permute-done | bytes 16416 | tf_op jit(solution)/shard_map/ppermute | solution.py:313
  46.2 0.0 collective-permute-done.1.m1_ref
  46.2 0.0 all-to-all-done.1.recv_ref
  46.2 0.0 copy-done
  46.2 0.8 %finish.1 = (f32[16,128]{1,0:T(8,128)}, f32[32,128]{1,0:T(8,128)}) custom-call(f32[64,1,384]{2,1,0:T(1,128)S(1)} %all-to-all-done.1.recv_ref, f32[32,128]{1,0:T(8,128)S(1)} %get-tuple-element.32.m0_ref, f32[32,128]{1,0:T(8,128)S(1)} %collective-permute-done.1.m1_ref, f32[32,128]{1,0:T(8,128)S(1)} %collective-permute-done.2.m2_ref, ...), custom_call_target="tpu_custom_call" | custom-call | tf_op jit(solution)/shard_map/finish/pallas_call | solution.py:287
  (2 shorter events, 0.0 us)
Async XLA Ops:
  2.1 23.2 %all-to-all-start = ((f32[32,16,128]{2,1,0:T(8,128)}), f32[32,16,128]{2,1,0:T(8,128)S(1)}, u32[]{:S(2)}, u32[]{:S(2)}) async-start(f32[32,16,128]{2,1,0:T(8,128)} %spread.1), calls=%async_computation | async-start | bytes 524288 | tf_op jit(solution)/shard_map/all_to_all | solution.py:302
  14.1 0.7 %copy-start.1 = (s32[1,48,1]{1,2,0:T(1,128)S(1)}, s32[1,48,1]{1,2,0:T(1,128)}, u32[]{:S(2)}) copy-start(s32[1,48,1]{1,2,0:T(1,128)} %param.10) | copy-start | bytes 580
  14.8 0.7 %copy-start.2 = (s32[1,48]{1,0:T(1,128)S(1)}, s32[1,48]{1,0:T(1,128)}, u32[]{:S(2)}) copy-start(s32[1,48]{1,0:T(1,128)} %local_in_ref.1) | copy-start | bytes 580
  15.4 0.7 %copy-start.3 = (s32[1,48]{1,0:T(1,128)S(1)}, s32[1,48]{1,0:T(1,128)}, u32[]{:S(2)}) copy-start(s32[1,48]{1,0:T(1,128)} %member_in_ref.1) | copy-start | bytes 580
  25.3 3.8 %collective-permute-start = (f32[512,128]{1,0:T(8,128)S(1)}, f32[512,128]{1,0:T(8,128)S(1)}, u32[]{:S(2)}, u32[]{:S(2)}) collective-permute-start(f32[512,128]{1,0:T(8,128)S(1)} %bitcast.3), channel_id=1, source_target_pairs={{0,4},{4,0},{1,5},{5,1},{2,6},{6,2},{3,7},{7,3},{8,12},{12,8},{9,1... | collective-permute-start | bytes 786440 | tf_op jit(solution)/shard_map/ppermute | solution.py:307
  31.2 15.0 %all-to-all-start.1 = ((f32[64,1,384]{2,1,0:T(1,128)}), f32[64,1,384]{2,1,0:T(1,128)S(1)}, u32[]{:S(2)}, u32[]{:S(2)}) async-start(f32[64,1,384]{2,1,0:T(1,128)} %bitcast.2), calls=%async_computation.1 | async-start | bytes 196608 | tf_op jit(solution)/shard_map/all_to_all | solution.py:311
  35.6 10.6 %copy-start = (s32[16,128]{1,0:T(8,128)S(1)}, s32[16,128]{1,0:T(8,128)}, u32[]{:S(2)}) copy-start(s32[16,128]{1,0:T(8,128)} %capacity_ref.1) | copy-start | bytes 24580
  39.4 4.2 %collective-permute-start.3 = (f32[32,128]{1,0:T(8,128)S(1)}, f32[32,128]{1,0:T(8,128)S(1)}, u32[]{:S(2)}, u32[]{:S(2)}) collective-permute-start(f32[32,128]{1,0:T(8,128)S(1)} %get-tuple-element.32.m0_ref), channel_id=1, source_target_pairs={{0,3},{1,2},{2,1},{3,0},{4,7},{5,6},{6,5},{7,4},{8,11},{9,10},{10,... | collective-permute-start | bytes 49160 | tf_op jit(solution)/shard_map/ppermute | solution.py:313
  42.0 4.3 %collective-permute-start.2 = (f32[32,128]{1,0:T(8,128)S(1)}, f32[32,128]{1,0:T(8,128)S(1)}, u32[]{:S(2)}, u32[]{:S(2)}) collective-permute-start(f32[32,128]{1,0:T(8,128)S(1)} %get-tuple-element.32.m0_ref), channel_id=1, source_target_pairs={{0,2},{1,3},{2,0},{3,1},{4,6},{5,7},{6,4},{7,5},{8,10},{9,11},{10,... | collective-permute-start | bytes 49160 | tf_op jit(solution)/shard_map/ppermute | solution.py:313
  42.5 3.7 %collective-permute-start.1 = (f32[32,128]{1,0:T(8,128)S(1)}, f32[32,128]{1,0:T(8,128)S(1)}, u32[]{:S(2)}, u32[]{:S(2)}) collective-permute-start(f32[32,128]{1,0:T(8,128)S(1)} %get-tuple-element.32.m0_ref), channel_id=1, source_target_pairs={{0,1},{1,0},{2,3},{3,2},{4,5},{5,4},{6,7},{7,6},{8,9},{9,8},{10,11... | collective-permute-start | bytes 49160 | tf_op jit(solution)/shard_map/ppermute | solution.py:313

commit v5 on v4

--- a/solution.py
+++ b/solution.py
@@ -15,8 +15,6 @@
 MIB = 1024 * 1024
 EARLY = 24
 LATE = CAP - EARLY
-CHUNKS = 3
-PER = CAP // CHUNKS
 HALF = Z * Y * JB_DEV
 MEMBER, ROW, OTHER, PLACE = (i * CAP for i in range(4))
 VMEM = pl.BlockSpec(memory_space=pltpu.VMEM)
@@ -140,32 +138,22 @@
 
 
 def primal_kernel(
-    number_ref, minus_ref, cost_in_ref, coef_in_ref,
-    primal_out_ref, member_out_ref, cost_ref, coef_ref, primal_ref, sums_ref, in_sem, out_sem,
+    number_ref, minus_ref, early_cost_ref, early_coef_ref, cost_in_ref, coef_in_ref,
+    primal_ref, member_out_ref, late_cost_ref, late_coef_ref, sums_ref, sem,
 ):
-    def loads(k):
-        part = pl.ds(k * PER, PER)
-        return (
-            pltpu.make_async_copy(cost_in_ref.at[part], cost_ref.at[part], in_sem.at[0, k]),
-            pltpu.make_async_copy(coef_in_ref.at[part], coef_ref.at[part], in_sem.at[1, k]),
-        )
-
-    def leave(k):
-        part = pl.ds(k * PER, PER)
-        return pltpu.make_async_copy(primal_ref.at[part], primal_out_ref.at[part], out_sem.at[k])
-
-    for k in range(CHUNKS):
-        for load in loads(k):
-            load.start()
+    load_cost = pltpu.make_async_copy(cost_in_ref.at[pl.ds(EARLY, LATE)], late_cost_ref, sem.at[0])
+    load_coef = pltpu.make_async_copy(coef_in_ref.at[pl.ds(EARLY, LATE)], late_coef_ref, sem.at[1])
+    load_cost.start()
+    load_coef.start()
     member_out_ref[...] = jnp.zeros((MB_DEV, BLOCK), jnp.float32)
     ones = jnp.ones((8, 2 * BLOCK), jnp.bfloat16)
 
-    def block(s):
+    def block(s, cost_ref, coef_ref, at):
         minus_dual = minus_ref[pl.ds(s, 1), :]
         parts = []
         for g in range(0, BLOCK, 32):
-            cost = cost_ref[s, g:g + 32].astype(jnp.float32)
-            coef = coef_ref[s, g:g + 32].astype(jnp.float32)
+            cost = cost_ref[at, g:g + 32].astype(jnp.float32)
+            coef = coef_ref[at, g:g + 32].astype(jnp.float32)
             alloc = jnp.minimum(jnp.maximum(coef * minus_dual - cost, 0.0), 1.0)
             high = alloc.astype(jnp.bfloat16)
             primal_ref[s, g:g + 32] = high
@@ -173,24 +161,24 @@
             parts.append(jnp.concatenate([high, rest], axis=1))
         return parts
 
-    for k in range(CHUNKS):
-        for load in loads(k):
-            load.wait()
-
+    def run(first, count, cost_ref, coef_ref):
         def pair(i, carry):
-            s = k * PER + 2 * i
-            both = jnp.concatenate(block(s) + block(s + 1), axis=0)
+            s = first + 2 * i
+            parts = block(s, cost_ref, coef_ref, 2 * i) + block(s + 1, cost_ref, coef_ref, 2 * i + 1)
+            both = jnp.concatenate(parts, axis=0)
             sums = lax.dot_general(ones, both, (((1,), (1,)), ((), ())), preferred_element_type=jnp.float32)
             sums_ref[pl.ds(s, 1), :] = sums[0:1, :BLOCK]
             sums_ref[pl.ds(s + 1, 1), :] = sums[0:1, BLOCK:]
             return carry
 
-        lax.fori_loop(0, PER // 2, pair, 0, unroll=PER // 2)
-        leave(k).start()
+        lax.fori_loop(0, count // 2, pair, 0, unroll=count // 2)
+
+    run(0, EARLY, early_cost_ref, early_coef_ref)
+    load_cost.wait()
+    load_coef.wait()
+    run(EARLY, LATE, late_cost_ref, late_coef_ref)
     for s in range(CAP):
         member_out_ref[pl.ds(number_ref[MEMBER + s], 1), :] += sums_ref[s:s + 1, :]
-    for k in range(CHUNKS):
-        leave(k).wait()
 
 
 def finish_kernel(recv_ref, m0_ref, m1_ref, m2_ref, m3_ref, capacity_ref, gradient_ref, share_ref):
@@ -260,27 +248,20 @@
     )(number, *map(in_vmem, blocks))
 
 
-def primal_and_members(number, minus, cost, coef):
-    blocks = (CAP, BLOCK, BLOCK)
+def primal_and_members(number, minus, early_cost, early_coef, cost, coef):
+    late = pltpu.VMEM((LATE, BLOCK, BLOCK), jnp.bfloat16)
     return pl.pallas_call(
         primal_kernel,
-        out_shape=(jax.ShapeDtypeStruct(blocks, jnp.bfloat16), pltpu.VMEM((MB_DEV, BLOCK), jnp.float32)),
-        in_specs=[SMEM, VMEM, ANY, ANY],
-        out_specs=(ANY, VMEM),
-        scratch_shapes=[
-            pltpu.VMEM(blocks, jnp.bfloat16),
-            pltpu.VMEM(blocks, jnp.bfloat16),
-            pltpu.VMEM(blocks, jnp.bfloat16),
-            pltpu.VMEM((CAP, BLOCK), jnp.float32),
-            pltpu.SemaphoreType.DMA((2, CHUNKS)),
-            pltpu.SemaphoreType.DMA((CHUNKS,)),
-        ],
+        out_shape=(pltpu.VMEM((CAP, BLOCK, BLOCK), jnp.bfloat16), pltpu.VMEM((MB_DEV, BLOCK), jnp.float32)),
+        in_specs=[SMEM] + [VMEM] * 3 + [ANY] * 2,
+        out_specs=(VMEM, VMEM),
+        scratch_shapes=[late, late, pltpu.VMEM((CAP, BLOCK), jnp.float32), pltpu.SemaphoreType.DMA((2,))],
         compiler_params=pltpu.CompilerParams(vmem_limit_bytes=8 * MIB),
         cost_estimate=pl.CostEstimate(
             flops=6 * CAP * BLOCK * BLOCK, bytes_accessed=6 * CAP * BLOCK * BLOCK, transcendentals=0
         ),
         name="primal",
-    )(number, minus, in_hbm(cost), in_hbm(coef))
+    )(number, in_vmem(minus), in_vmem(early_cost), in_vmem(early_coef), in_hbm(cost), in_hbm(coef))
 
 
 def finish(recv, share, others, capacity):
@@ -309,7 +290,7 @@
     send, minus = columns(number, named, rows, other_rows, cost, coef, late_cost, late_coef)
     send = send.reshape(MEM, 1, ROWS * BLOCK)
     recv = lax.all_to_all(send, ("z", "y", "c"), split_axis=0, concat_axis=0, tiled=True)
-    primal, share = primal_and_members(number, minus, pair_cost, pair_coef)
+    primal, share = primal_and_members(number, minus, cost, coef, pair_cost, pair_coef)
     others = [lax.ppermute(share, "x", [(i, i ^ k) for i in range(X)]) for k in (1, 2, 3)]
     gradient, share = finish(recv, share, others, capacity)
     return primal, gradient, share

time: 47.6 us -> 47.4 us (level)
  Pallas kernels: 11.9 us -> 10.7 us
  local copies, waits for them, and re-layouts: 1.97 us -> 3.11 us
    pallas_call x1, Pallas kernels: 3.72 us -> 2.52 us  [primal_and_members(): pl.pallas_call(primal_kernel, out_shape=(pltpu.VMEM((CAP, BLOCK, BLOCK),...]
    unnamed x8 -> x9, local copies, waits for them, and re-layouts: 1.97 us -> 3.11 us
    all_to_all x1, waiting for transfers between devices: 0.01 us -> 1.08 us  [per_device(): lax.all_to_all(send, ('z', 'y', 'c'), split_axis=0, concat_axis=0, tiled=...]
    ppermute x3, waiting for transfers between devices: 3.48 us -> 2.47 us  [per_device(): lax.ppermute(share, 'x', [(i, i ^ k) for i in range(X)])]
  transfers between devices with their start and end apart: 6 -> 6, of which waited for: 3 -> 3; matrix products, arithmetic and copies ran while one was open for 0% -> 2% of each run, Pallas kernels for 16% -> 14%
where the time goes in v5:
time: 47.4 us; the launch traced here: 47 us
  starting transfers between devices  22.2 us (47%)
  Pallas kernels  10.7 us (23%)
  waiting for transfers between devices  10.2 us (22%)
  local copies, waits for them, and re-layouts  3.11 us (7%)
  between operations  0.7 us (1%)
    all_to_all x1, starting transfers between devices, per_device(): lax.all_to_all(copies, ('z', 'y'), split_axis=0, concat_axis=0, tiled=True)  12 us
    all_to_all x1, waiting for transfers between devices, per_device(): lax.all_to_all(copies, ('z', 'y'), split_axis=0, concat_axis=0, tiled=True)  6.67 us
    all_to_all x1, starting transfers between devices, per_device(): lax.all_to_all(send, ('z', 'y', 'c'), split_axis=0, concat_axis=0, tiled=...  4.41 us
    ppermute x3, starting transfers between devices, per_device(): lax.ppermute(share, 'x', [(i, i ^ k) for i in range(X)])  3.34 us
    unnamed x9, local copies, waits for them, and re-layouts  3.11 us
    pallas_call x1, Pallas kernels, stage(): pl.pallas_call(stage_kernel, out_shape=(early, early, pltpu.VMEM((MEM, 1,...  2.54 us
    pallas_call x1, Pallas kernels, primal_and_members(): pl.pallas_call(primal_kernel, out_shape=(pltpu.VMEM((CAP, BLOCK, BLOCK),...  2.52 us
    ppermute x3, waiting for transfers between devices, per_device(): lax.ppermute(share, 'x', [(i, i ^ k) for i in range(X)])  2.47 us
  transfers between devices with their start and end apart: 6, of which 3 were waited for; matrix products, arithmetic and copies ran while one was open for 2% of the time, Pallas kernels for 14%

profile of v5, /device:TPU:1, one launch (start us, length us, event | category | flops | bytes accessed | tf_op | source)
XLA Modules:
  0.0 47.0 jit_solution(12470898006658631975)
XLA Ops:
  0.6 1.4 %spread.1 = f32[32,16,128]{2,1,0:T(8,128)} custom-call(f32[16,128]{1,0:T(8,128)} %duals_ref.1), custom_call_target="tpu_custom_call" | custom-call | tf_op jit(solution)/shard_map/spread/pallas_call | solution.py:45
  2.1 12.0 %all-to-all-start = ((f32[32,16,128]{2,1,0:T(8,128)}), f32[32,16,128]{2,1,0:T(8,128)S(1)}, u32[]{:S(2)}, u32[]{:S(2)}) async-start(f32[32,16,128]{2,1,0:T(8,128)} %spread.1), calls=%async_computation | async-start | bytes 524288 | tf_op jit(solution)/shard_map/all_to_all | solution.py:283
  14.1 0.0 copy-start.1
  14.1 0.6 %copy-done.1 = s32[1,48,1]{1,2,0:T(1,128)S(1)} copy-done((s32[1,48,1]{1,2,0:T(1,128)S(1)}, s32[1,48,1]{1,2,0:T(1,128)}, u32[]{:S(2)}) %copy-start.1) | copy-done | bytes 216
  14.8 0.7 %copy-done.2 = s32[1,48]{1,0:T(1,128)S(1)} copy-done((s32[1,48]{1,0:T(1,128)S(1)}, s32[1,48]{1,0:T(1,128)}, u32[]{:S(2)}) %copy-start.2) | copy-done | bytes 216
  15.4 0.7 %copy-done.3 = s32[1,48]{1,0:T(1,128)S(1)} copy-done((s32[1,48]{1,0:T(1,128)S(1)}, s32[1,48]{1,0:T(1,128)}, u32[]{:S(2)}) %copy-start.3) | copy-done | bytes 216
  16.1 2.5 %stage.1 = (bf16[24,128,128]{2,1,0:T(8,128)(2,1)S(1)}, bf16[24,128,128]{2,1,0:T(8,128)(2,1)S(1)}, f32[64,1,128]{2,1,0:T(1,128)S(1)}, s32[192]{0:T(256)S(1)}) custom-call(s32[1,48]{1,0:T(1,128)S(1)} %bitcast.5, s32[1,48]{1,0:T(1,128)S(1)} %copy-done.2, s32[1,48]{1,0:T(1,128)S(1)} %copy-done.3, bf16[48,128,128]{2,1,0:T(8,128)(2,1)} %cost_in_ref.4, ...), custom_call_target="tpu_custom_call" | custom-call | bytes 3145728 | tf_op jit(solution)/shard_map/stage/pallas_call | solution.py:202
  18.6 6.7 %all-to-all-done = f32[32,16,128]{2,1,0:T(8,128)S(1)} async-done(((f32[32,16,128]{2,1,0:T(8,128)}), f32[32,16,128]{2,1,0:T(8,128)S(1)}, u32[]{:S(2)}, u32[]{:S(2)}) %all-to-all-start) | async-done | bytes 262176 | tf_op jit(solution)/shard_map/all_to_all | solution.py:283
  25.3 2.5 %collective-permute-start = (f32[512,128]{1,0:T(8,128)S(1)}, f32[512,128]{1,0:T(8,128)S(1)}, u32[]{:S(2)}, u32[]{:S(2)}) collective-permute-start(f32[512,128]{1,0:T(8,128)S(1)} %bitcast.3), channel_id=1, source_target_pairs={{0,4},{4,0},{1,5},{5,1},{2,6},{6,2},{3,7},{7,3},{8,12},{12,8},{9,1... | collective-permute-start | bytes 786440 | tf_op jit(solution)/shard_map/ppermute | solution.py:288
  27.8 1.4 %stage_late.1 = (bf16[24,128,128]{2,1,0:T(8,128)(2,1)S(1)}, bf16[24,128,128]{2,1,0:T(8,128)(2,1)S(1)}) custom-call(bf16[48,128,128]{2,1,0:T(8,128)(2,1)} %cost_in_ref.4, bf16[48,128,128]{2,1,0:T(8,128)(2,1)} %coef_in_ref.4), custom_call_target="tpu_custom_call" | custom-call | bytes 3145728 | tf_op jit(solution)/shard_map/stage_late/pallas_call | solution.py:221
  29.2 0.0 collective-permute-done.other_rows_ref
  29.2 2.1 %columns.1 = (f32[192,1,128]{2,1,0:T(1,128)}, f32[48,128]{1,0:T(8,128)S(1)}) custom-call(s32[192]{0:T(256)S(1)} %get-tuple-element.20.number_ref, f32[64,1,128]{2,1,0:T(1,128)S(1)} %get-tuple-element.21.named_ref, f32[512,128]{1,0:T(8,128)S(1)} %bitcast.4, f32[512,128]{1,0:T(8,128)S(1)} %collective-permute-done.other_rows_ref, ...), custom_call_target="tpu_custom_call" | custom-call | flops 4718592 | bytes 3145728 | tf_op jit(solution)/shard_map/columns/pallas_call | solution.py:234
  31.2 4.4 %all-to-all-start.1 = ((f32[64,1,384]{2,1,0:T(1,128)}), f32[64,1,384]{2,1,0:T(1,128)S(1)}, u32[]{:S(2)}, u32[]{:S(2)}) async-start(f32[64,1,384]{2,1,0:T(1,128)} %bitcast.2), calls=%async_computation.1 | async-start | bytes 196608 | tf_op jit(solution)/shard_map/all_to_all | solution.py:292
  35.6 2.5 %primal.1 = (bf16[48,128,128]{2,1,0:T(8,128)(2,1)S(1)}, f32[32,128]{1,0:T(8,128)S(1)}) custom-call(s32[192]{0:T(256)S(1)} %get-tuple-element.20.number_ref, f32[48,128]{1,0:T(8,128)S(1)} %get-tuple-element.29.minus_ref, bf16[24,128,128]{2,1,0:T(8,128)(2,1)S(1)} %get-tuple-element.23.early_cost_ref, ...), custom_call_target="tpu_custom_call" | custom-call | flops 4718592 | bytes 4718592 | tf_op jit(solution)/shard_map/primal/pallas_call | solution.py:253
  38.2 2.6 %collective-permute-start.3 = (f32[32,128]{1,0:T(8,128)S(1)}, f32[32,128]{1,0:T(8,128)S(1)}, u32[]{:S(2)}, u32[]{:S(2)}) collective-permute-start(f32[32,128]{1,0:T(8,128)S(1)} %get-tuple-element.32.m0_ref), channel_id=1, source_target_pairs={{0,3},{1,2},{2,1},{3,0},{4,7},{5,6},{6,5},{7,4},{8,11},{9,10},{10,... | collective-permute-start | bytes 49160 | tf_op jit(solution)/shard_map/ppermute | solution.py:294
  40.7 0.5 %collective-permute-start.2 = (f32[32,128]{1,0:T(8,128)S(1)}, f32[32,128]{1,0:T(8,128)S(1)}, u32[]{:S(2)}, u32[]{:S(2)}) collective-permute-start(f32[32,128]{1,0:T(8,128)S(1)} %get-tuple-element.32.m0_ref), channel_id=1, source_target_pairs={{0,2},{1,3},{2,0},{3,1},{4,6},{5,7},{6,4},{7,5},{8,10},{9,11},{10,... | collective-permute-start | bytes 49160 | tf_op jit(solution)/shard_map/ppermute | solution.py:294
  41.3 0.3 collective-permute-start.1
  41.5 1.1 %copy.10 = bf16[48,128,128]{2,1,0:T(8,128)(2,1)} copy(bf16[48,128,128]{2,1,0:T(8,128)(2,1)S(1)} %get-tuple-element.35) | data formatting | bytes 3145728
  42.7 0.0 collective-permute-done.3.m3_ref
  42.7 2.5 %collective-permute-done.2.m2_ref = f32[32,128]{1,0:T(8,128)S(1)} collective-permute-done((f32[32,128]{1,0:T(8,128)S(1)}, f32[32,128]{1,0:T(8,128)S(1)}, u32[]{:S(2)}, u32[]{:S(2)}) %collective-permute-start.2) | collective-permute-done | bytes 16416 | tf_op jit(solution)/shard_map/ppermute | solution.py:294
  45.1 0.0 collective-permute-done.1.m1_ref
  45.1 1.1 %all-to-all-done.1.recv_ref = f32[64,1,384]{2,1,0:T(1,128)S(1)} async-done(((f32[64,1,384]{2,1,0:T(1,128)}), f32[64,1,384]{2,1,0:T(1,128)S(1)}, u32[]{:S(2)}, u32[]{:S(2)}) %all-to-all-start.1) | async-done | bytes 98336 | tf_op jit(solution)/shard_map/all_to_all | solution.py:292
  46.2 0.0 copy-done
  46.2 0.8 %finish.1 = (f32[16,128]{1,0:T(8,128)}, f32[32,128]{1,0:T(8,128)}) custom-call(f32[64,1,384]{2,1,0:T(1,128)S(1)} %all-to-all-done.1.recv_ref, f32[32,128]{1,0:T(8,128)S(1)} %get-tuple-element.32.m0_ref, f32[32,128]{1,0:T(8,128)S(1)} %collective-permute-done.1.m1_ref, f32[32,128]{1,0:T(8,128)S(1)} %collective-permute-done.2.m2_ref, ...), custom_call_target="tpu_custom_call" | custom-call | tf_op jit(solution)/shard_map/finish/pallas_call | solution.py:268
  (3 shorter events, 0.0 us)
Async XLA Ops:
  2.1 23.2 %all-to-all-start = ((f32[32,16,128]{2,1,0:T(8,128)}), f32[32,16,128]{2,1,0:T(8,128)S(1)}, u32[]{:S(2)}, u32[]{:S(2)}) async-start(f32[32,16,128]{2,1,0:T(8,128)} %spread.1), calls=%async_computation | async-start | bytes 524288 | tf_op jit(solution)/shard_map/all_to_all | solution.py:283
  14.1 0.7 %copy-start.1 = (s32[1,48,1]{1,2,0:T(1,128)S(1)}, s32[1,48,1]{1,2,0:T(1,128)}, u32[]{:S(2)}) copy-start(s32[1,48,1]{1,2,0:T(1,128)} %param.10) | copy-start | bytes 580
  14.8 0.7 %copy-start.2 = (s32[1,48]{1,0:T(1,128)S(1)}, s32[1,48]{1,0:T(1,128)}, u32[]{:S(2)}) copy-start(s32[1,48]{1,0:T(1,128)} %local_in_ref.1) | copy-start | bytes 580
  15.4 0.7 %copy-start.3 = (s32[1,48]{1,0:T(1,128)S(1)}, s32[1,48]{1,0:T(1,128)}, u32[]{:S(2)}) copy-start(s32[1,48]{1,0:T(1,128)} %member_in_ref.1) | copy-start | bytes 580
  25.3 3.8 %collective-permute-start = (f32[512,128]{1,0:T(8,128)S(1)}, f32[512,128]{1,0:T(8,128)S(1)}, u32[]{:S(2)}, u32[]{:S(2)}) collective-permute-start(f32[512,128]{1,0:T(8,128)S(1)} %bitcast.3), channel_id=1, source_target_pairs={{0,4},{4,0},{1,5},{5,1},{2,6},{6,2},{3,7},{7,3},{8,12},{12,8},{9,1... | collective-permute-start | bytes 786440 | tf_op jit(solution)/shard_map/ppermute | solution.py:288
  31.2 15.0 %all-to-all-start.1 = ((f32[64,1,384]{2,1,0:T(1,128)}), f32[64,1,384]{2,1,0:T(1,128)S(1)}, u32[]{:S(2)}, u32[]{:S(2)}) async-start(f32[64,1,384]{2,1,0:T(1,128)} %bitcast.2), calls=%async_computation.1 | async-start | bytes 196608 | tf_op jit(solution)/shard_map/all_to_all | solution.py:292
  38.2 4.5 %collective-permute-start.3 = (f32[32,128]{1,0:T(8,128)S(1)}, f32[32,128]{1,0:T(8,128)S(1)}, u32[]{:S(2)}, u32[]{:S(2)}) collective-permute-start(f32[32,128]{1,0:T(8,128)S(1)} %get-tuple-element.32.m0_ref), channel_id=1, source_target_pairs={{0,3},{1,2},{2,1},{3,0},{4,7},{5,6},{6,5},{7,4},{8,11},{9,10},{10,... | collective-permute-start | bytes 49160 | tf_op jit(solution)/shard_map/ppermute | solution.py:294
  40.7 4.4 %collective-permute-start.2 = (f32[32,128]{1,0:T(8,128)S(1)}, f32[32,128]{1,0:T(8,128)S(1)}, u32[]{:S(2)}, u32[]{:S(2)}) collective-permute-start(f32[32,128]{1,0:T(8,128)S(1)} %get-tuple-element.32.m0_ref), channel_id=1, source_target_pairs={{0,2},{1,3},{2,0},{3,1},{4,6},{5,7},{6,4},{7,5},{8,10},{9,11},{10,... | collective-permute-start | bytes 49160 | tf_op jit(solution)/shard_map/ppermute | solution.py:294
  41.3 3.9 %collective-permute-start.1 = (f32[32,128]{1,0:T(8,128)S(1)}, f32[32,128]{1,0:T(8,128)S(1)}, u32[]{:S(2)}, u32[]{:S(2)}) collective-permute-start(f32[32,128]{1,0:T(8,128)S(1)} %get-tuple-element.32.m0_ref), channel_id=1, source_target_pairs={{0,1},{1,0},{2,3},{3,2},{4,5},{5,4},{6,7},{7,6},{8,9},{9,8},{10,11... | collective-permute-start | bytes 49160 | tf_op jit(solution)/shard_map/ppermute | solution.py:294
  41.5 4.7 %copy-start = (s32[16,128]{1,0:T(8,128)S(1)}, s32[16,128]{1,0:T(8,128)}, u32[]{:S(2)}) copy-start(s32[16,128]{1,0:T(8,128)} %capacity_ref.1) | copy-start | bytes 24580

commit v6 on v5

--- a/solution.py
+++ b/solution.py
@@ -58,13 +58,13 @@
 
 
 def stage_kernel(
-    owner_ref, local_in_ref, member_in_ref, cost_in_ref, coef_in_ref,
-    cost_ref, coef_ref, named_ref, number_ref, count_ref, sem,
+    owner_ref, local_in_ref, member_in_ref, coef_in_ref,
+    early_ref, late_ref, named_ref, number_ref, count_ref, sem,
 ):
-    load_cost = pltpu.make_async_copy(cost_in_ref.at[pl.ds(0, EARLY)], cost_ref, sem.at[0])
-    load_coef = pltpu.make_async_copy(coef_in_ref.at[pl.ds(0, EARLY)], coef_ref, sem.at[1])
-    load_cost.start()
-    load_coef.start()
+    load_early = pltpu.make_async_copy(coef_in_ref.at[pl.ds(0, EARLY)], early_ref, sem.at[0])
+    load_late = pltpu.make_async_copy(coef_in_ref.at[pl.ds(EARLY, LATE)], late_ref, sem.at[1])
+    load_early.start()
+    load_late.start()
     core = lax.axis_index("c")
     lane = lax.broadcasted_iota(jnp.int32, (1, BLOCK), 1)
     named_ref[...] = jnp.full((MEM, 1, BLOCK), -1.0, jnp.float32)
@@ -89,22 +89,13 @@
         return carry
 
     lax.fori_loop(0, CAP, slot, 0)
-    load_cost.wait()
-    load_coef.wait()
-
-
-def stage_late_kernel(cost_in_ref, coef_in_ref, cost_ref, coef_ref, sem):
-    load_cost = pltpu.make_async_copy(cost_in_ref.at[pl.ds(EARLY, LATE)], cost_ref, sem.at[0])
-    load_coef = pltpu.make_async_copy(coef_in_ref.at[pl.ds(EARLY, LATE)], coef_ref, sem.at[1])
-    load_cost.start()
-    load_coef.start()
-    load_cost.wait()
-    load_coef.wait()
+    load_early.wait()
+    load_late.wait()
 
 
 def columns_kernel(
     number_ref, named_ref, own_rows_ref, other_rows_ref,
-    early_cost_ref, early_coef_ref, late_cost_ref, late_coef_ref,
+    cost_ref, early_coef_ref, late_coef_ref,
     send_ref, minus_ref, column_ref, total_ref,
 ):
     send_ref[...] = jnp.zeros((MEM * ROWS, 1, BLOCK), jnp.float32)
@@ -114,13 +105,13 @@
         at = pl.ds(number_ref[ROW + s], 1)
         minus_ref[s:s + 1, :] = -jnp.where(number_ref[OTHER + s] == 1, other_rows_ref[at, :], own_rows_ref[at, :])
 
-    def run(first, count, cost_ref, coef_ref):
+    def run(first, count, coef_ref):
         def block(i, carry):
             s = first + i
             minus_dual = minus_ref[pl.ds(s, 1), :]
             column = None
             for g in range(0, BLOCK, 32):
-                cost = cost_ref[i, g:g + 32].astype(jnp.float32)
+                cost = cost_ref[s, g:g + 32].astype(jnp.float32)
                 coef = coef_ref[i, g:g + 32].astype(jnp.float32)
                 alloc = jnp.minimum(jnp.maximum(coef * minus_dual - cost, 0.0), 1.0)
                 part = jnp.sum((coef * alloc).reshape(4, 8, BLOCK), axis=0)
@@ -130,21 +121,21 @@
 
         lax.fori_loop(0, count, block, 0, unroll=count)
 
-    run(0, EARLY, early_cost_ref, early_coef_ref)
-    run(EARLY, LATE, late_cost_ref, late_coef_ref)
+    run(0, EARLY, early_coef_ref)
+    run(EARLY, LATE, late_coef_ref)
     total_ref[...] = jnp.sum(column_ref[...].reshape(CAP, 8, BLOCK), axis=1)
     for s in range(CAP):
         send_ref[number_ref[PLACE + s]] = total_ref[s:s + 1, :]
 
 
 def primal_kernel(
-    number_ref, minus_ref, early_cost_ref, early_coef_ref, cost_in_ref, coef_in_ref,
-    primal_ref, member_out_ref, late_cost_ref, late_coef_ref, sums_ref, sem,
+    number_ref, minus_ref, early_coef_ref, late_coef_ref, cost_in_ref,
+    primal_ref, member_out_ref, early_cost_ref, late_cost_ref, sums_ref, sem,
 ):
-    load_cost = pltpu.make_async_copy(cost_in_ref.at[pl.ds(EARLY, LATE)], late_cost_ref, sem.at[0])
-    load_coef = pltpu.make_async_copy(coef_in_ref.at[pl.ds(EARLY, LATE)], late_coef_ref, sem.at[1])
-    load_cost.start()
-    load_coef.start()
+    load_early = pltpu.make_async_copy(cost_in_ref.at[pl.ds(0, EARLY)], early_cost_ref, sem.at[0])
+    load_late = pltpu.make_async_copy(cost_in_ref.at[pl.ds(EARLY, LATE)], late_cost_ref, sem.at[1])
+    load_early.start()
+    load_late.start()
     member_out_ref[...] = jnp.zeros((MB_DEV, BLOCK), jnp.float32)
     ones = jnp.ones((8, 2 * BLOCK), jnp.bfloat16)
 
@@ -173,9 +164,9 @@
 
         lax.fori_loop(0, count // 2, pair, 0, unroll=count // 2)
 
+    load_early.wait()
     run(0, EARLY, early_cost_ref, early_coef_ref)
-    load_cost.wait()
-    load_coef.wait()
+    load_late.wait()
     run(EARLY, LATE, late_cost_ref, late_coef_ref)
     for s in range(CAP):
         member_out_ref[pl.ds(number_ref[MEMBER + s], 1), :] += sums_ref[s:s + 1, :]
@@ -197,7 +188,7 @@
     gradient_ref[...] = summed - capacity_ref[...].astype(jnp.float32)
 
 
-def stage(owner, local, member, cost, coef):
+def stage(owner, local, member, coef):
     early = pltpu.VMEM((EARLY, BLOCK, BLOCK), jnp.bfloat16)
     return pl.pallas_call(
         stage_kernel,
@@ -207,27 +198,13 @@
             pltpu.VMEM((MEM, 1, BLOCK), jnp.float32),
             jax.ShapeDtypeStruct((4 * CAP,), jnp.int32),
         ),
-        in_specs=[SMEM] * 3 + [ANY] * 2,
+        in_specs=[SMEM] * 3 + [ANY],
         out_specs=(VMEM, VMEM, VMEM, SMEM),
         scratch_shapes=[pltpu.SMEM((MEM,), jnp.int32), pltpu.SemaphoreType.DMA((2,))],
         compiler_params=pltpu.CompilerParams(vmem_limit_bytes=4 * 1024 * 1024),
         cost_estimate=pl.CostEstimate(flops=0, bytes_accessed=8 * EARLY * BLOCK * BLOCK, transcendentals=0),
         name="stage",
-    )(owner, local, member, in_hbm(cost), in_hbm(coef))
-
-
-def stage_late(cost, coef):
-    late = pltpu.VMEM((LATE, BLOCK, BLOCK), jnp.bfloat16)
-    return pl.pallas_call(
-        stage_late_kernel,
-        out_shape=(late, late),
-        in_specs=[ANY] * 2,
-        out_specs=(VMEM, VMEM),
-        scratch_shapes=[pltpu.SemaphoreType.DMA((2,))],
-        compiler_params=pltpu.CompilerParams(vmem_limit_bytes=4 * 1024 * 1024),
-        cost_estimate=pl.CostEstimate(flops=0, bytes_accessed=8 * LATE * BLOCK * BLOCK, transcendentals=0),
-        name="stage_late",
-    )(in_hbm(cost), in_hbm(coef))
+    )(owner, local, member, in_hbm(coef))
 
 
 def columns(number, *blocks):
@@ -237,7 +214,7 @@
             jax.ShapeDtypeStruct((MEM * ROWS, 1, BLOCK), jnp.float32),
             pltpu.VMEM((CAP, BLOCK), jnp.float32),
         ),
-        in_specs=[SMEM] + [VMEM] * 7,
+        in_specs=[SMEM] + [VMEM] * 6,
         out_specs=(VMEM, VMEM),
         scratch_shapes=[pltpu.VMEM((CAP * 8, BLOCK), jnp.float32), pltpu.VMEM((CAP, BLOCK), jnp.float32)],
         compiler_params=pltpu.CompilerParams(vmem_limit_bytes=8 * MIB),
@@ -248,20 +225,20 @@
     )(number, *map(in_vmem, blocks))
 
 
-def primal_and_members(number, minus, early_cost, early_coef, cost, coef):
-    late = pltpu.VMEM((LATE, BLOCK, BLOCK), jnp.bfloat16)
+def primal_and_members(number, minus, early_coef, late_coef, cost):
+    half = pltpu.VMEM((EARLY, BLOCK, BLOCK), jnp.bfloat16)
     return pl.pallas_call(
         primal_kernel,
         out_shape=(pltpu.VMEM((CAP, BLOCK, BLOCK), jnp.bfloat16), pltpu.VMEM((MB_DEV, BLOCK), jnp.float32)),
-        in_specs=[SMEM] + [VMEM] * 3 + [ANY] * 2,
+        in_specs=[SMEM] + [VMEM] * 3 + [ANY],
         out_specs=(VMEM, VMEM),
-        scratch_shapes=[late, late, pltpu.VMEM((CAP, BLOCK), jnp.float32), pltpu.SemaphoreType.DMA((2,))],
+        scratch_shapes=[half, half, pltpu.VMEM((CAP, BLOCK), jnp.float32), pltpu.SemaphoreType.DMA((2,))],
         compiler_params=pltpu.CompilerParams(vmem_limit_bytes=8 * MIB),
         cost_estimate=pl.CostEstimate(
             flops=6 * CAP * BLOCK * BLOCK, bytes_accessed=6 * CAP * BLOCK * BLOCK, transcendentals=0
         ),
         name="primal",
-    )(number, in_vmem(minus), in_vmem(early_cost), in_vmem(early_coef), in_hbm(cost), in_hbm(coef))
+    )(number, in_vmem(minus), in_vmem(early_coef), in_vmem(late_coef), in_hbm(cost))
 
 
 def finish(recv, share, others, capacity):
@@ -281,16 +258,13 @@
 def per_device(pair_cost, pair_coef, slot_member, slot_owner, slot_local, duals, capacity):
     copies = spread(duals)
     rows = lax.all_to_all(copies, ("z", "y"), split_axis=0, concat_axis=0, tiled=True).reshape(HALF, BLOCK)
-    cost, coef, named, number = stage(
-        slot_owner.reshape(1, CAP), slot_local, slot_member, pair_cost, pair_coef
-    )
-    rows, number, late_cost, late_coef = lax.optimization_barrier((rows, number, pair_cost, pair_coef))
+    early, late, named, number = stage(slot_owner.reshape(1, CAP), slot_local, slot_member, pair_coef)
+    rows, number = lax.optimization_barrier((rows, number))
     other_rows = lax.ppermute(rows, "c", [(0, 1), (1, 0)])
-    late_cost, late_coef = stage_late(late_cost, late_coef)
-    send, minus = columns(number, named, rows, other_rows, cost, coef, late_cost, late_coef)
+    send, minus = columns(number, named, rows, other_rows, pair_cost, early, late)
     send = send.reshape(MEM, 1, ROWS * BLOCK)
     recv = lax.all_to_all(send, ("z", "y", "c"), split_axis=0, concat_axis=0, tiled=True)
-    primal, share = primal_and_members(number, minus, cost, coef, pair_cost, pair_coef)
+    primal, share = primal_and_members(number, minus, early, late, pair_cost)
     others = [lax.ppermute(share, "x", [(i, i ^ k) for i in range(X)]) for k in (1, 2, 3)]
     gradient, share = finish(recv, share, others, capacity)
     return primal, gradient, share

time: 47.4 us -> 47.5 us (level)
  Pallas kernels: 10.7 us -> 9.75 us
  waiting for transfers between devices: 10.2 us -> 11.1 us
    pallas_call x1 -> x0, Pallas kernels: 1.39 us -> none  [stage_late(): pl.pallas_call(stage_late_kernel, out_shape=(late, late), in_specs=[ANY]...]
    ppermute x1, waiting for transfers between devices: 0.01 us -> 1.16 us  [per_device(): other_rows = lax.ppermute(rows, 'c', [(0, 1), (1, 0)])]
    unnamed x9 -> x11, local copies, waits for them, and re-layouts: 3.11 us -> 3.11 us
  transfers between devices with their start and end apart: 6 -> 6, of which waited for: 3 -> 4; matrix products, arithmetic and copies ran while one was open for 2% -> 2% of each run, Pallas kernels for 14% -> 11%
where the time goes in v6:
time: 47.5 us; the launch traced here: 47.1 us
  starting transfers between devices  22.5 us (47%)
  waiting for transfers between devices  11.1 us (23%)
  Pallas kernels  9.75 us (21%)
  local copies, waits for them, and re-layouts  3.11 us (7%)
  between operations  0.7 us (1%)
    all_to_all x1, starting transfers between devices, per_device(): lax.all_to_all(copies, ('z', 'y'), split_axis=0, concat_axis=0, tiled=True)  12 us
    all_to_all x1, waiting for transfers between devices, per_device(): lax.all_to_all(copies, ('z', 'y'), split_axis=0, concat_axis=0, tiled=True)  6.67 us
    all_to_all x1, starting transfers between devices, per_device(): lax.all_to_all(send, ('z', 'y', 'c'), split_axis=0, concat_axis=0, tiled=...  4.63 us
    ppermute x3, starting transfers between devices, per_device(): lax.ppermute(share, 'x', [(i, i ^ k) for i in range(X)])  3.34 us
    unnamed x11, local copies, waits for them, and re-layouts  3.11 us
    pallas_call x1, Pallas kernels, primal_and_members(): pl.pallas_call(primal_kernel, out_shape=(pltpu.VMEM((CAP, BLOCK, BLOCK),...  2.81 us
    pallas_call x1, Pallas kernels, stage(): pl.pallas_call(stage_kernel, out_shape=(early, early, pltpu.VMEM((MEM, 1,...  2.54 us
    ppermute x3, waiting for transfers between devices, per_device(): lax.ppermute(share, 'x', [(i, i ^ k) for i in range(X)])  2.47 us
  transfers between devices with their start and end apart: 6, of which 4 were waited for; matrix products, arithmetic and copies ran while one was open for 2% of the time, Pallas kernels for 11%

profile of v6, /device:TPU:1, one launch (start us, length us, event | category | flops | bytes accessed | tf_op | source)
XLA Modules:
  0.0 47.1 jit_solution(11767272507756810708)
XLA Ops:
  0.6 0.0 copy-start
  0.6 1.6 %spread.1 = f32[32,16,128]{2,1,0:T(8,128)} custom-call(f32[16,128]{1,0:T(8,128)} %duals_ref.1), custom_call_target="tpu_custom_call" | custom-call | tf_op jit(solution)/shard_map/spread/pallas_call | solution.py:45
  2.2 12.0 %all-to-all-start = ((f32[32,16,128]{2,1,0:T(8,128)}), f32[32,16,128]{2,1,0:T(8,128)S(1)}, u32[]{:S(2)}, u32[]{:S(2)}) async-start(f32[32,16,128]{2,1,0:T(8,128)} %spread.1), calls=%async_computation | async-start | bytes 524288 | tf_op jit(solution)/shard_map/all_to_all | solution.py:260
  14.3 0.0 copy-start.2
  14.3 0.6 %copy-done.2 = s32[1,48,1]{1,2,0:T(1,128)S(1)} copy-done((s32[1,48,1]{1,2,0:T(1,128)S(1)}, s32[1,48,1]{1,2,0:T(1,128)}, u32[]{:S(2)}) %copy-start.2) | copy-done | bytes 216
  14.9 0.7 %copy-done.3 = s32[1,48]{1,0:T(1,128)S(1)} copy-done((s32[1,48]{1,0:T(1,128)S(1)}, s32[1,48]{1,0:T(1,128)}, u32[]{:S(2)}) %copy-start.3) | copy-done | bytes 216
  15.6 0.7 %copy-done.4 = s32[1,48]{1,0:T(1,128)S(1)} copy-done((s32[1,48]{1,0:T(1,128)S(1)}, s32[1,48]{1,0:T(1,128)}, u32[]{:S(2)}) %copy-start.4) | copy-done | bytes 216
  16.2 2.5 %stage.1 = (bf16[24,128,128]{2,1,0:T(8,128)(2,1)S(1)}, bf16[24,128,128]{2,1,0:T(8,128)(2,1)S(1)}, f32[64,1,128]{2,1,0:T(1,128)S(1)}, s32[192]{0:T(256)S(1)}) custom-call(s32[1,48]{1,0:T(1,128)S(1)} %bitcast.5, s32[1,48]{1,0:T(1,128)S(1)} %copy-done.3, s32[1,48]{1,0:T(1,128)S(1)} %copy-done.4, bf16[48,128,128]{2,1,0:T(8,128)(2,1)} %coef_in_ref.1), custom_call_target="tpu_custom_call" | custom-call | bytes 3145728 | tf_op jit(solution)/shard_map/stage/pallas_call | solution.py:193
  18.8 6.7 %all-to-all-done = f32[32,16,128]{2,1,0:T(8,128)S(1)} async-done(((f32[32,16,128]{2,1,0:T(8,128)}), f32[32,16,128]{2,1,0:T(8,128)S(1)}, u32[]{:S(2)}, u32[]{:S(2)}) %all-to-all-start) | async-done | bytes 262176 | tf_op jit(solution)/shard_map/all_to_all | solution.py:260
  25.4 2.5 %collective-permute-start = (f32[512,128]{1,0:T(8,128)S(1)}, f32[512,128]{1,0:T(8,128)S(1)}, u32[]{:S(2)}, u32[]{:S(2)}) collective-permute-start(f32[512,128]{1,0:T(8,128)S(1)} %bitcast.3), channel_id=1, source_target_pairs={{0,4},{4,0},{1,5},{5,1},{2,6},{6,2},{3,7},{7,3},{8,12},{12,8},{9,1... | collective-permute-start | bytes 786440 | tf_op jit(solution)/shard_map/ppermute | solution.py:263
  27.9 1.2 %collective-permute-done.other_rows_ref = f32[512,128]{1,0:T(8,128)S(1)} collective-permute-done((f32[512,128]{1,0:T(8,128)S(1)}, f32[512,128]{1,0:T(8,128)S(1)}, u32[]{:S(2)}, u32[]{:S(2)}) %collective-permute-start) | collective-permute-done | bytes 262176 | tf_op jit(solution)/shard_map/ppermute | solution.py:263
  29.1 0.0 copy-done
  29.1 2.1 %columns.1 = (f32[192,1,128]{2,1,0:T(1,128)}, f32[48,128]{1,0:T(8,128)S(1)}) custom-call(s32[192]{0:T(256)S(1)} %get-tuple-element.16.number_ref, f32[64,1,128]{2,1,0:T(1,128)S(1)} %get-tuple-element.17.named_ref, f32[512,128]{1,0:T(8,128)S(1)} %bitcast.4, f32[512,128]{1,0:T(8,128)S(1)} %collective-permute-done.other_rows_ref, ...), custom_call_target="tpu_custom_call" | custom-call | flops 4718592 | bytes 3145728 | tf_op jit(solution)/shard_map/columns/pallas_call | solution.py:211
  31.1 4.6 %all-to-all-start.1 = ((f32[64,1,384]{2,1,0:T(1,128)}), f32[64,1,384]{2,1,0:T(1,128)S(1)}, u32[]{:S(2)}, u32[]{:S(2)}) async-start(f32[64,1,384]{2,1,0:T(1,128)} %bitcast.2), calls=%async_computation.1 | async-start | bytes 196608 | tf_op jit(solution)/shard_map/all_to_all | solution.py:266
  35.8 2.8 %primal.1 = (bf16[48,128,128]{2,1,0:T(8,128)(2,1)S(1)}, f32[32,128]{1,0:T(8,128)S(1)}) custom-call(s32[192]{0:T(256)S(1)} %get-tuple-element.16.number_ref, f32[48,128]{1,0:T(8,128)S(1)} %get-tuple-element.21.minus_ref, bf16[24,128,128]{2,1,0:T(8,128)(2,1)S(1)} %get-tuple-element.19.early_coef_ref, ...), custom_call_target="tpu_custom_call" | custom-call | flops 4718592 | bytes 4718592 | tf_op jit(solution)/shard_map/primal/pallas_call | solution.py:230
  38.6 2.6 %collective-permute-start.3 = (f32[32,128]{1,0:T(8,128)S(1)}, f32[32,128]{1,0:T(8,128)S(1)}, u32[]{:S(2)}, u32[]{:S(2)}) collective-permute-start(f32[32,128]{1,0:T(8,128)S(1)} %get-tuple-element.24.m0_ref), channel_id=1, source_target_pairs={{0,3},{1,2},{2,1},{3,0},{4,7},{5,6},{6,5},{7,4},{8,11},{9,10},{10,... | collective-permute-start | bytes 49160 | tf_op jit(solution)/shard_map/ppermute | solution.py:268
  41.1 0.5 %collective-permute-start.2 = (f32[32,128]{1,0:T(8,128)S(1)}, f32[32,128]{1,0:T(8,128)S(1)}, u32[]{:S(2)}, u32[]{:S(2)}) collective-permute-start(f32[32,128]{1,0:T(8,128)S(1)} %get-tuple-element.24.m0_ref), channel_id=1, source_target_pairs={{0,2},{1,3},{2,0},{3,1},{4,6},{5,7},{6,4},{7,5},{8,10},{9,11},{10,... | collective-permute-start | bytes 49160 | tf_op jit(solution)/shard_map/ppermute | solution.py:268
  41.7 0.3 collective-permute-start.1
  41.9 1.1 %copy.10 = bf16[48,128,128]{2,1,0:T(8,128)(2,1)} copy(bf16[48,128,128]{2,1,0:T(8,128)(2,1)S(1)} %get-tuple-element.27) | data formatting | bytes 3145728
  43.1 0.0 collective-permute-done.3.m3_ref
  43.1 2.5 %collective-permute-done.2.m2_ref = f32[32,128]{1,0:T(8,128)S(1)} collective-permute-done((f32[32,128]{1,0:T(8,128)S(1)}, f32[32,128]{1,0:T(8,128)S(1)}, u32[]{:S(2)}, u32[]{:S(2)}) %collective-permute-start.2) | collective-permute-done | bytes 16416 | tf_op jit(solution)/shard_map/ppermute | solution.py:268
  45.5 0.0 collective-permute-done.1.m1_ref
  45.5 0.8 %all-to-all-done.1.recv_ref = f32[64,1,384]{2,1,0:T(1,128)S(1)} async-done(((f32[64,1,384]{2,1,0:T(1,128)}), f32[64,1,384]{2,1,0:T(1,128)S(1)}, u32[]{:S(2)}, u32[]{:S(2)}) %all-to-all-start.1) | async-done | bytes 98336 | tf_op jit(solution)/shard_map/all_to_all | solution.py:266
  46.3 0.8 %finish.1 = (f32[16,128]{1,0:T(8,128)}, f32[32,128]{1,0:T(8,128)}) custom-call(f32[64,1,384]{2,1,0:T(1,128)S(1)} %all-to-all-done.1.recv_ref, f32[32,128]{1,0:T(8,128)S(1)} %get-tuple-element.24.m0_ref, f32[32,128]{1,0:T(8,128)S(1)} %collective-permute-done.1.m1_ref, f32[32,128]{1,0:T(8,128)S(1)} %collective-permute-done.2.m2_ref, ...), custom_call_target="tpu_custom_call" | custom-call | tf_op jit(solution)/shard_map/finish/pallas_call | solution.py:245
  (4 shorter events, 0.0 us)
Async XLA Ops:
  0.6 28.4 %copy-start = (bf16[48,128,128]{2,1,0:T(8,128)(2,1)S(1)}, bf16[48,128,128]{2,1,0:T(8,128)(2,1)}, u32[]{:S(2)}) copy-start(bf16[48,128,128]{2,1,0:T(8,128)(2,1)} %cost_in_ref.1) | copy-start | bytes 4718596
  2.2 23.2 %all-to-all-start = ((f32[32,16,128]{2,1,0:T(8,128)}), f32[32,16,128]{2,1,0:T(8,128)S(1)}, u32[]{:S(2)}, u32[]{:S(2)}) async-start(f32[32,16,128]{2,1,0:T(8,128)} %spread.1), calls=%async_computation | async-start | bytes 524288 | tf_op jit(solution)/shard_map/all_to_all | solution.py:260
  14.3 0.7 %copy-start.2 = (s32[1,48,1]{1,2,0:T(1,128)S(1)}, s32[1,48,1]{1,2,0:T(1,128)}, u32[]{:S(2)}) copy-start(s32[1,48,1]{1,2,0:T(1,128)} %param.10) | copy-start | bytes 580
  14.9 0.7 %copy-start.3 = (s32[1,48]{1,0:T(1,128)S(1)}, s32[1,48]{1,0:T(1,128)}, u32[]{:S(2)}) copy-start(s32[1,48]{1,0:T(1,128)} %local_in_ref.1) | copy-start | bytes 580
  15.6 0.7 %copy-start.4 = (s32[1,48]{1,0:T(1,128)S(1)}, s32[1,48]{1,0:T(1,128)}, u32[]{:S(2)}) copy-start(s32[1,48]{1,0:T(1,128)} %member_in_ref.1) | copy-start | bytes 580
  25.4 3.6 %collective-permute-start = (f32[512,128]{1,0:T(8,128)S(1)}, f32[512,128]{1,0:T(8,128)S(1)}, u32[]{:S(2)}, u32[]{:S(2)}) collective-permute-start(f32[512,128]{1,0:T(8,128)S(1)} %bitcast.3), channel_id=1, source_target_pairs={{0,4},{4,0},{1,5},{5,1},{2,6},{6,2},{3,7},{7,3},{8,12},{12,8},{9,1... | collective-permute-start | bytes 786440 | tf_op jit(solution)/shard_map/ppermute | solution.py:263
  31.1 15.2 %all-to-all-start.1 = ((f32[64,1,384]{2,1,0:T(1,128)}), f32[64,1,384]{2,1,0:T(1,128)S(1)}, u32[]{:S(2)}, u32[]{:S(2)}) async-start(f32[64,1,384]{2,1,0:T(1,128)} %bitcast.2), calls=%async_computation.1 | async-start | bytes 196608 | tf_op jit(solution)/shard_map/all_to_all | solution.py:266
  38.6 4.5 %collective-permute-start.3 = (f32[32,128]{1,0:T(8,128)S(1)}, f32[32,128]{1,0:T(8,128)S(1)}, u32[]{:S(2)}, u32[]{:S(2)}) collective-permute-start(f32[32,128]{1,0:T(8,128)S(1)} %get-tuple-element.24.m0_ref), channel_id=1, source_target_pairs={{0,3},{1,2},{2,1},{3,0},{4,7},{5,6},{6,5},{7,4},{8,11},{9,10},{10,... | collective-permute-start | bytes 49160 | tf_op jit(solution)/shard_map/ppermute | solution.py:268
  41.1 4.4 %collective-permute-start.2 = (f32[32,128]{1,0:T(8,128)S(1)}, f32[32,128]{1,0:T(8,128)S(1)}, u32[]{:S(2)}, u32[]{:S(2)}) collective-permute-start(f32[32,128]{1,0:T(8,128)S(1)} %get-tuple-element.24.m0_ref), channel_id=1, source_target_pairs={{0,2},{1,3},{2,0},{3,1},{4,6},{5,7},{6,4},{7,5},{8,10},{9,11},{10,... | collective-permute-start | bytes 49160 | tf_op jit(solution)/shard_map/ppermute | solution.py:268
  41.7 3.9 %collective-permute-start.1 = (f32[32,128]{1,0:T(8,128)S(1)}, f32[32,128]{1,0:T(8,128)S(1)}, u32[]{:S(2)}, u32[]{:S(2)}) collective-permute-start(f32[32,128]{1,0:T(8,128)S(1)} %get-tuple-element.24.m0_ref), channel_id=1, source_target_pairs={{0,1},{1,0},{2,3},{3,2},{4,5},{5,4},{6,7},{7,6},{8,9},{9,8},{10,11... | collective-permute-start | bytes 49160 | tf_op jit(solution)/shard_map/ppermute | solution.py:268
  41.9 4.4 %copy-start.1 = (s32[16,128]{1,0:T(8,128)S(1)}, s32[16,128]{1,0:T(8,128)}, u32[]{:S(2)}) copy-start(s32[16,128]{1,0:T(8,128)} %capacity_ref.1) | copy-start | bytes 24580

commit v7 on v5

--- a/solution.py
+++ b/solution.py
@@ -67,7 +67,9 @@
     load_coef.start()
     core = lax.axis_index("c")
     lane = lax.broadcasted_iota(jnp.int32, (1, BLOCK), 1)
-    named_ref[...] = jnp.full((MEM, 1, BLOCK), -1.0, jnp.float32)
+    named_ref[...] = jnp.zeros((MEM * ROWS, 1, BLOCK), jnp.float32)
+    for i in range(MEM):
+        named_ref[i * ROWS + 2] = jnp.full((1, BLOCK), -1.0, jnp.float32)
 
     def clear(i, carry):
         count_ref[i] = 0
@@ -85,7 +87,8 @@
         count_ref[owner] = k + 1
         number_ref[PLACE + s] = owner * ROWS + k
         half = (lane >= BLOCK // 2) == (k == 1)
-        named_ref[owner] = jnp.where(half, local.astype(jnp.float32), named_ref[owner])
+        at = owner * ROWS + 2
+        named_ref[at] = jnp.where(half, local.astype(jnp.float32), named_ref[at])
         return carry
 
     lax.fori_loop(0, CAP, slot, 0)
@@ -107,9 +110,7 @@
     early_cost_ref, early_coef_ref, late_cost_ref, late_coef_ref,
     send_ref, minus_ref, column_ref, total_ref,
 ):
-    send_ref[...] = jnp.zeros((MEM * ROWS, 1, BLOCK), jnp.float32)
-    for i in range(MEM):
-        send_ref[i * ROWS + 2] = named_ref[i]
+    send_ref[...] = named_ref[...]
     for s in range(CAP):
         at = pl.ds(number_ref[ROW + s], 1)
         minus_ref[s:s + 1, :] = -jnp.where(number_ref[OTHER + s] == 1, other_rows_ref[at, :], own_rows_ref[at, :])
@@ -181,8 +182,7 @@
         member_out_ref[pl.ds(number_ref[MEMBER + s], 1), :] += sums_ref[s:s + 1, :]
 
 
-def finish_kernel(recv_ref, m0_ref, m1_ref, m2_ref, m3_ref, capacity_ref, gradient_ref, share_ref):
-    share_ref[...] = ((m0_ref[...] + m1_ref[...]) + (m2_ref[...] + m3_ref[...])) * (1.0 / BLOCK)
+def finish_kernel(recv_ref, capacity_ref, gradient_ref):
     low = lax.broadcasted_iota(jnp.int32, (8, BLOCK), 1) < BLOCK // 2
     totals = [jnp.zeros((8, BLOCK), jnp.float32) for _ in range(JB_DEV)]
     for i in range(0, MEM, 8):
@@ -204,7 +204,7 @@
         out_shape=(
             early,
             early,
-            pltpu.VMEM((MEM, 1, BLOCK), jnp.float32),
+            pltpu.VMEM((MEM * ROWS, 1, BLOCK), jnp.float32),
             jax.ShapeDtypeStruct((4 * CAP,), jnp.int32),
         ),
         in_specs=[SMEM] * 3 + [ANY] * 2,
@@ -264,18 +264,15 @@
     )(number, in_vmem(minus), in_vmem(early_cost), in_vmem(early_coef), in_hbm(cost), in_hbm(coef))
 
 
-def finish(recv, share, others, capacity):
+def finish(recv, capacity):
     return pl.pallas_call(
         finish_kernel,
-        out_shape=(
-            jax.ShapeDtypeStruct((JB_DEV, BLOCK), jnp.float32),
-            jax.ShapeDtypeStruct((MB_DEV, BLOCK), jnp.float32),
-        ),
-        in_specs=[VMEM] * 6,
-        out_specs=(VMEM, VMEM),
-        compiler_params=pltpu.CompilerParams(vmem_limit_bytes=2 * 1024 * 1024),
+        out_shape=jax.ShapeDtypeStruct((JB_DEV, BLOCK), jnp.float32),
+        in_specs=[VMEM] * 2,
+        out_specs=VMEM,
+        compiler_params=pltpu.CompilerParams(vmem_limit_bytes=2 * MIB),
         name="finish",
-    )(recv, share, *others, capacity)
+    )(recv, capacity)
 
 
 def per_device(pair_cost, pair_coef, slot_member, slot_owner, slot_local, duals, capacity):
@@ -292,7 +289,8 @@
     recv = lax.all_to_all(send, ("z", "y", "c"), split_axis=0, concat_axis=0, tiled=True)
     primal, share = primal_and_members(number, minus, cost, coef, pair_cost, pair_coef)
     others = [lax.ppermute(share, "x", [(i, i ^ k) for i in range(X)]) for k in (1, 2, 3)]
-    gradient, share = finish(recv, share, others, capacity)
+    share = ((share + others[0]) + (others[1] + others[2])) * (1.0 / BLOCK)
+    gradient = finish(recv, capacity)
     return primal, gradient, share
 
 

time: 47.4 us -> 55.2 us (1.16)
  waiting for transfers between devices: 10.2 us -> 16.6 us
  starting transfers between devices: 22.2 us -> 23.1 us
  other arithmetic: 0 us -> 0.61 us
    all_to_all x1, waiting for transfers between devices: 1.08 us -> 9.91 us  [per_device(): lax.all_to_all(send, ('z', 'y', 'c'), split_axis=0, concat_axis=0, tiled=...]
    ppermute x3, waiting for transfers between devices: 2.47 us -> 0.01 us  [per_device(): lax.ppermute(share, 'x', [(i, i ^ k) for i in range(X)])]
    all_to_all x1, starting transfers between devices: 4.41 us -> 5.25 us  [per_device(): lax.all_to_all(send, ('z', 'y', 'c'), split_axis=0, concat_axis=0, tiled=...]
    mul x0 -> x1, other arithmetic: none -> 0.61 us  [per_device(): share = (share + others[0] + (others[1] + others[2])) * (1.0 / BLOCK)]
  transfers between devices with their start and end apart: 6 -> 6, of which waited for: 3 -> 2; matrix products, arithmetic and copies ran while one was open for 2% -> 3% of each run, Pallas kernels for 14% -> 7%
where the time goes in v7:
time: 55.2 us; the launch traced here: 54.8 us
  starting transfers between devices  23.1 us (42%)
  waiting for transfers between devices  16.6 us (30%)
  Pallas kernels  10.7 us (19%)
  local copies, waits for them, and re-layouts  3.11 us (6%)
  between operations  0.73 us (1%)
  other arithmetic  0.61 us (1%)
    all_to_all x1, starting transfers between devices, per_device(): lax.all_to_all(copies, ('z', 'y'), split_axis=0, concat_axis=0, tiled=True)  12 us
    all_to_all x1, waiting for transfers between devices, per_device(): lax.all_to_all(send, ('z', 'y', 'c'), split_axis=0, concat_axis=0, tiled=...  9.91 us
    all_to_all x1, waiting for transfers between devices, per_device(): lax.all_to_all(copies, ('z', 'y'), split_axis=0, concat_axis=0, tiled=True)  6.67 us
    all_to_all x1, starting transfers between devices, per_device(): lax.all_to_all(send, ('z', 'y', 'c'), split_axis=0, concat_axis=0, tiled=...  5.25 us
    ppermute x3, starting transfers between devices, per_device(): lax.ppermute(share, 'x', [(i, i ^ k) for i in range(X)])  3.34 us
    unnamed x9, local copies, waits for them, and re-layouts  3.11 us
    pallas_call x1, Pallas kernels, stage(): pl.pallas_call(stage_kernel, out_shape=(early, early, pltpu.VMEM((MEM * R...  2.54 us
    pallas_call x1, Pallas kernels, primal_and_members(): pl.pallas_call(primal_kernel, out_shape=(pltpu.VMEM((CAP, BLOCK, BLOCK),...  2.51 us
  transfers between devices with their start and end apart: 6, of which 2 were waited for; matrix products, arithmetic and copies ran while one was open for 3% of the time, Pallas kernels for 7%

profile of v7, /device:TPU:1, one launch (start us, length us, event | category | flops | bytes accessed | tf_op | source)
XLA Modules:
  0.0 54.8 jit_solution(15130647622569587976)
XLA Ops:
  0.6 1.4 %spread.1 = f32[32,16,128]{2,1,0:T(8,128)} custom-call(f32[16,128]{1,0:T(8,128)} %duals_ref.1), custom_call_target="tpu_custom_call" | custom-call | tf_op jit(solution)/shard_map/spread/pallas_call | solution.py:45
  2.1 12.0 %all-to-all-start = ((f32[32,16,128]{2,1,0:T(8,128)}), f32[32,16,128]{2,1,0:T(8,128)S(1)}, u32[]{:S(2)}, u32[]{:S(2)}) async-start(f32[32,16,128]{2,1,0:T(8,128)} %spread.1), calls=%async_computation | async-start | bytes 524288 | tf_op jit(solution)/shard_map/all_to_all | solution.py:280
  14.1 0.0 copy-start.1
  14.1 0.6 %copy-done.1 = s32[1,48,1]{1,2,0:T(1,128)S(1)} copy-done((s32[1,48,1]{1,2,0:T(1,128)S(1)}, s32[1,48,1]{1,2,0:T(1,128)}, u32[]{:S(2)}) %copy-start.1) | copy-done | bytes 216
  14.8 0.7 %copy-done.2 = s32[1,48]{1,0:T(1,128)S(1)} copy-done((s32[1,48]{1,0:T(1,128)S(1)}, s32[1,48]{1,0:T(1,128)}, u32[]{:S(2)}) %copy-start.2) | copy-done | bytes 216
  15.4 0.7 %copy-done.3 = s32[1,48]{1,0:T(1,128)S(1)} copy-done((s32[1,48]{1,0:T(1,128)S(1)}, s32[1,48]{1,0:T(1,128)}, u32[]{:S(2)}) %copy-start.3) | copy-done | bytes 216
  16.1 2.5 %stage.1 = (bf16[24,128,128]{2,1,0:T(8,128)(2,1)S(1)}, bf16[24,128,128]{2,1,0:T(8,128)(2,1)S(1)}, f32[192,1,128]{2,1,0:T(1,128)S(1)}, s32[192]{0:T(256)S(1)}) custom-call(s32[1,48]{1,0:T(1,128)S(1)} %bitcast.5, s32[1,48]{1,0:T(1,128)S(1)} %copy-done.2, s32[1,48]{1,0:T(1,128)S(1)} %copy-done.3, bf16[48,128,128]{2,1,0:T(8,128)(2,1)} %cost_in_ref.4, ...), custom_call_target="tpu_custom_call" | custom-call | bytes 3145728 | tf_op jit(solution)/shard_map/stage/pallas_call | solution.py:202
  18.6 6.7 %all-to-all-done = f32[32,16,128]{2,1,0:T(8,128)S(1)} async-done(((f32[32,16,128]{2,1,0:T(8,128)}), f32[32,16,128]{2,1,0:T(8,128)S(1)}, u32[]{:S(2)}, u32[]{:S(2)}) %all-to-all-start) | async-done | bytes 262176 | tf_op jit(solution)/shard_map/all_to_all | solution.py:280
  25.3 2.5 %collective-permute-start = (f32[512,128]{1,0:T(8,128)S(1)}, f32[512,128]{1,0:T(8,128)S(1)}, u32[]{:S(2)}, u32[]{:S(2)}) collective-permute-start(f32[512,128]{1,0:T(8,128)S(1)} %bitcast.3), channel_id=1, source_target_pairs={{0,4},{4,0},{1,5},{5,1},{2,6},{6,2},{3,7},{7,3},{8,12},{12,8},{9,1... | collective-permute-start | bytes 786440 | tf_op jit(solution)/shard_map/ppermute | solution.py:285
  27.8 1.4 %stage_late.1 = (bf16[24,128,128]{2,1,0:T(8,128)(2,1)S(1)}, bf16[24,128,128]{2,1,0:T(8,128)(2,1)S(1)}) custom-call(bf16[48,128,128]{2,1,0:T(8,128)(2,1)} %cost_in_ref.4, bf16[48,128,128]{2,1,0:T(8,128)(2,1)} %coef_in_ref.4), custom_call_target="tpu_custom_call" | custom-call | bytes 3145728 | tf_op jit(solution)/shard_map/stage_late/pallas_call | solution.py:221
  29.2 0.0 collective-permute-done.other_rows_ref
  29.2 2.0 %columns.1 = (f32[192,1,128]{2,1,0:T(1,128)}, f32[48,128]{1,0:T(8,128)S(1)}) custom-call(s32[192]{0:T(256)S(1)} %get-tuple-element.18.number_ref, f32[192,1,128]{2,1,0:T(1,128)S(1)} %get-tuple-element.19.named_ref, f32[512,128]{1,0:T(8,128)S(1)} %bitcast.4, f32[512,128]{1,0:T(8,128)S(1)} %collective-permute-done.other_rows_ref, ...), custom_call_target="tpu_custom_call" | custom-call | flops 4718592 | bytes 3145728 | tf_op jit(solution)/shard_map/columns/pallas_call | solution.py:234
  31.2 2.5 %primal.1 = (bf16[48,128,128]{2,1,0:T(8,128)(2,1)S(1)}, f32[32,128]{1,0:T(8,128)S(1)}) custom-call(s32[192]{0:T(256)S(1)} %get-tuple-element.18.number_ref, f32[48,128]{1,0:T(8,128)S(1)} %get-tuple-element.27.minus_ref, bf16[24,128,128]{2,1,0:T(8,128)(2,1)S(1)} %get-tuple-element.21.early_cost_ref, ...), custom_call_target="tpu_custom_call" | custom-call | flops 4718592 | bytes 4718592 | tf_op jit(solution)/shard_map/primal/pallas_call | solution.py:253
  33.7 2.6 %collective-permute-start.3 = (f32[32,128]{1,0:T(8,128)S(1)}, f32[32,128]{1,0:T(8,128)S(1)}, u32[]{:S(2)}, u32[]{:S(2)}) collective-permute-start(f32[32,128]{1,0:T(8,128)S(1)} %get-tuple-element.30), channel_id=1, source_target_pairs={{0,3},{1,2},{2,1},{3,0},{4,7},{5,6},{6,5},{7,4},{8,11},{9,10},{10,... | collective-permute-start | bytes 49160 | tf_op jit(solution)/shard_map/ppermute | solution.py:291
  36.3 0.5 collective-permute-start.2
  36.8 0.3 collective-permute-start.1
  37.0 1.1 %copy.10 = bf16[48,128,128]{2,1,0:T(8,128)(2,1)} copy(bf16[48,128,128]{2,1,0:T(8,128)(2,1)S(1)} %get-tuple-element.31) | data formatting | bytes 3145728
  38.2 5.2 %all-to-all-start.1 = ((f32[64,1,384]{2,1,0:T(1,128)}), f32[64,1,384]{2,1,0:T(1,128)S(1)}, u32[]{:S(2)}, u32[]{:S(2)}) async-start(f32[64,1,384]{2,1,0:T(1,128)} %bitcast.2), calls=%async_computation.1 | async-start | bytes 196608 | tf_op jit(solution)/shard_map/all_to_all | solution.py:289
  43.4 0.0 collective-permute-done.3
  43.4 0.0 collective-permute-done.2
  43.5 0.0 collective-permute-done.1
  43.5 0.6 %add_multiply_fusion = f32[32,128]{1,0:T(8,128)} fusion(f32[32,128]{1,0:T(8,128)S(1)} %collective-permute-done.2, f32[32,128]{1,0:T(8,128)S(1)} %collective-permute-done.3, f32[32,128]{1,0:T(8,128)S(1)} %get-tuple-element.30, f32[32,128]{1,0:T(8,128)S(1)} %collective-permute-done.1), kind=kLoop, calls=%fused_computation | loop fusion | flops 16384 | bytes 81920 | tf_op jit(solution)/shard_map/mul | solution.py:292
  44.1 9.9 %all-to-all-done.1.recv_ref = f32[64,1,384]{2,1,0:T(1,128)S(1)} async-done(((f32[64,1,384]{2,1,0:T(1,128)}), f32[64,1,384]{2,1,0:T(1,128)S(1)}, u32[]{:S(2)}, u32[]{:S(2)}) %all-to-all-start.1) | async-done | bytes 98336 | tf_op jit(solution)/shard_map/all_to_all | solution.py:289
  54.0 0.8 %finish.1 = f32[16,128]{1,0:T(8,128)} custom-call(f32[64,1,384]{2,1,0:T(1,128)S(1)} %all-to-all-done.1.recv_ref, s32[16,128]{1,0:T(8,128)S(1)} %copy-done), custom_call_target="tpu_custom_call" | custom-call | tf_op jit(solution)/shard_map/finish/pallas_call | solution.py:268
  (4 shorter events, 0.0 us)
Async XLA Ops:
  2.1 23.2 %all-to-all-start = ((f32[32,16,128]{2,1,0:T(8,128)}), f32[32,16,128]{2,1,0:T(8,128)S(1)}, u32[]{:S(2)}, u32[]{:S(2)}) async-start(f32[32,16,128]{2,1,0:T(8,128)} %spread.1), calls=%async_computation | async-start | bytes 524288 | tf_op jit(solution)/shard_map/all_to_all | solution.py:280
  14.1 0.7 %copy-start.1 = (s32[1,48,1]{1,2,0:T(1,128)S(1)}, s32[1,48,1]{1,2,0:T(1,128)}, u32[]{:S(2)}) copy-start(s32[1,48,1]{1,2,0:T(1,128)} %param.10) | copy-start | bytes 580
  14.8 0.7 %copy-start.2 = (s32[1,48]{1,0:T(1,128)S(1)}, s32[1,48]{1,0:T(1,128)}, u32[]{:S(2)}) copy-start(s32[1,48]{1,0:T(1,128)} %local_in_ref.1) | copy-start | bytes 580
  15.4 0.7 %copy-start.3 = (s32[1,48]{1,0:T(1,128)S(1)}, s32[1,48]{1,0:T(1,128)}, u32[]{:S(2)}) copy-start(s32[1,48]{1,0:T(1,128)} %member_in_ref.1) | copy-start | bytes 580
  25.3 3.8 %collective-permute-start = (f32[512,128]{1,0:T(8,128)S(1)}, f32[512,128]{1,0:T(8,128)S(1)}, u32[]{:S(2)}, u32[]{:S(2)}) collective-permute-start(f32[512,128]{1,0:T(8,128)S(1)} %bitcast.3), channel_id=1, source_target_pairs={{0,4},{4,0},{1,5},{5,1},{2,6},{6,2},{3,7},{7,3},{8,12},{12,8},{9,1... | collective-permute-start | bytes 786440 | tf_op jit(solution)/shard_map/ppermute | solution.py:285
  33.7 9.7 %collective-permute-start.3 = (f32[32,128]{1,0:T(8,128)S(1)}, f32[32,128]{1,0:T(8,128)S(1)}, u32[]{:S(2)}, u32[]{:S(2)}) collective-permute-start(f32[32,128]{1,0:T(8,128)S(1)} %get-tuple-element.30), channel_id=1, source_target_pairs={{0,3},{1,2},{2,1},{3,0},{4,7},{5,6},{6,5},{7,4},{8,11},{9,10},{10,... | collective-permute-start | bytes 49160 | tf_op jit(solution)/shard_map/ppermute | solution.py:291
  36.3 7.2 %collective-permute-start.2 = (f32[32,128]{1,0:T(8,128)S(1)}, f32[32,128]{1,0:T(8,128)S(1)}, u32[]{:S(2)}, u32[]{:S(2)}) collective-permute-start(f32[32,128]{1,0:T(8,128)S(1)} %get-tuple-element.30), channel_id=1, source_target_pairs={{0,2},{1,3},{2,0},{3,1},{4,6},{5,7},{6,4},{7,5},{8,10},{9,11},{10,... | collective-permute-start | bytes 49160 | tf_op jit(solution)/shard_map/ppermute | solution.py:291
  36.8 6.7 %collective-permute-start.1 = (f32[32,128]{1,0:T(8,128)S(1)}, f32[32,128]{1,0:T(8,128)S(1)}, u32[]{:S(2)}, u32[]{:S(2)}) collective-permute-start(f32[32,128]{1,0:T(8,128)S(1)} %get-tuple-element.30), channel_id=1, source_target_pairs={{0,1},{1,0},{2,3},{3,2},{4,5},{5,4},{6,7},{7,6},{8,9},{9,8},{10,11... | collective-permute-start | bytes 49160 | tf_op jit(solution)/shard_map/ppermute | solution.py:291
  37.0 17.0 %copy-start = (s32[16,128]{1,0:T(8,128)S(1)}, s32[16,128]{1,0:T(8,128)}, u32[]{:S(2)}) copy-start(s32[16,128]{1,0:T(8,128)} %capacity_ref.1) | copy-start | bytes 24580
  38.2 15.8 %all-to-all-start.1 = ((f32[64,1,384]{2,1,0:T(1,128)}), f32[64,1,384]{2,1,0:T(1,128)S(1)}, u32[]{:S(2)}, u32[]{:S(2)}) async-start(f32[64,1,384]{2,1,0:T(1,128)} %bitcast.2), calls=%async_computation.1 | async-start | bytes 196608 | tf_op jit(solution)/shard_map/all_to_all | solution.py:289

commit v8 on v5

--- a/solution.py
+++ b/solution.py
@@ -67,7 +67,9 @@
     load_coef.start()
     core = lax.axis_index("c")
     lane = lax.broadcasted_iota(jnp.int32, (1, BLOCK), 1)
-    named_ref[...] = jnp.full((MEM, 1, BLOCK), -1.0, jnp.float32)
+    named_ref[...] = jnp.zeros((MEM * ROWS, 1, BLOCK), jnp.float32)
+    for i in range(MEM):
+        named_ref[i * ROWS + 2] = jnp.full((1, BLOCK), -1.0, jnp.float32)
 
     def clear(i, carry):
         count_ref[i] = 0
@@ -85,7 +87,8 @@
         count_ref[owner] = k + 1
         number_ref[PLACE + s] = owner * ROWS + k
         half = (lane >= BLOCK // 2) == (k == 1)
-        named_ref[owner] = jnp.where(half, local.astype(jnp.float32), named_ref[owner])
+        at = owner * ROWS + 2
+        named_ref[at] = jnp.where(half, local.astype(jnp.float32), named_ref[at])
         return carry
 
     lax.fori_loop(0, CAP, slot, 0)
@@ -107,9 +110,7 @@
     early_cost_ref, early_coef_ref, late_cost_ref, late_coef_ref,
     send_ref, minus_ref, column_ref, total_ref,
 ):
-    send_ref[...] = jnp.zeros((MEM * ROWS, 1, BLOCK), jnp.float32)
-    for i in range(MEM):
-        send_ref[i * ROWS + 2] = named_ref[i]
+    send_ref[...] = named_ref[...]
     for s in range(CAP):
         at = pl.ds(number_ref[ROW + s], 1)
         minus_ref[s:s + 1, :] = -jnp.where(number_ref[OTHER + s] == 1, other_rows_ref[at, :], own_rows_ref[at, :])
@@ -204,7 +205,7 @@
         out_shape=(
             early,
             early,
-            pltpu.VMEM((MEM, 1, BLOCK), jnp.float32),
+            pltpu.VMEM((MEM * ROWS, 1, BLOCK), jnp.float32),
             jax.ShapeDtypeStruct((4 * CAP,), jnp.int32),
         ),
         in_specs=[SMEM] * 3 + [ANY] * 2,

time: 47.4 us -> 47.3 us (level)
  no operation moved by 1% of the time
where the time goes in v8:
time: 47.3 us; the launch traced here: 47 us
  starting transfers between devices  22.2 us (47%)
  Pallas kernels  10.7 us (23%)
  waiting for transfers between devices  10.2 us (22%)
  local copies, waits for them, and re-layouts  3.11 us (7%)
  between operations  0.7 us (1%)
    all_to_all x1, starting transfers between devices, per_device(): lax.all_to_all(copies, ('z', 'y'), split_axis=0, concat_axis=0, tiled=True)  12 us
    all_to_all x1, waiting for transfers between devices, per_device(): lax.all_to_all(copies, ('z', 'y'), split_axis=0, concat_axis=0, tiled=True)  6.67 us
    all_to_all x1, starting transfers between devices, per_device(): lax.all_to_all(send, ('z', 'y', 'c'), split_axis=0, concat_axis=0, tiled=...  4.41 us
    ppermute x3, starting transfers between devices, per_device(): lax.ppermute(share, 'x', [(i, i ^ k) for i in range(X)])  3.34 us
    unnamed x9, local copies, waits for them, and re-layouts  3.11 us
    pallas_call x1, Pallas kernels, stage(): pl.pallas_call(stage_kernel, out_shape=(early, early, pltpu.VMEM((MEM * R...  2.54 us
    pallas_call x1, Pallas kernels, primal_and_members(): pl.pallas_call(primal_kernel, out_shape=(pltpu.VMEM((CAP, BLOCK, BLOCK),...  2.52 us
    ppermute x3, waiting for transfers between devices, per_device(): lax.ppermute(share, 'x', [(i, i ^ k) for i in range(X)])  2.47 us
  transfers between devices with their start and end apart: 6, of which 3 were waited for; matrix products, arithmetic and copies ran while one was open for 2% of the time, Pallas kernels for 14%

profile of v8, /device:TPU:1, one launch (start us, length us, event | category | flops | bytes accessed | tf_op | source)
XLA Modules:
  0.0 47.0 jit_solution(7725862207035269837)
XLA Ops:
  0.6 1.4 %spread.1 = f32[32,16,128]{2,1,0:T(8,128)} custom-call(f32[16,128]{1,0:T(8,128)} %duals_ref.1), custom_call_target="tpu_custom_call" | custom-call | tf_op jit(solution)/shard_map/spread/pallas_call | solution.py:45
  2.1 12.0 %all-to-all-start = ((f32[32,16,128]{2,1,0:T(8,128)}), f32[32,16,128]{2,1,0:T(8,128)S(1)}, u32[]{:S(2)}, u32[]{:S(2)}) async-start(f32[32,16,128]{2,1,0:T(8,128)} %spread.1), calls=%async_computation | async-start | bytes 524288 | tf_op jit(solution)/shard_map/all_to_all | solution.py:284
  14.1 0.0 copy-start.1
  14.1 0.6 %copy-done.1 = s32[1,48,1]{1,2,0:T(1,128)S(1)} copy-done((s32[1,48,1]{1,2,0:T(1,128)S(1)}, s32[1,48,1]{1,2,0:T(1,128)}, u32[]{:S(2)}) %copy-start.1) | copy-done | bytes 216
  14.8 0.7 %copy-done.2 = s32[1,48]{1,0:T(1,128)S(1)} copy-done((s32[1,48]{1,0:T(1,128)S(1)}, s32[1,48]{1,0:T(1,128)}, u32[]{:S(2)}) %copy-start.2) | copy-done | bytes 216
  15.4 0.7 %copy-done.3 = s32[1,48]{1,0:T(1,128)S(1)} copy-done((s32[1,48]{1,0:T(1,128)S(1)}, s32[1,48]{1,0:T(1,128)}, u32[]{:S(2)}) %copy-start.3) | copy-done | bytes 216
  16.1 2.5 %stage.1 = (bf16[24,128,128]{2,1,0:T(8,128)(2,1)S(1)}, bf16[24,128,128]{2,1,0:T(8,128)(2,1)S(1)}, f32[192,1,128]{2,1,0:T(1,128)S(1)}, s32[192]{0:T(256)S(1)}) custom-call(s32[1,48]{1,0:T(1,128)S(1)} %bitcast.5, s32[1,48]{1,0:T(1,128)S(1)} %copy-done.2, s32[1,48]{1,0:T(1,128)S(1)} %copy-done.3, bf16[48,128,128]{2,1,0:T(8,128)(2,1)} %cost_in_ref.4, ...), custom_call_target="tpu_custom_call" | custom-call | bytes 3145728 | tf_op jit(solution)/shard_map/stage/pallas_call | solution.py:203
  18.6 6.7 %all-to-all-done = f32[32,16,128]{2,1,0:T(8,128)S(1)} async-done(((f32[32,16,128]{2,1,0:T(8,128)}), f32[32,16,128]{2,1,0:T(8,128)S(1)}, u32[]{:S(2)}, u32[]{:S(2)}) %all-to-all-start) | async-done | bytes 262176 | tf_op jit(solution)/shard_map/all_to_all | solution.py:284
  25.3 2.5 %collective-permute-start = (f32[512,128]{1,0:T(8,128)S(1)}, f32[512,128]{1,0:T(8,128)S(1)}, u32[]{:S(2)}, u32[]{:S(2)}) collective-permute-start(f32[512,128]{1,0:T(8,128)S(1)} %bitcast.3), channel_id=1, source_target_pairs={{0,4},{4,0},{1,5},{5,1},{2,6},{6,2},{3,7},{7,3},{8,12},{12,8},{9,1... | collective-permute-start | bytes 786440 | tf_op jit(solution)/shard_map/ppermute | solution.py:289
  27.8 1.4 %stage_late.1 = (bf16[24,128,128]{2,1,0:T(8,128)(2,1)S(1)}, bf16[24,128,128]{2,1,0:T(8,128)(2,1)S(1)}) custom-call(bf16[48,128,128]{2,1,0:T(8,128)(2,1)} %cost_in_ref.4, bf16[48,128,128]{2,1,0:T(8,128)(2,1)} %coef_in_ref.4), custom_call_target="tpu_custom_call" | custom-call | bytes 3145728 | tf_op jit(solution)/shard_map/stage_late/pallas_call | solution.py:222
  29.2 0.0 collective-permute-done.other_rows_ref
  29.2 2.0 %columns.1 = (f32[192,1,128]{2,1,0:T(1,128)}, f32[48,128]{1,0:T(8,128)S(1)}) custom-call(s32[192]{0:T(256)S(1)} %get-tuple-element.20.number_ref, f32[192,1,128]{2,1,0:T(1,128)S(1)} %get-tuple-element.21.named_ref, f32[512,128]{1,0:T(8,128)S(1)} %bitcast.4, f32[512,128]{1,0:T(8,128)S(1)} %collective-permute-done.other_rows_ref, ...), custom_call_target="tpu_custom_call" | custom-call | flops 4718592 | bytes 3145728 | tf_op jit(solution)/shard_map/columns/pallas_call | solution.py:235
  31.2 4.4 %all-to-all-start.1 = ((f32[64,1,384]{2,1,0:T(1,128)}), f32[64,1,384]{2,1,0:T(1,128)S(1)}, u32[]{:S(2)}, u32[]{:S(2)}) async-start(f32[64,1,384]{2,1,0:T(1,128)} %bitcast.2), calls=%async_computation.1 | async-start | bytes 196608 | tf_op jit(solution)/shard_map/all_to_all | solution.py:293
  35.6 2.5 %primal.1 = (bf16[48,128,128]{2,1,0:T(8,128)(2,1)S(1)}, f32[32,128]{1,0:T(8,128)S(1)}) custom-call(s32[192]{0:T(256)S(1)} %get-tuple-element.20.number_ref, f32[48,128]{1,0:T(8,128)S(1)} %get-tuple-element.29.minus_ref, bf16[24,128,128]{2,1,0:T(8,128)(2,1)S(1)} %get-tuple-element.23.early_cost_ref, ...), custom_call_target="tpu_custom_call" | custom-call | flops 4718592 | bytes 4718592 | tf_op jit(solution)/shard_map/primal/pallas_call | solution.py:254
  38.1 2.6 %collective-permute-start.3 = (f32[32,128]{1,0:T(8,128)S(1)}, f32[32,128]{1,0:T(8,128)S(1)}, u32[]{:S(2)}, u32[]{:S(2)}) collective-permute-start(f32[32,128]{1,0:T(8,128)S(1)} %get-tuple-element.32.m0_ref), channel_id=1, source_target_pairs={{0,3},{1,2},{2,1},{3,0},{4,7},{5,6},{6,5},{7,4},{8,11},{9,10},{10,... | collective-permute-start | bytes 49160 | tf_op jit(solution)/shard_map/ppermute | solution.py:295
  40.7 0.5 %collective-permute-start.2 = (f32[32,128]{1,0:T(8,128)S(1)}, f32[32,128]{1,0:T(8,128)S(1)}, u32[]{:S(2)}, u32[]{:S(2)}) collective-permute-start(f32[32,128]{1,0:T(8,128)S(1)} %get-tuple-element.32.m0_ref), channel_id=1, source_target_pairs={{0,2},{1,3},{2,0},{3,1},{4,6},{5,7},{6,4},{7,5},{8,10},{9,11},{10,... | collective-permute-start | bytes 49160 | tf_op jit(solution)/shard_map/ppermute | solution.py:295
  41.2 0.2 collective-permute-start.1
  41.5 1.1 %copy.10 = bf16[48,128,128]{2,1,0:T(8,128)(2,1)} copy(bf16[48,128,128]{2,1,0:T(8,128)(2,1)S(1)} %get-tuple-element.35) | data formatting | bytes 3145728
  42.6 0.0 collective-permute-done.3.m3_ref
  42.6 2.5 %collective-permute-done.2.m2_ref = f32[32,128]{1,0:T(8,128)S(1)} collective-permute-done((f32[32,128]{1,0:T(8,128)S(1)}, f32[32,128]{1,0:T(8,128)S(1)}, u32[]{:S(2)}, u32[]{:S(2)}) %collective-permute-start.2) | collective-permute-done | bytes 16416 | tf_op jit(solution)/shard_map/ppermute | solution.py:295
  45.1 0.0 collective-permute-done.1.m1_ref
  45.1 1.1 %all-to-all-done.1.recv_ref = f32[64,1,384]{2,1,0:T(1,128)S(1)} async-done(((f32[64,1,384]{2,1,0:T(1,128)}), f32[64,1,384]{2,1,0:T(1,128)S(1)}, u32[]{:S(2)}, u32[]{:S(2)}) %all-to-all-start.1) | async-done | bytes 98336 | tf_op jit(solution)/shard_map/all_to_all | solution.py:293
  46.1 0.0 copy-done
  46.2 0.8 %finish.1 = (f32[16,128]{1,0:T(8,128)}, f32[32,128]{1,0:T(8,128)}) custom-call(f32[64,1,384]{2,1,0:T(1,128)S(1)} %all-to-all-done.1.recv_ref, f32[32,128]{1,0:T(8,128)S(1)} %get-tuple-element.32.m0_ref, f32[32,128]{1,0:T(8,128)S(1)} %collective-permute-done.1.m1_ref, f32[32,128]{1,0:T(8,128)S(1)} %collective-permute-done.2.m2_ref, ...), custom_call_target="tpu_custom_call" | custom-call | tf_op jit(solution)/shard_map/finish/pallas_call | solution.py:269
  (3 shorter events, 0.0 us)
Async XLA Ops:
  2.1 23.2 %all-to-all-start = ((f32[32,16,128]{2,1,0:T(8,128)}), f32[32,16,128]{2,1,0:T(8,128)S(1)}, u32[]{:S(2)}, u32[]{:S(2)}) async-start(f32[32,16,128]{2,1,0:T(8,128)} %spread.1), calls=%async_computation | async-start | bytes 524288 | tf_op jit(solution)/shard_map/all_to_all | solution.py:284
  14.1 0.7 %copy-start.1 = (s32[1,48,1]{1,2,0:T(1,128)S(1)}, s32[1,48,1]{1,2,0:T(1,128)}, u32[]{:S(2)}) copy-start(s32[1,48,1]{1,2,0:T(1,128)} %param.10) | copy-start | bytes 580
  14.8 0.7 %copy-start.2 = (s32[1,48]{1,0:T(1,128)S(1)}, s32[1,48]{1,0:T(1,128)}, u32[]{:S(2)}) copy-start(s32[1,48]{1,0:T(1,128)} %local_in_ref.1) | copy-start | bytes 580
  15.4 0.7 %copy-start.3 = (s32[1,48]{1,0:T(1,128)S(1)}, s32[1,48]{1,0:T(1,128)}, u32[]{:S(2)}) copy-start(s32[1,48]{1,0:T(1,128)} %member_in_ref.1) | copy-start | bytes 580
  25.3 3.8 %collective-permute-start = (f32[512,128]{1,0:T(8,128)S(1)}, f32[512,128]{1,0:T(8,128)S(1)}, u32[]{:S(2)}, u32[]{:S(2)}) collective-permute-start(f32[512,128]{1,0:T(8,128)S(1)} %bitcast.3), channel_id=1, source_target_pairs={{0,4},{4,0},{1,5},{5,1},{2,6},{6,2},{3,7},{7,3},{8,12},{12,8},{9,1... | collective-permute-start | bytes 786440 | tf_op jit(solution)/shard_map/ppermute | solution.py:289
  31.2 15.0 %all-to-all-start.1 = ((f32[64,1,384]{2,1,0:T(1,128)}), f32[64,1,384]{2,1,0:T(1,128)S(1)}, u32[]{:S(2)}, u32[]{:S(2)}) async-start(f32[64,1,384]{2,1,0:T(1,128)} %bitcast.2), calls=%async_computation.1 | async-start | bytes 196608 | tf_op jit(solution)/shard_map/all_to_all | solution.py:293
  38.1 4.5 %collective-permute-start.3 = (f32[32,128]{1,0:T(8,128)S(1)}, f32[32,128]{1,0:T(8,128)S(1)}, u32[]{:S(2)}, u32[]{:S(2)}) collective-permute-start(f32[32,128]{1,0:T(8,128)S(1)} %get-tuple-element.32.m0_ref), channel_id=1, source_target_pairs={{0,3},{1,2},{2,1},{3,0},{4,7},{5,6},{6,5},{7,4},{8,11},{9,10},{10,... | collective-permute-start | bytes 49160 | tf_op jit(solution)/shard_map/ppermute | solution.py:295
  40.7 4.4 %collective-permute-start.2 = (f32[32,128]{1,0:T(8,128)S(1)}, f32[32,128]{1,0:T(8,128)S(1)}, u32[]{:S(2)}, u32[]{:S(2)}) collective-permute-start(f32[32,128]{1,0:T(8,128)S(1)} %get-tuple-element.32.m0_ref), channel_id=1, source_target_pairs={{0,2},{1,3},{2,0},{3,1},{4,6},{5,7},{6,4},{7,5},{8,10},{9,11},{10,... | collective-permute-start | bytes 49160 | tf_op jit(solution)/shard_map/ppermute | solution.py:295
  41.2 3.9 %collective-permute-start.1 = (f32[32,128]{1,0:T(8,128)S(1)}, f32[32,128]{1,0:T(8,128)S(1)}, u32[]{:S(2)}, u32[]{:S(2)}) collective-permute-start(f32[32,128]{1,0:T(8,128)S(1)} %get-tuple-element.32.m0_ref), channel_id=1, source_target_pairs={{0,1},{1,0},{2,3},{3,2},{4,5},{5,4},{6,7},{7,6},{8,9},{9,8},{10,11... | collective-permute-start | bytes 49160 | tf_op jit(solution)/shard_map/ppermute | solution.py:295
  41.5 4.7 %copy-start = (s32[16,128]{1,0:T(8,128)S(1)}, s32[16,128]{1,0:T(8,128)}, u32[]{:S(2)}) copy-start(s32[16,128]{1,0:T(8,128)} %capacity_ref.1) | copy-start | bytes 24580
